TPU v7x, 32 devices: a whole 2x2x4 slice. The times are simulated.
32 devices in a mesh: dp: 2 (over x), fsdp: 16 (over z, y, core).
Axes of the slice: x: 2, y: 2, z: 4, core: 2. Of those that a mesh axis runs over, the one named last changes fastest.
Arguments:
- tokens: bfloat16 [12288, 960], P(('dp', 'fsdp')), may hold values from -6 to 6
- lengths: int32 [32, 4], P(('dp', 'fsdp')), may hold values from 1 to 168, 336 in all within a row
- w_query: bfloat16 [960, 960], P('fsdp'), may hold values from -0.1875 to 0.1875
- key_weight: bfloat16 [960, 320], P('fsdp'), may hold values from -0.1875 to 0.1875
- value_weight: bfloat16 [960, 320], P('fsdp'), may hold values from -0.1875 to 0.1875
- output_weight: bfloat16 [960, 960], P('fsdp'), may hold values from -0.75 to 0.75
- w_gate: bfloat16 [960, 2560], P('fsdp'), may hold values from -0.1875 to 0.1875
- w_up: bfloat16 [960, 2560], P('fsdp'), may hold values from -0.1875 to 0.1875
- w_down: bfloat16 [2560, 960], P('fsdp'), may hold values from -0.125 to 0.125
- gain_attn: bfloat16 [960], P('fsdp'), may hold values from 0.099609375 to 1.8984375
- gain_ffn: bfloat16 [960], P('fsdp'), may hold values from 0.099609375 to 1.8984375
- out_grad: bfloat16 [12288, 960], P(('dp', 'fsdp')), may hold values from -6 to 6
Outputs:
- output: bfloat16 [12288, 960], P(('dp', 'fsdp'))
- input_grad: bfloat16 [12288, 960], P(('dp', 'fsdp'))
- grad_query: float32 [960, 960], P('fsdp')
- key_weight_gradient: float32 [960, 320], P('fsdp')
- value_weight_gradient: float32 [960, 320], P('fsdp')
- grad_out: float32 [960, 960], P('fsdp')
- grad_gate: float32 [960, 2560], P('fsdp')
- grad_up: float32 [960, 2560], P('fsdp')
- grad_down: float32 [2560, 960], P('fsdp')
- grad_gain_attn: float32 [960], P('fsdp')
- grad_gain_ffn: float32 [960], P('fsdp')
Inputs may be any that keep to these rules, and one draw needn't show every extreme that they name: A row holds the lengths of the 4 documents of one sequence from its first slot on; each row sums to 336 and its largest entry is 168.
All inputs are finite; a program needn't handle non-finite values.
Results may differ from a plain program's by a relative error of at most 0.028.
Values may be sent and summed in bfloat16 or wider, within the bound.
No kernel may reach another device: no remote copies, remote signals or barrier semaphores. Data moves between devices by JAX's collectives and lax.ppermute only.
A program may use at most 192 MiB of HBM per device.

v0:
```python
import math

import jax
import jax.numpy as jnp
from jax import lax
from jax.sharding import PartitionSpec as P

MODEL_WIDTH = 960
QUERY_HEADS = 15
KEY_VALUE_HEADS = 5
HEAD_SIZE = 64


rope_base = 10000.0
norm_eps = 1e-05


def layout(doc_lengths, token_count):
    ends = jnp.cumsum(doc_lengths, axis=1)
    starts = ends - doc_lengths
    place = jnp.arange(token_count, dtype=jnp.int32)
    document = jnp.sum((place[None, :, None] >= ends[:, None, :]).astype(jnp.int32), axis=2)
    inside = place[None, :] < ends[:, -1:]
    segment = jnp.where(inside, document, -1)
    chosen = (
        document[:, :, None] == jnp.arange(doc_lengths.shape[1], dtype=jnp.int32)[None, None, :]
    )
    begin = jnp.sum(jnp.where(chosen, starts[:, None, :], 0), axis=2)
    positions = jnp.where(inside, place[None, :] - begin, 0)
    causal = place[:, None] >= place[None, :]
    same = (segment[:, :, None] == segment[:, None, :]) & (segment[:, :, None] >= 0)
    allowed = same & causal[None] | (place[:, None] == place[None, :])[None]
    return (positions, allowed)


def rotation(positions):
    half = HEAD_SIZE // 2
    frequency = jnp.exp(
        jnp.arange(half, dtype=jnp.float32) * (-2.0 * math.log(rope_base) / HEAD_SIZE)
    )
    angle = positions.astype(jnp.float32)[..., None] * frequency
    return (jnp.cos(angle), jnp.sin(angle))


def apply_rotary(values, cosine_table, sine_table):
    half = values.shape[-1] // 2
    first = values[..., :half]
    second = values[..., half:]
    cosine_table = cosine_table[..., None, :]
    sine_table = sine_table[..., None, :]
    return jnp.concatenate(
        [first * cosine_table - second * sine_table, second * cosine_table + first * sine_table],
        axis=-1,
    )


def apply_rotary_backward(values, cosine_table, sine_table):
    half = values.shape[-1] // 2
    first = values[..., :half]
    second = values[..., half:]
    cosine_table = cosine_table[..., None, :]
    sine_table = sine_table[..., None, :]
    return jnp.concatenate(
        [first * cosine_table + second * sine_table, second * cosine_table - first * sine_table],
        axis=-1,
    )


def matrix_product(left, right):
    return jnp.dot(left, right, preferred_element_type=jnp.float32)


def matrix_product_backward(left, right):
    return lax.dot_general(
        left, right, (((1,), (1,)), ((), ())), preferred_element_type=jnp.float32
    )


def outer_sum(left, right):
    return lax.dot_general(
        left, right, (((0,), (0,)), ((), ())), preferred_element_type=jnp.float32
    )


def norm_forward(values, gain):
    scale = lax.rsqrt(jnp.mean(values * values, axis=-1, keepdims=True) + norm_eps)
    return (scale, (values * scale * gain.astype(jnp.float32)).astype(jnp.bfloat16))


def norm_backward(values, scale, gain, grad):
    unit = values * scale
    gain_grad = jnp.sum(grad * unit, axis=0)
    inner = grad * gain.astype(jnp.float32)
    return (gain_grad, scale * (inner - unit * jnp.mean(inner * unit, axis=-1, keepdims=True)))


def scores(query_rows, key, allowed):
    score = jnp.einsum(
        "tkrd,ukd->krtu", query_rows, key, preferred_element_type=jnp.float32
    ) * HEAD_SIZE ** (-0.5)
    return jnp.where(allowed, score, -1e30)


def block_forward(source, weights, cosine_table, sine_table, allowed):
    w_query, key_weight, value_weight, output_weight, w_gate, w_up, w_down, gain_attn, gain_ffn = (
        weights
    )
    token_count = source.shape[0]
    scale_attn, normalized_input = norm_forward(source, gain_attn)
    query_rows = apply_rotary(
        matrix_product(normalized_input, w_query).reshape(token_count, QUERY_HEADS, HEAD_SIZE),
        cosine_table,
        sine_table,
    ).astype(jnp.bfloat16)
    query_rows = query_rows.reshape(
        token_count, KEY_VALUE_HEADS, QUERY_HEADS // KEY_VALUE_HEADS, HEAD_SIZE
    )
    key = apply_rotary(
        matrix_product(normalized_input, key_weight).reshape(
            token_count, KEY_VALUE_HEADS, HEAD_SIZE
        ),
        cosine_table,
        sine_table,
    ).astype(jnp.bfloat16)
    value_rows = (
        matrix_product(normalized_input, value_weight)
        .astype(jnp.bfloat16)
        .reshape(token_count, KEY_VALUE_HEADS, HEAD_SIZE)
    )
    score = scores(query_rows, key, allowed)
    highest = jnp.max(score, axis=-1, keepdims=True)
    powers = jnp.exp(score - highest)
    summed = jnp.sum(powers, axis=-1, keepdims=True)
    log_total = highest + jnp.log(summed)
    attention = (powers / summed).astype(jnp.bfloat16)
    mixed = jnp.einsum("krtu,ukd->tkrd", attention, value_rows, preferred_element_type=jnp.float32)
    mixed = mixed.reshape(token_count, MODEL_WIDTH).astype(jnp.bfloat16)
    hidden = source + matrix_product(mixed, output_weight)
    scale_ffn, normed_ffn = norm_forward(hidden, gain_ffn)
    gate = matrix_product(normed_ffn, w_gate)
    up_value = matrix_product(normed_ffn, w_up)
    inner = (jax.nn.silu(gate) * up_value).astype(jnp.bfloat16)
    result = hidden + matrix_product(inner, w_down)
    kept = (
        source,
        scale_attn,
        normalized_input,
        query_rows,
        key,
        value_rows,
        log_total,
        mixed,
        hidden,
        scale_ffn,
        normed_ffn,
        gate,
        up_value,
        inner,
    )
    return (result, kept)


def block_backward(grad, weights, kept, cosine_table, sine_table, allowed):
    w_query, key_weight, value_weight, output_weight, w_gate, w_up, w_down, gain_attn, gain_ffn = (
        weights
    )
    (
        source,
        scale_attn,
        normalized_input,
        query_rows,
        key,
        value_rows,
        log_total,
        mixed,
        hidden,
        scale_ffn,
        normed_ffn,
        gate,
        up_value,
        inner,
    ) = kept
    token_count = source.shape[0]
    grad_low = grad.astype(jnp.bfloat16)
    grad_down = outer_sum(inner, grad_low)
    grad_inner = matrix_product_backward(grad_low, w_down)
    sigmoid_gate = jax.nn.sigmoid(gate)
    grad_gate = (grad_inner * up_value * sigmoid_gate * (1.0 + gate * (1.0 - sigmoid_gate))).astype(
        jnp.bfloat16
    )
    grad_up = (grad_inner * gate * sigmoid_gate).astype(jnp.bfloat16)
    grad_w_gate = outer_sum(normed_ffn, grad_gate)
    grad_w_up = outer_sum(normed_ffn, grad_up)
    grad_normed_ffn = matrix_product_backward(grad_gate, w_gate) + matrix_product_backward(
        grad_up, w_up
    )
    grad_gain_ffn, grad_hidden = norm_backward(hidden, scale_ffn, gain_ffn, grad_normed_ffn)
    grad_hidden = grad + grad_hidden
    attention_gradient = grad_hidden.astype(jnp.bfloat16)
    grad_w_out = outer_sum(mixed, attention_gradient)
    grad_mixed = (
        matrix_product_backward(attention_gradient, output_weight)
        .astype(jnp.bfloat16)
        .reshape(token_count, KEY_VALUE_HEADS, QUERY_HEADS // KEY_VALUE_HEADS, HEAD_SIZE)
    )
    attention = jnp.exp(scores(query_rows, key, allowed) - log_total)
    grad_attention = jnp.einsum(
        "tkrd,ukd->krtu", grad_mixed, value_rows, preferred_element_type=jnp.float32
    )
    value_weight_gradient = jnp.einsum(
        "krtu,tkrd->ukd",
        attention.astype(jnp.bfloat16),
        grad_mixed,
        preferred_element_type=jnp.float32,
    )
    grad_score = attention * (
        grad_attention - jnp.sum(attention * grad_attention, axis=-1, keepdims=True)
    )
    grad_score = (grad_score * HEAD_SIZE ** (-0.5)).astype(jnp.bfloat16)
    grad_query = jnp.einsum("krtu,ukd->tkrd", grad_score, key, preferred_element_type=jnp.float32)
    key_weight_gradient = jnp.einsum(
        "krtu,tkrd->ukd", grad_score, query_rows, preferred_element_type=jnp.float32
    )
    grad_query = (
        apply_rotary_backward(
            grad_query.reshape(token_count, QUERY_HEADS, HEAD_SIZE), cosine_table, sine_table
        )
        .reshape(token_count, MODEL_WIDTH)
        .astype(jnp.bfloat16)
    )
    key_weight_gradient = (
        apply_rotary_backward(key_weight_gradient, cosine_table, sine_table)
        .reshape(token_count, KEY_VALUE_HEADS * HEAD_SIZE)
        .astype(jnp.bfloat16)
    )
    value_weight_gradient = value_weight_gradient.reshape(
        token_count, KEY_VALUE_HEADS * HEAD_SIZE
    ).astype(jnp.bfloat16)
    grad_w_query = outer_sum(normalized_input, grad_query)
    grad_w_key = outer_sum(normalized_input, key_weight_gradient)
    grad_w_value = outer_sum(normalized_input, value_weight_gradient)
    grad_normed = (
        matrix_product_backward(grad_query, w_query)
        + matrix_product_backward(key_weight_gradient, key_weight)
        + matrix_product_backward(value_weight_gradient, value_weight)
    )
    grad_gain_attn, grad_source = norm_backward(source, scale_attn, gain_attn, grad_normed)
    terms = (
        grad_w_query,
        grad_w_key,
        grad_w_value,
        grad_w_out,
        grad_w_gate,
        grad_w_up,
        grad_down,
        grad_gain_attn,
        grad_gain_ffn,
    )
    return (grad_hidden + grad_source, terms)


def shards(
    tokens,
    lengths,
    w_query,
    key_weight,
    value_weight,
    output_weight,
    w_gate,
    w_up,
    w_down,
    gain_attn,
    gain_ffn,
    out_grad,
):
    weights = (
        lax.all_gather(w_query, "fsdp", axis=0, tiled=True),
        lax.all_gather(key_weight, "fsdp", axis=0, tiled=True),
        lax.all_gather(value_weight, "fsdp", axis=0, tiled=True),
        lax.all_gather(output_weight, "fsdp", axis=0, tiled=True),
        lax.all_gather(w_gate, "fsdp", axis=0, tiled=True),
        lax.all_gather(w_up, "fsdp", axis=0, tiled=True),
        lax.all_gather(w_down, "fsdp", axis=0, tiled=True),
        lax.all_gather(gain_attn, "fsdp", axis=0, tiled=True),
        lax.all_gather(gain_ffn, "fsdp", axis=0, tiled=True),
    )
    positions, allowed = layout(lengths, tokens.shape[0])
    cosine_table, sine_table = rotation(positions[0])
    allowed = allowed[0]
    first, kept_first = block_forward(
        tokens.astype(jnp.float32), weights, cosine_table, sine_table, allowed
    )
    second, kept_second = block_forward(first, weights, cosine_table, sine_table, allowed)
    carried, terms_second = block_backward(
        out_grad.astype(jnp.float32), weights, kept_second, cosine_table, sine_table, allowed
    )
    input_grad, terms_first = block_backward(
        carried, weights, kept_first, cosine_table, sine_table, allowed
    )
    totals = tuple((left + right for left, right in zip(terms_first, terms_second)))
    shares = (
        lax.psum_scatter(
            totals[0].astype(jnp.bfloat16), "fsdp", scatter_dimension=0, tiled=True
        ).astype(jnp.float32),
        lax.psum_scatter(
            totals[1].astype(jnp.bfloat16), "fsdp", scatter_dimension=0, tiled=True
        ).astype(jnp.float32),
        lax.psum_scatter(
            totals[2].astype(jnp.bfloat16), "fsdp", scatter_dimension=0, tiled=True
        ).astype(jnp.float32),
        lax.psum_scatter(
            totals[3].astype(jnp.bfloat16), "fsdp", scatter_dimension=0, tiled=True
        ).astype(jnp.float32),
        lax.psum_scatter(
            totals[4].astype(jnp.bfloat16), "fsdp", scatter_dimension=0, tiled=True
        ).astype(jnp.float32),
        lax.psum_scatter(
            totals[5].astype(jnp.bfloat16), "fsdp", scatter_dimension=0, tiled=True
        ).astype(jnp.float32),
        lax.psum_scatter(
            totals[6].astype(jnp.bfloat16), "fsdp", scatter_dimension=0, tiled=True
        ).astype(jnp.float32),
        lax.psum_scatter(
            totals[7].astype(jnp.bfloat16), "fsdp", scatter_dimension=0, tiled=True
        ).astype(jnp.float32),
        lax.psum_scatter(
            totals[8].astype(jnp.bfloat16), "fsdp", scatter_dimension=0, tiled=True
        ).astype(jnp.float32),
    )
    final = (
        lax.psum(shares[0].astype(jnp.bfloat16), "dp").astype(jnp.float32),
        lax.psum(shares[1].astype(jnp.bfloat16), "dp").astype(jnp.float32),
        lax.psum(shares[2].astype(jnp.bfloat16), "dp").astype(jnp.float32),
        lax.psum(shares[3].astype(jnp.bfloat16), "dp").astype(jnp.float32),
        lax.psum(shares[4].astype(jnp.bfloat16), "dp").astype(jnp.float32),
        lax.psum(shares[5].astype(jnp.bfloat16), "dp").astype(jnp.float32),
        lax.psum(shares[6].astype(jnp.bfloat16), "dp").astype(jnp.float32),
        lax.psum(shares[7].astype(jnp.bfloat16), "dp").astype(jnp.float32),
        lax.psum(shares[8].astype(jnp.bfloat16), "dp").astype(jnp.float32),
    )
    return (
        second.astype(jnp.bfloat16),
        input_grad.astype(jnp.bfloat16),
        final[0],
        final[1],
        final[2],
        final[3],
        final[4],
        final[5],
        final[6],
        final[7],
        final[8],
    )


def solution(mesh):
    return jax.shard_map(
        shards,
        mesh=mesh,
        in_specs=(
            P(("dp", "fsdp"), None),
            P(("dp", "fsdp"), None),
            P("fsdp", None),
            P("fsdp", None),
            P("fsdp", None),
            P("fsdp", None),
            P("fsdp", None),
            P("fsdp", None),
            P("fsdp", None),
            P("fsdp"),
            P("fsdp"),
            P(("dp", "fsdp"), None),
        ),
        out_specs=(
            P(("dp", "fsdp"), None),
            P(("dp", "fsdp"), None),
            P("fsdp", None),
            P("fsdp", None),
            P("fsdp", None),
            P("fsdp", None),
            P("fsdp", None),
            P("fsdp", None),
            P("fsdp", None),
            P("fsdp"),
            P("fsdp"),
        ),
        check_vma=False,
    )
```

profile of v0, /device:TPU:0, one launch (start us, length us, event | category | flops | bytes accessed | tf_op | source)
XLA Modules:
  0.0 798.0 jit_solution(11669562284645938201)
XLA Ops:
  17.1 35.3 %all-reduce.17 = (bf16[960]{0:T(1024)(128)(2,1)S(1)}, bf16[960]{0:T(1024)(128)(2,1)S(1)}) all-reduce(bf16[960]{0:T(1024)(128)(2,1)S(1)} %dynamic-update-slice, bf16[960]{0:T(1024)(128)(2,1)S(1)} %dynamic-update-slice.1), channel_id=1, replica_groups=mesh['dp'=2,'fsdp'=16] {'fsdp'}, use_global_device_ids=true, to_apply=%add | all-reduce | flops 1920 | bytes 7680
  52.4 20.3 %all-gather.1 = bf16[16,60,320]{2,1,0:T(8,128)(2,1)S(1)} all-gather(bf16[1,60,320]{2,1,0:T(8,128)(2,1)} %bitcast.287), channel_id=1, replica_groups=mesh['dp'=2,'fsdp'=16] {'fsdp'}, dimensions={0}, use_global_device_ids=true | all-gather | bytes 652800 | tf_op jit(solution)/shard_map/all_gather | solution.py:278
  73.0 21.9 %all-gather = bf16[16,60,320]{2,1,0:T(8,128)(2,1)S(1)} all-gather(bf16[1,60,320]{2,1,0:T(8,128)(2,1)S(1)} %bitcast.288), channel_id=1, replica_groups=mesh['dp'=2,'fsdp'=16] {'fsdp'}, dimensions={0}, use_global_device_ids=true | all-gather | bytes 652800 | tf_op jit(solution)/shard_map/all_gather | solution.py:279
  120.9 36.6 %all-gather.18.cloned.1.call-done = bf16[16,60,2560]{2,1,0:T(8,128)(2,1)} async-done(((bf16[1,60,2560]{2,1,0:T(8,128)(2,1)}), bf16[16,60,2560]{2,1,0:T(8,128)(2,1)}) %all-gather.18.cloned.1.call-update) | async-done | bytes 4915216 | tf_op jit(solution)/shard_map/all_gather | solution.py:281
  157.5 7.3 reshape.437
  164.8 49.4 %all-gather.20.cloned.1.call-done = bf16[16,60,2560]{2,1,0:T(8,128)(2,1)} async-done(((bf16[1,60,2560]{2,1,0:T(8,128)(2,1)}), bf16[16,60,2560]{2,1,0:T(8,128)(2,1)}) %all-gather.20.cloned.1.call-update) | async-done | bytes 4915216 | tf_op jit(solution)/shard_map/all_gather | solution.py:282
  214.2 7.5 reshape.439
  228.6 5.6 multiply_convert_fusion.5
  234.2 36.8 %all-gather.12.cloned.1.call-done = bf16[2560,960]{1,0:T(8,128)(2,1)} async-done(((bf16[160,960]{1,0:T(8,128)(2,1)}), bf16[2560,960]{1,0:T(8,128)(2,1)}) %all-gather.12.cloned.1.call-update) | async-done | bytes 4915216 | tf_op jit(solution)/shard_map/all_gather | solution.py:283
  270.9 6.4 multiply_reduce_fusion.7
  298.6 11.2 %multiply_convert_fusion.2 = (bf16[384,2560]{1,0:T(8,128)(2,1)}, bf16[384,2560]{1,0:T(8,128)(2,1)}, bf16[384,2560]{1,0:T(8,128)(2,1)}) fusion(f32[384,2560]{1,0:T(8,128)} %fusion.105, f32[384,2560]{1,0:T(8,128)} %fusion.106, bf16[384,960]{0,1:T(8,128)(2,1)} %param.23, bf16[2560,960]{1,0:T(8,128)(2,1)} %all-gather.12.cloned.1.call-done), kind=kOutput, calls=%fused_computation.37 | convolution fusion | flops 1903165440 | bytes 19415040 | tf_op jit(solution)/shard_map/dot_general | solution.py:74
  327.5 16.5 %fusion.47 = f32[384,5,64]{0,2,1:T(8,128)} fusion(f32[5,384,384,3]{2,1,3,0:T(8,128)} %fusion.108, f32[5,3,384,384]{2,3,1,0:T(8,128)} %copy-done.1, f32[5,3,384]{2,1,0:T(4,128)S(1)} %log_add_fusion.1, bf16[384,5,3,32]{0,3,2,1:T(8,128)(2,1)} %bitcast.282, bf16[384,5,3,32]{0,3,2,1:T(8,128)(2,1)} %bitcast.280), kind=kOutput, calls=%fused_computation.93 | convolution fusion | flops 300079104 | bytes 18946560 | tf_op jit(solution)/shard_map/krtu,tkrd->ukd/dot_general | solution.py:221
  343.9 16.8 %fusion.28 = f32[5,64,3,384]{3,1,2,0:T(8,128)} fusion(f32[5,384,384,3]{2,1,3,0:T(8,128)} %fusion.108, f32[5,3,384,384]{2,3,1,0:T(8,128)} %copy-done.1, f32[5,3,384]{2,1,0:T(4,128)S(1)} %log_add_fusion.1, bf16[384,5,32]{0,2,1:T(8,128)(2,1)} %copy-done.72, bf16[384,5,32]{0,2,1:T(8,128)(2,1)S(1)} %copy-done.71), kind=kOutput, calls=%fused_computation.45 | convolution fusion | flops 299096064 | bytes 19438080 | tf_op jit(solution)/shard_map/krtu,ukd->tkrd/dot_general | solution.py:220
  369.9 6.7 fusion.65
  376.7 8.8 %multiply_convert_fusion = (bf16[384,2560]{1,0:T(8,128)(2,1)}, bf16[384,2560]{1,0:T(8,128)(2,1)S(1)}) fusion(f32[384,2560]{1,0:T(8,128)S(1)} %copy-done.27, f32[384,2560]{1,0:T(8,128)} %get-tuple-element.77, bf16[2560,960]{1,0:T(8,128)(2,1)} %all-gather.12.cloned.1.call-done, f32[384,960]{0,1:T(8,128)S(1)} %multiply_add_fusion.1), kind=kOutput, calls=%fused_computation.35 | convolution fusion | flops 1900584960 | bytes 18186240 | tf_op jit(solution)/shard_map/dot_general | solution.py:74
  394.7 5.1 fusion.110
  402.1 16.1 %fusion.46 = f32[384,5,64]{0,2,1:T(8,128)} fusion(f32[5,384,384,3]{2,1,3,0:T(8,128)} %fusion.110, f32[5,3,384,384]{2,3,1,0:T(8,128)} %copy-done, f32[5,3,384]{2,1,0:T(4,128)} %log_add_fusion, bf16[384,5,3,32]{0,3,2,1:T(8,128)(2,1)} %bitcast.278, bf16[384,5,3,32]{0,3,2,1:T(8,128)(2,1)} %bitcast.276), kind=kOutput, calls=%fused_computation.92 | convolution fusion | flops 300079104 | bytes 18946560 | tf_op jit(solution)/shard_map/krtu,tkrd->ukd/dot_general | solution.py:221
  418.2 16.1 %fusion.31 = f32[5,64,3,384]{3,1,2,0:T(8,128)} fusion(f32[5,384,384,3]{2,1,3,0:T(8,128)} %fusion.110, f32[5,3,384,384]{2,3,1,0:T(8,128)} %copy-done, f32[5,3,384]{2,1,0:T(4,128)} %log_add_fusion, bf16[384,5,32]{0,2,1:T(8,128)(2,1)} %get-tuple-element.66, bf16[384,5,32]{0,2,1:T(8,128)(2,1)} %get-tuple-element.65), kind=kOutput, calls=%fused_computation.48 | convolution fusion | flops 299096064 | bytes 19438080 | tf_op jit(solution)/shard_map/krtu,ukd->tkrd/dot_general | solution.py:220
  437.1 7.8 add_convert_fusion
  475.0 179.4 %fusion.97 = (bf16[64,960]{1,0:T(8,128)(2,1)}, bf16[64,960]{1,0:T(8,128)(2,1)}, bf16[64,2560]{1,0:T(8,128)(2,1)}, bf16[64,2560]{1,0:T(8,128)(2,1)}, bf16[64,320]{1,0:T(8,128)(2,1)S(1)}, /*index=5*/bf16[64,320]{1,0:T(8,128)(2,1)S(1)}) fusion(bf16[960,960]{1,0:T(8,128)(2,1)S(1)} %copy-done.15, bf16[960,960]{1,0:T(8,128)(2,1)} %add_convert_fusion.3, ...), kind=kCustom, calls=%all-reduce-scatter.6 | all-reduce-scatter fusion | flops 7864321 | bytes 15729152
  654.4 8.3 %collective-permute-start.2 = (bf16[60,320]{1,0:T(8,128)(2,1)S(1)}, bf16[60,320]{1,0:T(8,128)(2,1)S(1)}, u32[]{:S(2)}, u32[]{:S(2)}) collective-permute-start(bf16[60,320]{1,0:T(8,128)(2,1)S(1)} %slice.86), channel_id=1, source_target_pairs={{0,1},{1,2},{2,3},{3,4},{4,5},{5,6},{6,7},{7,8},{8,9},{9,10},{10,1... | collective-permute-start | bytes 115208
  669.3 32.0 %all-reduce.16 = (bf16[960]{0:T(1024)(128)(2,1)S(1)}, bf16[960]{0:T(1024)(128)(2,1)S(1)}) all-reduce(bf16[960]{0:T(1024)(128)(2,1)S(1)} %get-tuple-element.89, bf16[960]{0:T(1024)(128)(2,1)S(1)} %get-tuple-element.88), channel_id=9, replica_groups=mesh['dp'=2,'fsdp'=16] {'fsdp'}, use_global_device_ids=true, to_apply=%region_33.34.clone | all-reduce | flops 1920 | bytes 7680
  732.2 6.1 add_convert_fusion.7
  743.5 40.4 %all-reduce.26.cloned.1.call-done = (bf16[60,960]{1,0:T(8,128)(2,1)}, bf16[60,960]{1,0:T(8,128)(2,1)}, bf16[60,2560]{1,0:T(8,128)(2,1)}, bf16[60,2560]{1,0:T(8,128)(2,1)}, bf16[160,960]{1,0:T(8,128)(2,1)}) async-done(((bf16[60,960]{1,0:T(8,128)(2,1)}, bf16[60,960]{1,0:T(8,128)(2,1)}, bf16[60,2560]{1,0:T(8,128)(2,1)}, bf16[60,2560]{1,0:T(8,128)(2,1)}, bf16[160,960]{1,0:T(8,128)(2,1)}), ...) | async-done | bytes 1152016 | tf_op jit(solution)/shard_map/psum | solution.py:331
  (343 shorter events, 181.8 us)
Async XLA Ops:
  7.2 65.8 %copy-start.75 = (bf16[60,320]{1,0:T(8,128)(2,1)S(1)}, bf16[60,320]{1,0:T(8,128)(2,1)}, u32[]{:S(2)}) copy-start(bf16[60,320]{1,0:T(8,128)(2,1)} %param.16) | copy-start | bytes 115204
  7.2 92.5 %all-gather.14.cloned.1.call-start = ((), (), s32[]{:S(2)}) async-start(), calls=%async_computation.3 | async-start | bytes 2228224 | tf_op jit(solution)/shard_map/all_gather | solution.py:277
  7.9 95.8 %all-gather.16.cloned.1.call-start = ((), (), s32[]{:S(2)}) async-start(), calls=%async_computation.4 | async-start | bytes 2228224 | tf_op jit(solution)/shard_map/all_gather | solution.py:280
  8.7 148.8 %all-gather.18.cloned.1.call-start = ((), (), s32[]{:S(2)}) async-start(), calls=%async_computation.5 | async-start | bytes 5570560 | tf_op jit(solution)/shard_map/all_gather | solution.py:281
  9.4 204.8 %all-gather.20.cloned.1.call-start = ((), (), s32[]{:S(2)}) async-start(), calls=%async_computation.6 | async-start | bytes 5570560 | tf_op jit(solution)/shard_map/all_gather | solution.py:282
  10.0 261.0 %all-gather.12.cloned.1.call-start = ((), (), s32[]{:S(2)}) async-start(), calls=%async_computation.1 | async-start | bytes 5570560 | tf_op jit(solution)/shard_map/all_gather | solution.py:283
  10.6 718.8 %reduce-scatter.14.cloned.1.call-start = ((), (), s32[]{:S(2)}) async-start(), calls=%async_computation.2 | async-start | bytes 5570560 | tf_op jit(solution)/shard_map/reduce_scatter | solution.py:320
  72.7 22.7 %copy-start.79 = (s32[1,4]{1,0:T(1,128)S(1)}, s32[1,4]{1,0:T(1,128)}, u32[]{:S(2)}) copy-start(s32[1,4]{1,0:T(1,128)} %param.13) | copy-start | bytes 52
  72.7 22.8 %copy-start.3 = (bf16[384,960]{0,1:T(8,128)(2,1)S(1)}, bf16[384,960]{0,1:T(8,128)(2,1)}, u32[]{:S(2)}) copy-start(bf16[384,960]{0,1:T(8,128)(2,1)} %param.12) | copy-start | bytes 2211844
  73.0 206.6 %copy-start.12 = (bf16[960,320]{1,0:T(8,128)(2,1)}, bf16[960,320]{1,0:T(8,128)(2,1)S(1)}, u32[]{:S(2)}) copy-start(bf16[960,320]{1,0:T(8,128)(2,1)S(1)} %reshape.431) | copy-start | bytes 1843204
  283.8 42.1 %copy-start.1 = (f32[5,3,384,384]{2,3,1,0:T(8,128)}, f32[5,3,384,384]{2,3,1,0:T(8,128)S(1)}, u32[]{:S(2)}) copy-start(f32[5,3,384,384]{2,3,1,0:T(8,128)S(1)} %get-tuple-element.81) | copy-start | bytes 26542084
  445.0 293.3 %all-reduce.24.cloned.1.call-start = ((), (), s32[]{:S(2)}) async-start(), calls=%async_computation.7 | async-start | bytes 198656 | tf_op jit(solution)/shard_map/psum | solution.py:332
  475.0 187.7 %copy-start.14 = (bf16[960,320]{1,0:T(8,128)(2,1)S(1)}, bf16[960,320]{1,0:T(8,128)(2,1)}, u32[]{:S(2)}) copy-start(bf16[960,320]{1,0:T(8,128)(2,1)} %copy-done.12) | copy-start | bytes 1843204
  654.4 55.5 %collective-permute-start.2 = (bf16[60,320]{1,0:T(8,128)(2,1)S(1)}, bf16[60,320]{1,0:T(8,128)(2,1)S(1)}, u32[]{:S(2)}, u32[]{:S(2)}) collective-permute-start(bf16[60,320]{1,0:T(8,128)(2,1)S(1)} %slice.86), channel_id=1, source_target_pairs={{0,1},{1,2},{2,3},{3,4},{4,5},{5,6},{6,7},{7,8},{8,9},{9,10},{10,1... | collective-permute-start | bytes 115208
  667.2 36.6 %copy-start.55 = (bf16[64,960]{1,0:T(8,128)(2,1)S(1)}, bf16[64,960]{1,0:T(8,128)(2,1)}, u32[]{:S(2)}) copy-start(bf16[64,960]{1,0:T(8,128)(2,1)} %get-tuple-element.38) | copy-start | bytes 368644
  667.2 36.6 %copy-start.56 = (bf16[64,960]{1,0:T(8,128)(2,1)S(1)}, bf16[64,960]{1,0:T(8,128)(2,1)}, u32[]{:S(2)}) copy-start(bf16[64,960]{1,0:T(8,128)(2,1)} %get-tuple-element.39) | copy-start | bytes 368644
  667.2 40.5 %copy-start.34 = (bf16[64,2560]{1,0:T(8,128)(2,1)S(1)}, bf16[64,2560]{1,0:T(8,128)(2,1)}, u32[]{:S(2)}) copy-start(bf16[64,2560]{1,0:T(8,128)(2,1)} %get-tuple-element.40) | copy-start | bytes 983044
  667.2 41.3 %copy-start.35 = (bf16[64,2560]{1,0:T(8,128)(2,1)S(1)}, bf16[64,2560]{1,0:T(8,128)(2,1)}, u32[]{:S(2)}) copy-start(bf16[64,2560]{1,0:T(8,128)(2,1)} %get-tuple-element.41) | copy-start | bytes 983044
  702.4 9.9 %collective-permute-start.1 = (bf16[60,320]{1,0:T(8,128)(2,1)S(1)}, bf16[60,320]{1,0:T(8,128)(2,1)S(1)}, u32[]{:S(2)}, u32[]{:S(2)}) collective-permute-start(bf16[60,320]{1,0:T(8,128)(2,1)S(1)} %slice.85), channel_id=1, source_target_pairs={{0,1},{1,2},{2,3},{3,4},{4,5},{5,6},{6,7},{7,8},{8,9},{9,10},{10,1... | collective-permute-start | bytes 115208
  703.9 9.5 %collective-permute-start.3 = (bf16[60,960]{1,0:T(8,128)(2,1)S(1)}, bf16[60,960]{1,0:T(8,128)(2,1)}, u32[]{:S(2)}, u32[]{:S(2)}) collective-permute-start(bf16[60,960]{1,0:T(8,128)(2,1)S(1)} %slice.87), channel_id=1, source_target_pairs={{0,1},{1,2},{2,3},{3,4},{4,5},{5,6},{6,7},{7,8},{8,9},{9,10},{10,1... | collective-permute-start | bytes 345608
  705.8 8.8 %collective-permute-start = (bf16[60,960]{1,0:T(8,128)(2,1)S(1)}, bf16[60,960]{1,0:T(8,128)(2,1)}, u32[]{:S(2)}, u32[]{:S(2)}) collective-permute-start(bf16[60,960]{1,0:T(8,128)(2,1)S(1)} %slice.84), channel_id=1, source_target_pairs={{0,1},{1,2},{2,3},{3,4},{4,5},{5,6},{6,7},{7,8},{8,9},{9,10},{10,1... | collective-permute-start | bytes 345608
  708.6 8.6 %collective-permute-start.5 = (bf16[60,2560]{1,0:T(8,128)(2,1)S(1)}, bf16[60,2560]{1,0:T(8,128)(2,1)S(1)}, u32[]{:S(2)}, u32[]{:S(2)}) collective-permute-start(bf16[60,2560]{1,0:T(8,128)(2,1)S(1)} %slice.89), channel_id=1, source_target_pairs={{0,1},{1,2},{2,3},{3,4},{4,5},{5,6},{6,7},{7,8},{8,9},{9,10},{10,1... | collective-permute-start | bytes 921608
  709.9 13.4 %collective-permute-start.4 = (bf16[60,2560]{1,0:T(8,128)(2,1)}, bf16[60,2560]{1,0:T(8,128)(2,1)S(1)}, u32[]{:S(2)}, u32[]{:S(2)}) collective-permute-start(bf16[60,2560]{1,0:T(8,128)(2,1)} %slice.88), channel_id=1, source_target_pairs={{0,1},{1,2},{2,3},{3,4},{4,5},{5,6},{6,7},{7,8},{8,9},{9,10},{10,1... | collective-permute-start | bytes 921608
  713.3 70.6 %all-reduce.26.cloned.1.call-start = ((), (), s32[]{:S(2)}) async-start(), calls=%async_computation.8 | async-start | bytes 2490368 | tf_op jit(solution)/shard_map/psum | solution.py:331
  (81 other events, 333.6 us)
Sparse Core Ops, SparseCore 0:
  10.2 44.1 all-gather.13
  56.5 42.8 all-gather.15
  101.7 55.7 all-gather.17
  159.6 54.5 all-gather.19
  216.3 54.5 all-gather.11
  445.1 121.6 reduce-scatter.13
  713.5 21.3 all-reduce.23
  738.1 45.8 all-reduce.25
where the time goes:
time: 809 us; the launch traced here: 798 us
  blocking collectives  289 us (36%)
  matrix products  217 us (27%)
  waiting for transfers between devices  166 us (21%)
  local copies, waits for them, and re-layouts  61.7 us (8%)
  other arithmetic  30.1 us (4%)
  between operations  17.6 us (2%)
  starting transfers between devices  16.6 us (2%)
    unnamed x3, blocking collectives  247 us
    unnamed x213, local copies, waits for them, and re-layouts  61.1 us
    all_gather x1, waiting for transfers between devices, shards(): lax.all_gather(w_up, 'fsdp', axis=0, tiled=True)  49.4 us
    dot_general x14, matrix products, matrix_product_backward(): lax.dot_general(left, right, (((1,), (1,)), ((), ())), preferred_element_...  47.1 us
    dot_general x14, matrix products, outer_sum(): lax.dot_general(left, right, (((0,), (0,)), ((), ())), preferred_element_...  42.9 us
    dot_general x14, matrix products, matrix_product(): return jnp.dot(left, right, preferred_element_type=jnp.float32)  40.8 us
    psum x1, waiting for transfers between devices, shards(): lax.psum(shares[0].astype(jnp.bfloat16), 'dp').astype(jnp.float32)  40.4 us
    all_gather x1, waiting for transfers between devices, shards(): lax.all_gather(w_down, 'fsdp', axis=0, tiled=True)  36.8 us
  transfers between devices with their start and end apart: 14, of which 4 were waited for; matrix products, arithmetic and copies ran while one was open for 38% of the time, Pallas kernels for 0%

commit v1 on v0

v1 whole, which is shorter than its diff:
```python
import functools
import math

import jax
import jax.numpy as jnp
from jax import lax
from jax.experimental import pallas as pl
from jax.experimental.pallas import tpu as pltpu
from jax.sharding import PartitionSpec as P

HEAD_SIZE = 64
GROUP = 3
ROPE_BASE = 10000.0
EPS = 1e-05
BF = jnp.bfloat16
F32 = jnp.float32


def layout(doc_lengths, token_count):
    ends = jnp.cumsum(doc_lengths, axis=1)
    starts = ends - doc_lengths
    place = jnp.arange(token_count, dtype=jnp.int32)
    document = jnp.sum((place[None, :, None] >= ends[:, None, :]).astype(jnp.int32), axis=2)
    inside = place[None, :] < ends[:, -1:]
    segment = jnp.where(inside, document, -1)
    chosen = (
        document[:, :, None] == jnp.arange(doc_lengths.shape[1], dtype=jnp.int32)[None, None, :]
    )
    begin = jnp.sum(jnp.where(chosen, starts[:, None, :], 0), axis=2)
    positions = jnp.where(inside, place[None, :] - begin, 0)
    causal = place[:, None] >= place[None, :]
    same = (segment[:, :, None] == segment[:, None, :]) & (segment[:, :, None] >= 0)
    allowed = same & causal[None] | (place[:, None] == place[None, :])[None]
    return (positions, allowed)


def rotation(positions):
    half = HEAD_SIZE // 2
    frequency = jnp.exp(
        jnp.arange(half, dtype=jnp.float32) * (-2.0 * math.log(ROPE_BASE) / HEAD_SIZE)
    )
    angle = positions.astype(jnp.float32)[..., None] * frequency
    return (jnp.cos(angle), jnp.sin(angle))


def apply_rotary(values, cosine_table, sine_table):
    half = values.shape[-1] // 2
    first = values[..., :half]
    second = values[..., half:]
    cosine_table = cosine_table[..., None, :]
    sine_table = sine_table[..., None, :]
    return jnp.concatenate(
        [first * cosine_table - second * sine_table, second * cosine_table + first * sine_table],
        axis=-1,
    )


class Place:
    def __init__(self, mesh):
        self.n, self.groups = mesh.shape["fsdp"], mesh.shape["dp"]
        self.nz = self.n // 4
        i = lax.axis_index("fsdp")
        self.c, self.y, self.z = i % 2, (i // 2) % 2, i // 4
        self.p = lax.axis_index("dp") % 2

    def swap_core(self, v):
        return lax.ppermute(v, "fsdp", [(i, i ^ 1) for i in range(self.n)])

    def shift_z(self, v, k):
        return lax.ppermute(v, "fsdp", [(i, (i + 4 * k) % self.n) for i in range(self.n)])

    def swap_x(self, v):
        return lax.ppermute(v, "dp", [(d, d ^ 1) for d in range(self.groups)])

    def cross(self, v, first):
        pairs = []
        for d in range(self.groups):
            for i in range(self.n):
                along_x = (i % 2 == 0) == first
                e, j = (d ^ 1, i) if along_x else (d, i ^ 2)
                pairs.append((d * self.n + i, e * self.n + j))
        return lax.ppermute(v, ("dp", "fsdp"), pairs)


def pick(v, k, axis=0):
    return lax.dynamic_index_in_dim(v, k, axis, keepdims=False)


def gather_pieces(at, shard):
    rows, cols = shard.shape
    halves = shard.reshape(2, rows // 2, cols)
    keep = pick(halves, at.c)
    got = at.swap_core(pick(halves, 1 - at.c))
    mine = jnp.where(at.p == at.c, keep, got)
    rest = jnp.where(at.p == at.c, got, keep)
    del rest
    line = jnp.stack([mine] + [at.shift_z(mine, k) for k in range(1, at.nz)])
    second = at.cross(line, False)
    both = jnp.concatenate([line, second])
    third = at.cross(both, True)
    own = jnp.concatenate([both, third])
    return own, at.swap_core(own)


def assemble(at, pieces, splits):
    own, other = pieces
    count, half, cols = own.shape
    order = []
    for core_of_piece in (0, 1):
        h = at.c if core_of_piece == 0 else 1 - at.c
        for j in range(count):
            dz, slot = j % at.nz, j // at.nz
            lo, hi = slot % 2, slot // 2
            dy = jnp.where(h == 0, lo, hi)
            dc = jnp.where(h == 0, hi, lo)
            z = (at.z - dz + at.nz) % at.nz
            order.append((((z * 2 + (at.y ^ dy)) * 2 + (at.p ^ dc)) * 2 + h).astype(jnp.int32))
    order = jnp.stack(order)
    bounds = [0]
    for width in splits:
        bounds.append(bounds[-1] + width)

    def body(order_ref, own_ref, other_ref, *rest):
        outs, sem = rest[:-1], rest[-1]
        copies = []
        for source, ref in enumerate((own_ref, other_ref)):
            for j in range(count):
                to = order_ref[source * count + j]
                for k, out in enumerate(outs):
                    copies.append(
                        pltpu.make_async_copy(
                            ref.at[j, :, pl.ds(bounds[k], splits[k])],
                            out.at[to],
                            sem.at[(source * count + j) * len(outs) + k],
                        )
                    )
        for copy in copies:
            copy.start()
        for copy in copies:
            copy.wait()

    outs = pl.pallas_call(
        body,
        grid_spec=pltpu.PrefetchScalarGridSpec(
            num_scalar_prefetch=1,
            grid=(),
            in_specs=[pl.BlockSpec(memory_space=pl.ANY)] * 2,
            out_specs=[pl.BlockSpec(memory_space=pltpu.VMEM)] * len(splits),
            scratch_shapes=[pltpu.SemaphoreType.DMA((2 * count * len(splits),))],
        ),
        out_shape=[jax.ShapeDtypeStruct((2 * count, half, w), BF) for w in splits],
    )(order, own, other)
    return [o.reshape(2 * count * half, o.shape[2]) for o in outs]


def reduce_scatter(at, grad):
    n, rows, cols = grad.shape
    half = rows // 2
    g = grad.reshape(at.nz, 4, 2, half, cols)
    own = pick(g, at.c, 2)
    got = at.swap_core(pick(g, 1 - at.c, 2))

    def chip(k):
        return pick(own, k, 1).astype(F32) + pick(got, k, 1).astype(F32)

    mine = jnp.where(at.c == 0, at.p, at.y)

    def slot(u, v):
        return jnp.where(at.c == 0, 2 * v + u, 2 * u + v)

    first = at.cross(jnp.stack([chip(slot(1 - mine, v)) for v in (0, 1)]).astype(BF), True)
    mine2 = jnp.where(at.c == 0, at.y, at.p)

    def stage1(v):
        return chip(slot(mine, v)) + pick(first, v).astype(F32)

    second = at.cross(stage1(1 - mine2).astype(BF), False)
    kept = stage1(mine2) + second.astype(F32)
    low = kept.astype(BF)
    total = pick(kept, at.z)
    for k in range(1, at.nz):
        total = total + at.shift_z(pick(low, (at.z + k) % at.nz), k).astype(F32)
    step = 2
    while step < at.groups:
        total = total + lax.ppermute(
            total.astype(BF), "dp", [(d, d ^ step) for d in range(at.groups)]
        ).astype(F32)
        step *= 2
    low = total.astype(BF)
    swapped = at.swap_x(low)
    mine_here = at.p == at.c
    keep = jnp.where(mine_here, low, swapped)
    other = at.swap_core(jnp.where(mine_here, swapped, low))
    return jnp.concatenate(
        [jnp.where(at.c == 0, keep, other), jnp.where(at.c == 0, other, keep)]
    ).astype(F32)


def product(left, right):
    return jnp.dot(left, right, preferred_element_type=F32)


def product_back(left, right):
    return lax.dot_general(left, right, (((1,), (1,)), ((), ())), preferred_element_type=F32)


def outer_sum(left, right):
    return lax.dot_general(left, right, (((0,), (0,)), ((), ())), preferred_element_type=F32)


def norm_forward(values, gain, width):
    scale = lax.rsqrt(jnp.sum(values * values, axis=-1, keepdims=True) / width + EPS)
    return (scale, (values * scale * gain).astype(BF))


def norm_backward(values, scale, gain, grad, width):
    unit = values * scale
    gain_grad = jnp.sum(grad * unit, axis=0)
    inner = grad * gain
    mean = jnp.sum(inner * unit, axis=-1, keepdims=True) / width
    return (gain_grad, scale * (inner - unit * mean))


def scores(q, k, allowed):
    score = jnp.einsum("tkrd,ukd->krtu", q, k, preferred_element_type=F32) * HEAD_SIZE ** (-0.5)
    return jnp.where(allowed, score, -1e30)


def block_forward(source, w, rope, allowed, width):
    wqkv, wo, wgate, wup, wdown, gain_attn, gain_ffn = w
    cos, sin = rope
    t = source.shape[0]
    kv = (wqkv.shape[1] - width) // 2
    kvh = kv // HEAD_SIZE
    scale_attn, a1 = norm_forward(source, gain_attn, width)
    qkv = product(a1, wqkv)
    q = apply_rotary(qkv[:, :width].reshape(t, -1, HEAD_SIZE), cos, sin).astype(BF)
    q = q.reshape(t, kvh, GROUP, HEAD_SIZE)
    k = apply_rotary(qkv[:, width : width + kv].reshape(t, kvh, HEAD_SIZE), cos, sin).astype(BF)
    v = qkv[:, width + kv :].astype(BF).reshape(t, kvh, HEAD_SIZE)
    score = scores(q, k, allowed)
    highest = jnp.max(score, axis=-1, keepdims=True)
    powers = jnp.exp(score - highest)
    summed = jnp.sum(powers, axis=-1, keepdims=True)
    lse = highest + jnp.log(summed)
    prob = (powers / summed).astype(BF)
    mixed = jnp.einsum("krtu,ukd->tkrd", prob, v, preferred_element_type=F32)
    mixed = mixed.reshape(t, width).astype(BF)
    hidden = source + product(mixed, wo)
    scale_ffn, a2 = norm_forward(hidden, gain_ffn, width)
    gate = product(a2, wgate)
    up = product(a2, wup)
    inner = (jax.nn.silu(gate) * up).astype(BF)
    result = hidden + product(inner, wdown)
    return result, (source, scale_attn, a1, q, k, v, lse, mixed, hidden, scale_ffn, a2, gate, up, inner)


def block_backward(grad, w, kept, rope, allowed, width):
    wqkv, wo, wgate, wup, wdown, gain_attn, gain_ffn = w
    source, scale_attn, a1, q, k, v, lse, mixed, hidden, scale_ffn, a2, gate, up, inner = kept
    cos, sin = rope
    t = source.shape[0]
    kvh = k.shape[1]
    cl = grad.astype(BF)
    g_inner = product_back(cl, wdown)
    sg = jax.nn.sigmoid(gate)
    g_gate = (g_inner * up * sg * (1.0 + gate * (1.0 - sg))).astype(BF)
    g_up = (g_inner * gate * sg).astype(BF)
    g_a2 = product_back(g_gate, wgate) + product_back(g_up, wup)
    g_gain_ffn, g_hidden = norm_backward(hidden, scale_ffn, gain_ffn, g_a2, width)
    g_hidden = grad + g_hidden
    gl = g_hidden.astype(BF)
    g_mixed = product_back(gl, wo).astype(BF).reshape(t, kvh, GROUP, HEAD_SIZE)
    p = jnp.exp(scores(q, k, allowed) - lse)
    g_p = jnp.einsum("tkrd,ukd->krtu", g_mixed, v, preferred_element_type=F32)
    g_v = jnp.einsum("krtu,tkrd->ukd", p.astype(BF), g_mixed, preferred_element_type=F32)
    g_s = p * (g_p - jnp.sum(p * g_p, axis=-1, keepdims=True))
    g_s = (g_s * HEAD_SIZE ** (-0.5)).astype(BF)
    g_q = jnp.einsum("krtu,ukd->tkrd", g_s, k, preferred_element_type=F32)
    g_k = jnp.einsum("krtu,tkrd->ukd", g_s, q, preferred_element_type=F32)
    g_q = apply_rotary(g_q.reshape(t, -1, HEAD_SIZE), cos, -sin).reshape(t, -1).astype(BF)
    g_k = apply_rotary(g_k, cos, -sin).reshape(t, -1).astype(BF)
    g_v = g_v.reshape(t, -1).astype(BF)
    g_qkv = jnp.concatenate([g_q, g_k, g_v], axis=1)
    g_a1 = product_back(g_qkv, wqkv)
    g_gain_attn, g_source = norm_backward(source, scale_attn, gain_attn, g_a1, width)
    return g_hidden + g_source, (a1, g_qkv, mixed, gl, a2, g_gate, g_up, inner, cl, g_gain_attn, g_gain_ffn)


def spread(v, n, real, padded):
    lead = v.shape[:-1]
    v = v.reshape(lead + (n, real))
    v = jnp.pad(v, [(0, 0)] * len(lead) + [(0, 0), (0, padded - real)])
    return v.reshape(lead + (n * padded,))


def narrow(v, n, real, padded):
    lead = v.shape[:-1]
    return v.reshape(lead + (n, padded))[..., :real].reshape(lead + (n * real,))


def shards(mesh, tokens, lengths, w_query, key_weight, value_weight, output_weight, w_gate, w_up, w_down, gain_attn, gain_ffn, out_grad):
    at = Place(mesh)
    n = at.n
    real, width = w_query.shape
    padded = -(-(real + 2) // 16) * 16
    wide = n * padded

    def pad_rows(v):
        return jnp.pad(v, ((0, padded - v.shape[0]), (0, 0)))

    qkv = jnp.concatenate([w_query, key_weight, value_weight], axis=1)
    gains = jnp.pad(jnp.stack([gain_attn, gain_ffn]), ((0, 0), (0, qkv.shape[1] - real)))
    qkv = pad_rows(jnp.concatenate([qkv, gains]))
    attn = jnp.concatenate([pad_rows(spread(output_weight, n, real, padded)), qkv], axis=1)
    down = spread(w_down, n, real, padded)

    wo, wqkv = assemble(at, gather_pieces(at, attn), [wide, qkv.shape[1]])
    (wgate,) = assemble(at, gather_pieces(at, pad_rows(w_gate)), [w_gate.shape[1]])
    (wup,) = assemble(at, gather_pieces(at, pad_rows(w_up)), [w_up.shape[1]])
    (wdown,) = assemble(at, gather_pieces(at, down), [wide])
    wo = wo.reshape(n, padded, wide)[:, :real].reshape(width, wide)
    gains = wqkv.reshape(n, padded, -1)[:, real : real + 2, :padded].astype(F32)
    weights = (wqkv, wo, wgate, wup, wdown, gains[:, 0].reshape(wide), gains[:, 1].reshape(wide))

    positions, allowed = layout(lengths, tokens.shape[0])
    rope = rotation(positions[0])
    allowed = allowed[0]
    x = spread(tokens, n, real, padded).astype(F32)
    first, kept1 = block_forward(x, weights, rope, allowed, width)
    second, kept2 = block_forward(first, weights, rope, allowed, width)
    cot = spread(out_grad, n, real, padded).astype(F32)
    carried, t2 = block_backward(cot, weights, kept2, rope, allowed, width)
    g_x, t1 = block_backward(carried, weights, kept1, rope, allowed, width)
    a1, g_qkv, mixed, gl, a2, g_gate, g_up, inner, cl = (
        jnp.concatenate([l, r]) for l, r in zip(t1[:9], t2[:9])
    )
    gain_sums = jnp.stack([t1[9] + t2[9], t1[10] + t2[10]], axis=0)

    g_down = outer_sum(inner, cl).astype(BF).reshape(n, -1, wide)
    r_down = reduce_scatter(at, g_down)
    r_gate = reduce_scatter(at, outer_sum(a2, g_gate).astype(BF).reshape(n, padded, -1))
    r_up = reduce_scatter(at, outer_sum(a2, g_up).astype(BF).reshape(n, padded, -1))
    g_out = outer_sum(spread(mixed, n, real, padded), gl).astype(BF).reshape(n, padded, wide)
    g_in = outer_sum(a1, g_qkv).astype(BF).reshape(n, padded, -1)
    g_gains = gain_sums.astype(BF).reshape(2, n, padded).transpose(1, 0, 2)
    g_in = lax.dynamic_update_slice(g_in, g_gains, (0, real, 0))
    r_attn = reduce_scatter(at, jnp.concatenate([g_out, g_in], axis=2))
    r_in = r_attn[:, wide:]
    kv = (r_in.shape[1] - width) // 2
    return (
        narrow(second.astype(BF), n, real, padded),
        narrow(g_x.astype(BF), n, real, padded),
        r_in[:real, :width],
        r_in[:real, width : width + kv],
        r_in[:real, width + kv :],
        narrow(r_attn[:real, :wide], n, real, padded),
        r_gate[:real],
        r_up[:real],
        narrow(r_down, n, real, padded),
        r_in[real, :real],
        r_in[real + 1, :real],
    )


def solution(mesh):
    rows, split, gain = P(("dp", "fsdp"), None), P("fsdp", None), P("fsdp")
    return jax.shard_map(
        functools.partial(shards, mesh),
        mesh=mesh,
        in_specs=(rows, rows) + (split,) * 7 + (gain, gain, rows),
        out_specs=(rows, rows) + (split,) * 7 + (gain, gain),
        check_vma=False,
    )
```

time: 809 us -> 602 us (0.74)
  blocking collectives: 289 us -> 0 us
  starting transfers between devices: 16.6 us -> 107 us
  matrix products: 217 us -> 190 us
  Pallas kernels: 0 us -> 23.7 us
  waiting for transfers between devices: 166 us -> 144 us
  other arithmetic: 30.1 us -> 51.4 us
  local copies, waits for them, and re-layouts: 61.7 us -> 78.9 us
  between operations: 17.6 us -> 3.18 us
    unnamed x3 -> x0, blocking collectives: 247 us -> none
    ppermute x0 -> x60, waiting for transfers between devices: none -> 144 us  [the longest x16 108 us: cross(): return lax.ppermute(v, ('dp', 'fsdp'), pairs)]
    all_gather x5 -> x0, waiting for transfers between devices: 123 us -> none  [the longest x1 49.4 us: shards(): lax.all_gather(w_up, 'fsdp', axis=0, tiled=True)]
    ppermute x0 -> x60, starting transfers between devices: none -> 107 us  [the longest x24 66.6 us: shift_z(): lax.ppermute(v, 'fsdp', [(i, (i + 4 * k) % self.n) for i in range(self.n)])]
    all_gather x2 -> x0, blocking collectives: 42.3 us -> none  [the longest x1 21.9 us: shards(): lax.all_gather(value_weight, 'fsdp', axis=0, tiled=True)]
    psum x2 -> x0, waiting for transfers between devices: 40.4 us -> none  [the longest x1 40.4 us: shards(): lax.psum(shares[0].astype(jnp.bfloat16), 'dp').astype(jnp.float32)]
    unnamed x213 -> x226, local copies, waits for them, and re-layouts: 61.1 us -> 24.9 us
    pallas_call x0 -> x4, Pallas kernels: none -> 23.7 us  [assemble(): pl.pallas_call(body, grid_spec=pltpu.PrefetchScalarGridSpec(num_scalar_pr...]
  transfers between devices with their start and end apart: 14 -> 60, of which waited for: 4 -> 21; matrix products, arithmetic and copies ran while one was open for 38% -> 17% of each run, Pallas kernels for 0% -> 3%
where the time goes in v1:
time: 602 us; the launch traced here: 597 us
  matrix products  190 us (32%)
  waiting for transfers between devices  144 us (24%)
  starting transfers between devices  107 us (18%)
  local copies, waits for them, and re-layouts  78.9 us (13%)
  other arithmetic  51.4 us (9%)
  Pallas kernels  23.7 us (4%)
    ppermute x16, waiting for transfers between devices, cross(): return lax.ppermute(v, ('dp', 'fsdp'), pairs)  108 us
    ppermute x24, starting transfers between devices, shift_z(): lax.ppermute(v, 'fsdp', [(i, (i + 4 * k) % self.n) for i in range(self.n)])  66.6 us
    dot_general x10, matrix products, product_back(): lax.dot_general(left, right, (((1,), (1,)), ((), ())), preferred_element_...  38 us
    dot_general x10, matrix products, product(): return jnp.dot(left, right, preferred_element_type=F32)  37.3 us
    dot_general x5, matrix products, outer_sum(): lax.dot_general(left, right, (((0,), (0,)), ((), ())), preferred_element_...  34.7 us
    dot_general x2, matrix products, block_backward(): g_k = jnp.einsum('krtu,tkrd->ukd', g_s, q, preferred_element_type=F32)  29.6 us
    dot_general x2, matrix products, block_backward(): g_q = jnp.einsum('krtu,ukd->tkrd', g_s, k, preferred_element_type=F32)  29.5 us
    ppermute x24, waiting for transfers between devices, shift_z(): lax.ppermute(v, 'fsdp', [(i, (i + 4 * k) % self.n) for i in range(self.n)])  29.4 us
  transfers between devices with their start and end apart: 60, of which 21 were waited for; matrix products, arithmetic and copies ran while one was open for 17% of the time, Pallas kernels for 3%

profile of v1, /device:TPU:0, one launch (start us, length us, event | category | flops | bytes accessed | tf_op | source)
XLA Modules:
  0.0 597.0 jit_solution(10259818486933072674)
XLA Ops:
  25.2 9.3 %collective-permute-start.22 = (bf16[80,1024]{1,0:T(8,128)(2,1)S(1)}, bf16[80,1024]{1,0:T(8,128)(2,1)S(1)}, u32[]{:S(2)}, u32[]{:S(2)}) collective-permute-start(bf16[80,1024]{1,0:T(8,128)(2,1)S(1)} %get-tuple-element.38), channel_id=1, source_target_pairs={{0,4},{1,5},{2,6},{3,7},{4,8},{5,9},{6,10},{7,11},{8,12},{9,13},{1... | collective-permute-start | bytes 491528 | tf_op jit(solution)/shard_map/ppermute | solution.py:70
  73.1 8.6 %collective-permute-done.18 = bf16[4,32,2560]{2,1,0:T(8,128)(2,1)S(1)} collective-permute-done((bf16[4,32,2560]{2,1,0:T(8,128)(2,1)S(1)}, bf16[4,32,2560]{2,1,0:T(8,128)(2,1)S(1)}, u32[]{:S(2)}, u32[]{:S(2)}) %collective-permute-start.18) | collective-permute-done | bytes 655392 | tf_op jit(solution)/shard_map/ppermute | solution.py:82
  85.9 10.0 %collective-permute-done.25 = bf16[4,80,1024]{2,1,0:T(8,128)(2,1)S(1)} collective-permute-done((bf16[4,80,1024]{2,1,0:T(8,128)(2,1)S(1)}, bf16[4,80,1024]{2,1,0:T(8,128)(2,1)S(1)}, u32[]{:S(2)}, u32[]{:S(2)}) %collective-permute-start.25) | collective-permute-done | bytes 655392 | tf_op jit(solution)/shard_map/ppermute | solution.py:82
  99.2 11.3 %collective-permute-done.4 = bf16[4,32,2624]{2,1,0:T(8,128)(2,1)S(1)} collective-permute-done((bf16[4,32,2624]{2,1,0:T(8,128)(2,1)S(1)}, bf16[4,32,2624]{2,1,0:T(8,128)(2,1)S(1)}, u32[]{:S(2)}, u32[]{:S(2)}) %collective-permute-start.4) | collective-permute-done | bytes 671776 | tf_op jit(solution)/shard_map/ppermute | solution.py:82
  121.4 11.0 %collective-permute-done.26 = bf16[8,80,1024]{2,1,0:T(8,128)(2,1)S(1)} collective-permute-done((bf16[8,80,1024]{2,1,0:T(8,128)(2,1)S(1)}, bf16[8,80,1024]{2,1,0:T(8,128)(2,1)S(1)}, u32[]{:S(2)}, u32[]{:S(2)}) %collective-permute-start.26) | collective-permute-done | bytes 1310752 | tf_op jit(solution)/shard_map/ppermute | solution.py:82
  135.6 11.6 %collective-permute-done.5 = bf16[8,32,2624]{2,1,0:T(8,128)(2,1)S(1)} collective-permute-done((bf16[8,32,2624]{2,1,0:T(8,128)(2,1)S(1)}, bf16[8,32,2624]{2,1,0:T(8,128)(2,1)S(1)}, u32[]{:S(2)}, u32[]{:S(2)}) %collective-permute-start.5) | collective-permute-done | bytes 1343520 | tf_op jit(solution)/shard_map/ppermute | solution.py:82
  173.9 6.7 %fusion.173 = f32[384,2560]{1,0:T(8,128)} fusion(bf16[384,1024]{0,1:T(8,128)(2,1)S(1)} %bitcast.614, bf16[2560,1024]{1,0:T(8,128)(2,1)} %bitcast.571), kind=kOutput, calls=%fused_computation.414 | convolution fusion | flops 2013265920 | bytes 9961472 | tf_op jit(solution)/shard_map/dot_general | solution.py:204
  180.5 6.2 %shard_map.203 = (bf16[32,32,1024]{2,1,0:T(8,128)(2,1)}, bf16[32,32,1600]{2,1,0:T(8,128)(2,1)}) custom-call(s32[32]{0:T(128)} %stack.158.order_ref, bf16[16,32,2624]{2,1,0:T(8,128)(2,1)} %constant_dynamic-update-slice_fusion.5.own_ref, bf16[16,32,2624]{2,1,0:T(8,128)(2,1)} %collective-permute-done.6.other_ref), custom_call_target="tpu_custom_call" | custom-call | tf_op jit(solution)/shard_map/pallas_call | solution.py:142
  237.5 7.1 %multiply_convert_fusion.3 = (bf16[384,2560]{1,0:T(8,128)(2,1)}, bf16[384,2560]{1,0:T(8,128)(2,1)}, bf16[384,2560]{1,0:T(8,128)(2,1)}) fusion(f32[384,2560]{1,0:T(8,128)S(1)} %copy-done.77, f32[384,2560]{1,0:T(8,128)} %fusion.172, bf16[384,1024]{1,0:T(8,128)(2,1)S(1)} %multiply_convert_fusion.7, bf16[1024,2560]{1,0:T(8,128)(2,1)S(1)} %bitcast.582), kind=kOutput, calls=%fused_computation.55 | convolution fusion | flops 2028994560 | bytes 19791872 | tf_op jit(solution)/shard_map/dot_general | solution.py:200
  261.1 15.7 %fusion.90 = f32[384,5,64]{0,2,1:T(8,128)} fusion(f32[5,384,384,3]{2,1,3,0:T(8,128)} %fusion.175, f32[5,3,384,384]{2,3,1,0:T(8,128)} %copy-done.1, f32[5,3,384]{2,1,0:T(4,128)} %copy-done.63, bf16[384,5,3,32]{0,3,2,1:T(8,128)(2,1)} %bitcast.666, bf16[384,5,3,32]{0,3,2,1:T(8,128)(2,1)} %bitcast.664), kind=kOutput, calls=%fused_computation.186 | convolution fusion | flops 300079104 | bytes 18946560 | tf_op jit(solution)/shard_map/krtu,tkrd->ukd/dot_general | solution.py:280
  276.8 16.3 %fusion.33 = f32[5,64,3,384]{3,1,2,0:T(8,128)} fusion(f32[5,384,384,3]{2,1,3,0:T(8,128)} %fusion.175, f32[5,3,384,384]{2,3,1,0:T(8,128)} %copy-done.1, f32[5,3,384]{2,1,0:T(4,128)} %copy-done.63, bf16[384,5,32]{0,2,1:T(8,128)(2,1)} %copy-done.69, bf16[384,5,32]{0,2,1:T(8,128)(2,1)} %copy-done.68), kind=kOutput, calls=%fused_computation.66 | convolution fusion | flops 299096064 | bytes 19438080 | tf_op jit(solution)/shard_map/krtu,ukd->tkrd/dot_general | solution.py:279
  302.7 9.0 %multiply_convert_fusion.1 = (bf16[384,2560]{1,0:T(8,128)(2,1)S(1)}, bf16[384,2560]{1,0:T(8,128)(2,1)S(1)}) fusion(f32[384,2560]{1,0:T(8,128)S(1)} %copy-done.81, f32[384,2560]{1,0:T(8,128)} %get-tuple-element.142, bf16[384,1024]{1,0:T(8,128)(2,1)S(1)} %get-tuple-element.35, bf16[2560,1024]{1,0:T(8,128)(2,1)} %bitcast.572), kind=kOutput, calls=%fused_computation.53 | convolution fusion | flops 2026045440 | bytes 17825792 | tf_op jit(solution)/shard_map/dot_general | solution.py:204
  327.5 13.8 %fusion.89 = f32[384,5,64]{0,2,1:T(8,128)} fusion(f32[5,384,384,3]{2,1,3,0:T(8,128)} %fusion.177, f32[5,3,384,384]{2,3,1,0:T(8,128)} %copy-done, f32[5,3,384]{2,1,0:T(4,128)} %copy-done.61, bf16[384,5,3,32]{0,3,2,1:T(8,128)(2,1)S(1)} %bitcast.662, bf16[384,5,3,32]{0,3,2,1:T(8,128)(2,1)S(1)} %bitcast.660), kind=kOutput, calls=%fused_computation.185 | convolution fusion | flops 300079104 | bytes 18946560 | tf_op jit(solution)/shard_map/krtu,tkrd->ukd/dot_general | solution.py:280
  341.4 13.2 %fusion.36 = f32[5,64,3,384]{3,1,2,0:T(8,128)S(1)} fusion(f32[5,384,384,3]{2,1,3,0:T(8,128)} %fusion.177, f32[5,3,384,384]{2,3,1,0:T(8,128)} %copy-done, f32[5,3,384]{2,1,0:T(4,128)S(1)} %copy-done.62, bf16[384,5,32]{0,2,1:T(8,128)(2,1)S(1)} %copy-done.67, bf16[384,5,32]{0,2,1:T(8,128)(2,1)S(1)} %copy-done.65), kind=kOutput, calls=%fused_computation.69 | convolution fusion | flops 299096064 | bytes 19438080 | tf_op jit(solution)/shard_map/krtu,ukd->tkrd/dot_general | solution.py:279
  354.6 9.1 %convolution_convert_fusion.2 = bf16[1024,2560]{1,0:T(8,128)(2,1)} fusion(bf16[384,2560]{1,0:T(8,128)(2,1)} %get-tuple-element.57, bf16[384,2560]{1,0:T(8,128)(2,1)} %copy-done.79, bf16[384,1024]{1,0:T(8,128)(2,1)} %copy-done.31, bf16[384,1024]{1,0:T(8,128)(2,1)S(1)} %copy-done.30), kind=kOutput, calls=%fused_computation.36 | convolution fusion | flops 4040163328 | bytes 10747904 | tf_op jit(solution)/shard_map/dot_general | solution.py:208
  363.7 6.1 %convolution_convert_fusion.1 = bf16[1024,2560]{1,0:T(8,128)(2,1)} fusion(bf16[384,2560]{1,0:T(8,128)(2,1)S(1)} %copy-done.82, bf16[384,2560]{1,0:T(8,128)(2,1)S(1)} %copy-done.84, bf16[384,1024]{1,0:T(8,128)(2,1)S(1)} %copy-done.32, bf16[384,1024]{1,0:T(8,128)(2,1)S(1)} %copy-done.30), kind=kOutput, calls=%fused_computation.35 | convolution fusion | flops 4040163328 | bytes 10747904 | tf_op jit(solution)/shard_map/dot_general | solution.py:208
  374.4 13.1 %convolution_convert_fusion.3 = bf16[1024,1600]{0,1:T(8,128)(2,1)} fusion(bf16[384,320]{0,1:T(8,128)(2,1)S(1)} %bitcast.668, bf16[384,320]{0,1:T(8,128)(2,1)S(1)} %bitcast.670, bf16[384,960]{0,1:T(8,128)(2,1)S(1)} %bitcast.644, bf16[384,320]{0,1:T(8,128)(2,1)S(1)} %bitcast.672, bf16[384,320]{0,1:T(8,128)(2,1)S(1)} %bitcast.674, ...), kind=kOutput, calls=%fused_computation.60 | convolution fusion | flops 2536112128 | bytes 7307264 | tf_op jit(solution)/shard_map/dot_general | solution.py:208
  418.9 6.6 %add_convert_fusion.1 = bf16[384,1024]{1,0:T(8,128)(2,1)} fusion(f32[384,1024]{1,0:T(8,128)} %copy-done.5, bf16[384,2560]{1,0:T(8,128)(2,1)} %get-tuple-element.58, bf16[2560,1024]{1,0:T(8,128)(2,1)} %bitcast.573), kind=kOutput, calls=%fused_computation.111 | convolution fusion | flops 2014052352 | bytes 9568256 | tf_op jit(solution)/shard_map/dot_general | solution.py:200
  456.2 15.9 %collective-permute-done.45 = bf16[2,4,32,2560]{3,2,1,0:T(8,128)(2,1)} collective-permute-done((bf16[2,4,32,2560]{3,2,1,0:T(8,128)(2,1)}, bf16[2,4,32,2560]{3,2,1,0:T(8,128)(2,1)}, u32[]{:S(2)}, u32[]{:S(2)}) %collective-permute-start.45) | collective-permute-done | bytes 1310752 | tf_op jit(solution)/shard_map/ppermute | solution.py:82
  475.4 17.8 %collective-permute-done.53 = bf16[2,4,80,1024]{3,2,1,0:T(8,128)(2,1)} collective-permute-done((bf16[2,4,80,1024]{3,2,1,0:T(8,128)(2,1)}, bf16[2,4,80,1024]{3,2,1,0:T(8,128)(2,1)}, u32[]{:S(2)}, u32[]{:S(2)}) %collective-permute-start.53) | collective-permute-done | bytes 1310752 | tf_op jit(solution)/shard_map/ppermute | solution.py:82
  496.6 18.4 %collective-permute-done.29 = bf16[2,4,32,2624]{3,2,1,0:T(8,128)(2,1)} collective-permute-done((bf16[2,4,32,2624]{3,2,1,0:T(8,128)(2,1)}, bf16[2,4,32,2624]{3,2,1,0:T(8,128)(2,1)}, u32[]{:S(2)}, u32[]{:S(2)}) %collective-permute-start.29) | collective-permute-done | bytes 1343520 | tf_op jit(solution)/shard_map/ppermute | solution.py:82
  520.1 6.0 %collective-permute-start.41 = (bf16[32,2560]{1,0:T(8,128)(2,1)S(1)}, bf16[32,2560]{1,0:T(8,128)(2,1)S(1)}, u32[]{:S(2)}, u32[]{:S(2)}) collective-permute-start(bf16[32,2560]{1,0:T(8,128)(2,1)S(1)} %get-tuple-element.81), channel_id=1, source_target_pairs={{0,12},{1,13},{2,14},{3,15},{4,0},{5,1},{6,2},{7,3},{8,4},{9,5},{1... | collective-permute-start | bytes 491528 | tf_op jit(solution)/shard_map/ppermute | solution.py:70
  545.1 9.6 %collective-permute-start.56 = (bf16[80,1024]{1,0:T(8,128)(2,1)S(1)}, bf16[80,1024]{1,0:T(8,128)(2,1)S(1)}, u32[]{:S(2)}, u32[]{:S(2)}) collective-permute-start(bf16[80,1024]{1,0:T(8,128)(2,1)S(1)} %get-tuple-element.76), channel_id=1, source_target_pairs={{0,8},{1,9},{2,10},{3,11},{4,12},{5,13},{6,14},{7,15},{8,0},{9,1},... | collective-permute-start | bytes 491528 | tf_op jit(solution)/shard_map/ppermute | solution.py:70
  559.3 9.9 %collective-permute-start.32 = (bf16[32,2624]{1,0:T(8,128)(2,1)S(1)}, bf16[32,2624]{1,0:T(8,128)(2,1)S(1)}, u32[]{:S(2)}, u32[]{:S(2)}) collective-permute-start(bf16[32,2624]{1,0:T(8,128)(2,1)S(1)} %get-tuple-element.71), channel_id=1, source_target_pairs={{0,8},{1,9},{2,10},{3,11},{4,12},{5,13},{6,14},{7,15},{8,0},{9,1},... | collective-permute-start | bytes 503816 | tf_op jit(solution)/shard_map/ppermute | solution.py:70
  (528 shorter events, 331.3 us)
Async XLA Ops:
  17.7 27.4 %collective-permute-start.16 = (bf16[32,2560]{1,0:T(8,128)(2,1)S(1)}, bf16[32,2560]{1,0:T(8,128)(2,1)S(1)}, u32[]{:S(2)}, u32[]{:S(2)}) collective-permute-start(bf16[32,2560]{1,0:T(8,128)(2,1)S(1)} %get-tuple-element.42), channel_id=1, source_target_pairs={{0,8},{1,9},{2,10},{3,11},{4,12},{5,13},{6,14},{7,15},{8,0},{9,1},... | collective-permute-start | bytes 491528 | tf_op jit(solution)/shard_map/ppermute | solution.py:70
  18.8 30.8 %collective-permute-start.17 = (bf16[32,2560]{1,0:T(8,128)(2,1)S(1)}, bf16[32,2560]{1,0:T(8,128)(2,1)S(1)}, u32[]{:S(2)}, u32[]{:S(2)}) collective-permute-start(bf16[32,2560]{1,0:T(8,128)(2,1)S(1)} %get-tuple-element.42), channel_id=1, source_target_pairs={{0,12},{1,13},{2,14},{3,15},{4,0},{5,1},{6,2},{7,3},{8,4},{9,5},{1... | collective-permute-start | bytes 491528 | tf_op jit(solution)/shard_map/ppermute | solution.py:70
  25.2 28.6 %collective-permute-start.22 = (bf16[80,1024]{1,0:T(8,128)(2,1)S(1)}, bf16[80,1024]{1,0:T(8,128)(2,1)S(1)}, u32[]{:S(2)}, u32[]{:S(2)}) collective-permute-start(bf16[80,1024]{1,0:T(8,128)(2,1)S(1)} %get-tuple-element.38), channel_id=1, source_target_pairs={{0,4},{1,5},{2,6},{3,7},{4,8},{5,9},{6,10},{7,11},{8,12},{9,13},{1... | collective-permute-start | bytes 491528 | tf_op jit(solution)/shard_map/ppermute | solution.py:70
  63.6 32.2 %collective-permute-start.25 = (bf16[4,80,1024]{2,1,0:T(8,128)(2,1)S(1)}, bf16[4,80,1024]{2,1,0:T(8,128)(2,1)S(1)}, u32[]{:S(2)}, u32[]{:S(2)}) collective-permute-start(bf16[4,80,1024]{2,1,0:T(8,128)(2,1)S(1)} %pad_maximum_fusion.15), channel_id=1, source_target_pairs={{0,2},{1,17},{2,0},{3,19},{4,6},{5,21},{6,4},{7,23},{8,10},{9,25},... | collective-permute-start | bytes 1966088 | tf_op jit(solution)/shard_map/ppermute | solution.py:82
  67.4 43.2 %collective-permute-start.4 = (bf16[4,32,2624]{2,1,0:T(8,128)(2,1)S(1)}, bf16[4,32,2624]{2,1,0:T(8,128)(2,1)S(1)}, u32[]{:S(2)}, u32[]{:S(2)}) collective-permute-start(bf16[4,32,2624]{2,1,0:T(8,128)(2,1)S(1)} %pad_maximum_fusion.11), channel_id=1, source_target_pairs={{0,2},{1,17},{2,0},{3,19},{4,6},{5,21},{6,4},{7,23},{8,10},{9,25},... | collective-permute-start | bytes 2015240 | tf_op jit(solution)/shard_map/ppermute | solution.py:82
  71.6 42.3 %collective-permute-start.12 = (bf16[8,32,2560]{2,1,0:T(8,128)(2,1)S(1)}, bf16[8,32,2560]{2,1,0:T(8,128)(2,1)S(1)}, u32[]{:S(2)}, u32[]{:S(2)}) collective-permute-start(bf16[8,32,2560]{2,1,0:T(8,128)(2,1)S(1)} %get-tuple-element.85), channel_id=1, source_target_pairs={{0,16},{1,3},{2,18},{3,1},{4,20},{5,7},{6,22},{7,5},{8,24},{9,11},... | collective-permute-start | bytes 3932168 | tf_op jit(solution)/shard_map/ppermute | solution.py:82
  82.7 35.7 %collective-permute-start.19 = (bf16[8,32,2560]{2,1,0:T(8,128)(2,1)S(1)}, bf16[8,32,2560]{2,1,0:T(8,128)(2,1)S(1)}, u32[]{:S(2)}, u32[]{:S(2)}) collective-permute-start(bf16[8,32,2560]{2,1,0:T(8,128)(2,1)S(1)} %get-tuple-element.87), channel_id=1, source_target_pairs={{0,16},{1,3},{2,18},{3,1},{4,20},{5,7},{6,22},{7,5},{8,24},{9,11},... | collective-permute-start | bytes 3932168 | tf_op jit(solution)/shard_map/ppermute | solution.py:82
  96.8 35.7 %collective-permute-start.26 = (bf16[8,80,1024]{2,1,0:T(8,128)(2,1)S(1)}, bf16[8,80,1024]{2,1,0:T(8,128)(2,1)S(1)}, u32[]{:S(2)}, u32[]{:S(2)}) collective-permute-start(bf16[8,80,1024]{2,1,0:T(8,128)(2,1)S(1)} %get-tuple-element.83), channel_id=1, source_target_pairs={{0,16},{1,3},{2,18},{3,1},{4,20},{5,7},{6,22},{7,5},{8,24},{9,11},... | collective-permute-start | bytes 3932168 | tf_op jit(solution)/shard_map/ppermute | solution.py:82
  111.5 35.7 %collective-permute-start.5 = (bf16[8,32,2624]{2,1,0:T(8,128)(2,1)S(1)}, bf16[8,32,2624]{2,1,0:T(8,128)(2,1)S(1)}, u32[]{:S(2)}, u32[]{:S(2)}) collective-permute-start(bf16[8,32,2624]{2,1,0:T(8,128)(2,1)S(1)} %get-tuple-element.72), channel_id=1, source_target_pairs={{0,16},{1,3},{2,18},{3,1},{4,20},{5,7},{6,22},{7,5},{8,24},{9,11},... | collective-permute-start | bytes 4030472 | tf_op jit(solution)/shard_map/ppermute | solution.py:82
  115.2 41.2 %collective-permute-start.13 = (bf16[16,32,2560]{2,1,0:T(8,128)(2,1)}, bf16[16,32,2560]{2,1,0:T(8,128)(2,1)}, u32[]{:S(2)}, u32[]{:S(2)}) collective-permute-start(bf16[16,32,2560]{2,1,0:T(8,128)(2,1)} %constant_dynamic-update-slice_fusion.16.own_ref), channel_id=1, source_target_pairs={{0,1},{1,0},{2,3},{3,2},{4,5},{5,4},{6,7},{7,6},{8,9},{9,8},{10,11... | collective-permute-start | bytes 7864328 | tf_op jit(solution)/shard_map/ppermute | solution.py:67
  119.5 42.7 %collective-permute-start.20 = (bf16[16,32,2560]{2,1,0:T(8,128)(2,1)}, bf16[16,32,2560]{2,1,0:T(8,128)(2,1)}, u32[]{:S(2)}, u32[]{:S(2)}) collective-permute-start(bf16[16,32,2560]{2,1,0:T(8,128)(2,1)} %constant_dynamic-update-slice_fusion.27.own_ref), channel_id=1, source_target_pairs={{0,1},{1,0},{2,3},{3,2},{4,5},{5,4},{6,7},{7,6},{8,9},{9,8},{10,11... | collective-permute-start | bytes 7864328 | tf_op jit(solution)/shard_map/ppermute | solution.py:67
  133.7 34.4 %collective-permute-start.27 = (bf16[16,80,1024]{2,1,0:T(8,128)(2,1)}, bf16[16,80,1024]{2,1,0:T(8,128)(2,1)}, u32[]{:S(2)}, u32[]{:S(2)}) collective-permute-start(bf16[16,80,1024]{2,1,0:T(8,128)(2,1)} %constant_dynamic-update-slice_fusion.38.own_ref), channel_id=1, source_target_pairs={{0,1},{1,0},{2,3},{3,2},{4,5},{5,4},{6,7},{7,6},{8,9},{9,8},{10,11... | collective-permute-start | bytes 7864328 | tf_op jit(solution)/shard_map/ppermute | solution.py:67
  148.4 32.1 %collective-permute-start.6 = (bf16[16,32,2624]{2,1,0:T(8,128)(2,1)}, bf16[16,32,2624]{2,1,0:T(8,128)(2,1)}, u32[]{:S(2)}, u32[]{:S(2)}) collective-permute-start(bf16[16,32,2624]{2,1,0:T(8,128)(2,1)} %constant_dynamic-update-slice_fusion.5.own_ref), channel_id=1, source_target_pairs={{0,1},{1,0},{2,3},{3,2},{4,5},{5,4},{6,7},{7,6},{8,9},{9,8},{10,11... | collective-permute-start | bytes 8060936 | tf_op jit(solution)/shard_map/ppermute | solution.py:67
  399.8 30.0 %collective-permute-start.36 = (bf16[4,4,32,2560]{3,2,0,1:T(8,128)(2,1)}, bf16[4,4,32,2560]{3,2,0,1:T(8,128)(2,1)}, u32[]{:S(2)}, u32[]{:S(2)}) collective-permute-start(bf16[4,4,32,2560]{3,2,0,1:T(8,128)(2,1)} %copy_bitcast_fusion.3), channel_id=1, source_target_pairs={{0,1},{1,0},{2,3},{3,2},{4,5},{5,4},{6,7},{7,6},{8,9},{9,8},{10,11... | collective-permute-start | bytes 7864328 | tf_op jit(solution)/shard_map/ppermute | solution.py:67
  403.4 31.2 %collective-permute-start.44 = (bf16[4,4,32,2560]{3,2,0,1:T(8,128)(2,1)}, bf16[4,4,32,2560]{3,2,0,1:T(8,128)(2,1)}, u32[]{:S(2)}, u32[]{:S(2)}) collective-permute-start(bf16[4,4,32,2560]{3,2,0,1:T(8,128)(2,1)} %copy_bitcast_fusion.2), channel_id=1, source_target_pairs={{0,1},{1,0},{2,3},{3,2},{4,5},{5,4},{6,7},{7,6},{8,9},{9,8},{10,11... | collective-permute-start | bytes 7864328 | tf_op jit(solution)/shard_map/ppermute | solution.py:67
  411.6 26.8 %collective-permute-start.52 = (bf16[4,4,80,1024]{3,2,0,1:T(8,128)(2,1)}, bf16[4,4,80,1024]{3,2,0,1:T(8,128)(2,1)}, u32[]{:S(2)}, u32[]{:S(2)}) collective-permute-start(bf16[4,4,80,1024]{3,2,0,1:T(8,128)(2,1)} %copy_bitcast_fusion.1), channel_id=1, source_target_pairs={{0,1},{1,0},{2,3},{3,2},{4,5},{5,4},{6,7},{7,6},{8,9},{9,8},{10,11... | collective-permute-start | bytes 7864328 | tf_op jit(solution)/shard_map/ppermute | solution.py:67
  437.8 34.3 %collective-permute-start.45 = (bf16[2,4,32,2560]{3,2,1,0:T(8,128)(2,1)}, bf16[2,4,32,2560]{3,2,1,0:T(8,128)(2,1)}, u32[]{:S(2)}, u32[]{:S(2)}) collective-permute-start(bf16[2,4,32,2560]{3,2,1,0:T(8,128)(2,1)} %pad_maximum_fusion.3), channel_id=1, source_target_pairs={{0,16},{1,3},{2,18},{3,1},{4,20},{5,7},{6,22},{7,5},{8,24},{9,11},... | collective-permute-start | bytes 3932168 | tf_op jit(solution)/shard_map/ppermute | solution.py:82
  441.8 51.4 %collective-permute-start.53 = (bf16[2,4,80,1024]{3,2,1,0:T(8,128)(2,1)}, bf16[2,4,80,1024]{3,2,1,0:T(8,128)(2,1)}, u32[]{:S(2)}, u32[]{:S(2)}) collective-permute-start(bf16[2,4,80,1024]{3,2,1,0:T(8,128)(2,1)} %pad_maximum_fusion.4), channel_id=1, source_target_pairs={{0,16},{1,3},{2,18},{3,1},{4,20},{5,7},{6,22},{7,5},{8,24},{9,11},... | collective-permute-start | bytes 3932168 | tf_op jit(solution)/shard_map/ppermute | solution.py:82
  446.4 68.5 %collective-permute-start.29 = (bf16[2,4,32,2624]{3,2,1,0:T(8,128)(2,1)}, bf16[2,4,32,2624]{3,2,1,0:T(8,128)(2,1)}, u32[]{:S(2)}, u32[]{:S(2)}) collective-permute-start(bf16[2,4,32,2624]{3,2,1,0:T(8,128)(2,1)} %pad_maximum_fusion.1), channel_id=1, source_target_pairs={{0,16},{1,3},{2,18},{3,1},{4,20},{5,7},{6,22},{7,5},{8,24},{9,11},... | collective-permute-start | bytes 4030472 | tf_op jit(solution)/shard_map/ppermute | solution.py:82
  454.6 63.5 %collective-permute-start.38 = (bf16[4,32,2560]{2,1,0:T(8,128)(2,1)S(1)}, bf16[4,32,2560]{2,1,0:T(8,128)(2,1)S(1)}, u32[]{:S(2)}, u32[]{:S(2)}) collective-permute-start(bf16[4,32,2560]{2,1,0:T(8,128)(2,1)S(1)} %fusion.73), channel_id=1, source_target_pairs={{0,2},{1,17},{2,0},{3,19},{4,6},{5,21},{6,4},{7,23},{8,10},{9,25},... | collective-permute-start | bytes 1966088 | tf_op jit(solution)/shard_map/ppermute | solution.py:82
  473.9 52.2 %collective-permute-start.46 = (bf16[4,32,2560]{2,1,0:T(8,128)(2,1)S(1)}, bf16[4,32,2560]{2,1,0:T(8,128)(2,1)S(1)}, u32[]{:S(2)}, u32[]{:S(2)}) collective-permute-start(bf16[4,32,2560]{2,1,0:T(8,128)(2,1)S(1)} %fusion.69), channel_id=1, source_target_pairs={{0,2},{1,17},{2,0},{3,19},{4,6},{5,21},{6,4},{7,23},{8,10},{9,25},... | collective-permute-start | bytes 1966088 | tf_op jit(solution)/shard_map/ppermute | solution.py:82
  495.0 33.6 %collective-permute-start.54 = (bf16[4,80,1024]{2,1,0:T(8,128)(2,1)S(1)}, bf16[4,80,1024]{2,1,0:T(8,128)(2,1)S(1)}, u32[]{:S(2)}, u32[]{:S(2)}) collective-permute-start(bf16[4,80,1024]{2,1,0:T(8,128)(2,1)S(1)} %fusion.65), channel_id=1, source_target_pairs={{0,2},{1,17},{2,0},{3,19},{4,6},{5,21},{6,4},{7,23},{8,10},{9,25},... | collective-permute-start | bytes 1966088 | tf_op jit(solution)/shard_map/ppermute | solution.py:82
  541.2 28.2 %collective-permute-start.57 = (bf16[80,1024]{1,0:T(8,128)(2,1)S(1)}, bf16[80,1024]{1,0:T(8,128)(2,1)S(1)}, u32[]{:S(2)}, u32[]{:S(2)}) collective-permute-start(bf16[80,1024]{1,0:T(8,128)(2,1)S(1)} %get-tuple-element.75), channel_id=1, source_target_pairs={{0,12},{1,13},{2,14},{3,15},{4,0},{5,1},{6,2},{7,3},{8,4},{9,5},{1... | collective-permute-start | bytes 491528 | tf_op jit(solution)/shard_map/ppermute | solution.py:70
  545.1 28.1 %collective-permute-start.56 = (bf16[80,1024]{1,0:T(8,128)(2,1)S(1)}, bf16[80,1024]{1,0:T(8,128)(2,1)S(1)}, u32[]{:S(2)}, u32[]{:S(2)}) collective-permute-start(bf16[80,1024]{1,0:T(8,128)(2,1)S(1)} %get-tuple-element.76), channel_id=1, source_target_pairs={{0,8},{1,9},{2,10},{3,11},{4,12},{5,13},{6,14},{7,15},{8,0},{9,1},... | collective-permute-start | bytes 491528 | tf_op jit(solution)/shard_map/ppermute | solution.py:70
  (142 other events, 1467.1 us)

commit v2 on v1

v2 whole, which is shorter than its diff:
```python
import functools
import math

import jax
import jax.numpy as jnp
from jax import lax
from jax.experimental import pallas as pl
from jax.experimental.pallas import tpu as pltpu
from jax.sharding import PartitionSpec as P

HEAD_SIZE = 64
GROUP = 3
ROPE_BASE = 10000.0
EPS = 1e-05
BF = jnp.bfloat16
F32 = jnp.float32
MIB = 1024 * 1024


def layout(doc_lengths, token_count):
    ends = jnp.cumsum(doc_lengths, axis=1)
    starts = ends - doc_lengths
    place = jnp.arange(token_count, dtype=jnp.int32)
    document = jnp.sum((place[None, :, None] >= ends[:, None, :]).astype(jnp.int32), axis=2)
    inside = place[None, :] < ends[:, -1:]
    segment = jnp.where(inside, document, -1)
    chosen = (
        document[:, :, None] == jnp.arange(doc_lengths.shape[1], dtype=jnp.int32)[None, None, :]
    )
    begin = jnp.sum(jnp.where(chosen, starts[:, None, :], 0), axis=2)
    positions = jnp.where(inside, place[None, :] - begin, 0)
    causal = place[:, None] >= place[None, :]
    same = (segment[:, :, None] == segment[:, None, :]) & (segment[:, :, None] >= 0)
    allowed = same & causal[None] | (place[:, None] == place[None, :])[None]
    return (positions, allowed)


def rotation(positions):
    half = HEAD_SIZE // 2
    frequency = jnp.exp(jnp.arange(half, dtype=F32) * (-2.0 * math.log(ROPE_BASE) / HEAD_SIZE))
    angle = positions.astype(F32)[None, :] * frequency[:, None]
    return (jnp.cos(angle), jnp.sin(angle))


class Place:
    def __init__(self, mesh):
        self.n, self.groups = mesh.shape["fsdp"], mesh.shape["dp"]
        self.nz = self.n // 4
        i = lax.axis_index("fsdp")
        self.c, self.y, self.z = i % 2, (i // 2) % 2, i // 4
        self.p = lax.axis_index("dp") % 2

    def swap_core(self, v):
        return lax.ppermute(v, "fsdp", [(i, i ^ 1) for i in range(self.n)])

    def shift_z(self, v, k):
        return lax.ppermute(v, "fsdp", [(i, (i + 4 * k) % self.n) for i in range(self.n)])

    def swap_x(self, v):
        return lax.ppermute(v, "dp", [(d, d ^ 1) for d in range(self.groups)])

    def cross(self, v, first):
        pairs = []
        for d in range(self.groups):
            for i in range(self.n):
                along_x = (i % 2 == 0) == first
                e, j = (d ^ 1, i) if along_x else (d, i ^ 2)
                pairs.append((d * self.n + i, e * self.n + j))
        return lax.ppermute(v, ("dp", "fsdp"), pairs)

    def piece_order(self):
        order = []
        for h in (self.c, 1 - self.c):
            for j in range(4 * self.nz):
                dz, slot = j % self.nz, j // self.nz
                lo, hi = slot % 2, slot // 2
                dy, dc = jnp.where(h == 0, lo, hi), jnp.where(h == 0, hi, lo)
                z = (self.z - dz + self.nz) % self.nz
                order.append((((z * 2 + (self.y ^ dy)) * 2 + (self.p ^ dc)) * 2 + h).astype(jnp.int32))
        return jnp.stack(order)

    def grad_order(self):
        order = []
        for b in range(2 * self.n):
            h, dc, dy, z = b % 2, (b // 2) % 2, (b // 4) % 2, b // 8
            keep_c, keep_y = (self.p == dc).astype(jnp.int32), (self.y == dy).astype(jnp.int32)
            hi, lo = (keep_c, keep_y) if h == 0 else (keep_y, keep_c)
            dz = (z - self.z + self.nz) % self.nz
            place = (2 * hi + lo) * self.nz + dz
            order.append(place + jnp.where(self.c == h, 0, 4 * self.nz))
        return jnp.stack(order).astype(jnp.int32)


def pick(v, k, axis=0):
    return lax.dynamic_index_in_dim(v, k, axis, keepdims=False)


class Order:
    def __init__(self):
        self.last = ()

    def do(self, step, *inputs):
        leaves, tree = jax.tree.flatten(inputs)
        if self.last:
            leaves = lax.optimization_barrier((*leaves, *self.last))[: len(leaves)]
        out = step(*jax.tree.unflatten(tree, leaves))
        self.last = (jax.tree.leaves(out)[0],)
        return out

    def tie(self, v):
        return lax.optimization_barrier((v, *self.last))[0] if self.last else v

    def got(self, *received):
        out = lax.optimization_barrier((*received, *self.last))[: len(received)]
        self.last = (out[0],)
        return out[0] if len(out) == 1 else out


def add(*terms):
    return functools.reduce(lambda a, b: a + b, [t.astype(F32) for t in terms])


class Gather:
    def __init__(self, at, order):
        self.at, self.order = at, order

    def start(self, make, *inputs):
        def step(*inputs):
            shard = make(*inputs)
            halves = shard.reshape(2, shard.shape[0] // 2, shard.shape[1])
            return pick(halves, self.at.c), pick(halves, 1 - self.at.c)

        self.keep, send = self.order.do(step, *inputs)
        self.moving = self.at.swap_core(send)

    def ready(self):
        at = self.at
        got = self.order.got(self.moving)
        self.mine = self.order.do(lambda k, g: jnp.where(at.p == at.c, k, g)[None], self.keep, got)

    def along_z(self):
        mine = self.order.tie(self.mine)
        self.moving = [self.at.shift_z(mine, k) for k in range(1, self.at.nz)]

    def come(self):
        parts = self.order.got(*self.moving)
        self.parts = parts if isinstance(parts, tuple) else (parts,)

    def line_up(self):
        self.line = self.order.do(lambda *v: jnp.concatenate(v), self.mine, *self.parts)

    def first(self):
        self.moving = self.at.cross(self.order.tie(self.line), False)

    def got_first(self):
        self.got = self.order.got(self.moving)

    def join(self):
        self.both = self.order.do(lambda *v: jnp.concatenate(v), self.line, self.got)

    def second(self):
        both = self.order.tie(self.both)
        self.moving = self.at.cross(both, True)
        self.other = self.at.swap_core(both)

    def got_second(self):
        self.third = self.order.got(self.moving)

    def cores(self):
        self.other_third = self.at.swap_core(self.order.tie(self.third))

    def pieces(self):
        other, other_third = self.order.got(self.other, self.other_third)
        return self.both, self.third, other, other_third


class Scatter:
    def __init__(self, at, order, own, send0, send1):
        self.at, self.order, self.own = at, order, own
        self.swaps = at.swap_core(order.tie(send0)), at.swap_core(order.tie(send1))

    def come(self):
        self.got = self.order.got(self.moving)

    def first(self):
        cut = 2 * self.at.nz
        other = self.order.got(self.swaps[0])
        sent = self.order.do(lambda a, b: add(a[:cut], b).astype(BF), self.own, other)
        self.moving = self.at.cross(sent, True)

    def rest(self):
        self.other = self.order.got(self.swaps[1])

    def second(self):
        nz = self.at.nz
        self.crossed = self.got
        sent = self.order.do(
            lambda a, b, c: add(a[2 * nz : 3 * nz], b[:nz], c[:nz]).astype(BF), self.own, self.other, self.crossed
        )
        self.moving = self.at.cross(sent, False)

    def along_z(self):
        nz = self.at.nz
        self.low = self.order.do(
            lambda a, b, c, d: add(a[3 * nz :], b[nz:], c[nz:], d).astype(BF), self.own, self.other, self.crossed, self.got
        )
        self.moving = [self.at.shift_z(self.low[k], k) for k in range(1, nz)]

    def come_z(self):
        parts = self.order.got(*self.moving)
        self.parts = parts if isinstance(parts, tuple) else (parts,)

    def along_x(self):
        total = self.order.do(lambda v, *w: add(v[0], *w).astype(BF), self.low, *self.parts)
        step = 2
        while step < self.at.groups:
            pairs = [(d, d ^ step) for d in range(self.at.groups)]
            total = add(total, lax.ppermute(total, "dp", pairs)).astype(BF)
            step *= 2
        self.total = total
        self.moving = self.at.swap_x(total)

    def cores(self):
        here = self.at.p == self.at.c
        self.keep, send = self.order.do(
            lambda a, b: (jnp.where(here, a, b), jnp.where(here, b, a)), self.total, self.got
        )
        self.moving = self.at.swap_core(send)

    def result(self):
        first = self.at.c == 0
        return self.order.do(
            lambda a, b: jnp.concatenate([jnp.where(first, a, b), jnp.where(first, b, a)]).astype(F32), self.keep, self.got
        )


VM = pl.BlockSpec(memory_space=pltpu.VMEM)
ANY = pl.BlockSpec(memory_space=pl.ANY)
SMEM = pl.BlockSpec(memory_space=pltpu.SMEM)


def nn(left, right):
    return jnp.dot(left, right, preferred_element_type=F32)


def nt(left, right):
    return lax.dot_general(left, right, (((1,), (1,)), ((), ())), preferred_element_type=F32)


def tn(left, right):
    return lax.dot_general(left, right, (((0,), (0,)), ((), ())), preferred_element_type=F32)


def tt(left, right):
    return lax.dot_general(left, right, (((0,), (1,)), ((), ())), preferred_element_type=F32)


def join(parts, axis):
    return jnp.concatenate(parts, axis=axis) if len(parts) > 1 else parts[0]


def call(body, ins, outs, scratch, flops, limit, specs=None, out_specs=None):
    return pl.pallas_call(
        body,
        in_specs=specs or [VM] * len(ins),
        out_specs=out_specs or [VM] * len(outs),
        out_shape=outs,
        scratch_shapes=scratch,
        compiler_params=pltpu.CompilerParams(vmem_limit_bytes=max(limit, 60) * MIB),
        cost_estimate=pl.CostEstimate(flops=1000, bytes_accessed=1000, transcendentals=0),
    )(*ins)


def fetches(order_ref, pieces, dests, sem, base):
    copies = []
    half = pieces[0].shape[1]
    at = 0
    for ref in pieces:
        for j in range(ref.shape[0]):
            row = pl.multiple_of(order_ref[at] * half, half)
            at += 1
            for dest, col in dests:
                whole = col == 0 and dest.shape[1] == ref.shape[2]
                src = ref.at[j] if whole else ref.at[j, :, pl.ds(col, dest.shape[1])]
                copies.append(
                    pltpu.make_async_copy(src, dest.at[pl.ds(row, half), :], sem.at[base + len(copies)])
                )
    return copies


class Copies:
    def __init__(self, sem):
        self.sem, self.used, self.open = sem, 0, []

    def start(self, source, dest):
        copy = pltpu.make_async_copy(source, dest, self.sem.at[self.used])
        self.used += 1
        copy.start()
        return copy

    def store(self, source, dest):
        self.open.append(self.start(source, dest))

    def blocks(self, order_ref, source, first, count, half, own, send0, send1):
        places, part = own.shape[0], send0.shape[0]
        for b in range(first, first + count):
            src = source.at[pl.ds(b * half, half), :]
            sem = self.sem.at[self.used]
            self.used += 1
            to = order_ref[b]

            @pl.when(to < places)
            def _(src=src, to=to, sem=sem):
                pltpu.make_async_copy(src, own.at[to], sem).start()

            @pl.when((to >= places) & (to < places + part))
            def _(src=src, to=to, sem=sem):
                pltpu.make_async_copy(src, send0.at[to - places], sem).start()

            @pl.when(to >= places + part)
            def _(src=src, to=to, sem=sem):
                pltpu.make_async_copy(src, send1.at[to - places - part], sem).start()

            self.open.append(pltpu.make_async_copy(src, own.at[0], sem))

    def close(self):
        wait(self.open)
        self.open = []


def start(copies):
    for copy in copies:
        copy.start()
    return copies


def wait(copies):
    for copy in copies:
        copy.wait()


def inverse_rms(v, width):
    return lax.rsqrt(jnp.sum(v * v, axis=1, keepdims=True) * (1.0 / width) + EPS)


def norm_back(values, gain, grad, width):
    scale = inverse_rms(values, width)
    unit = values * scale
    gain_grad = jnp.sum(grad * unit, axis=0, keepdims=True)
    inner = grad * gain
    mean = jnp.sum(inner * unit, axis=1, keepdims=True) * (1.0 / width)
    return gain_grad, scale * (inner - unit * mean)


class Sizes:
    def __init__(self, n, real, padded, ff, t, kv):
        self.n, self.real, self.padded, self.ff, self.t = n, real, padded, ff, t
        self.width, self.wide = n * real, n * padded
        self.hq, self.kvh = self.width // HEAD_SIZE, kv // HEAD_SIZE
        self.heads = self.hq + 2 * self.kvh
        self.feat = self.heads * HEAD_SIZE
        self.group = self.hq // self.kvh
        self.lse = -(-self.hq // 8) * 8
        self.block = 128 if t % 128 == 0 else t
        self.blocks = t // self.block
        self.tile = 512 if ff % 512 == 0 else ff


def head(ref, h):
    return ref[h * HEAD_SIZE : (h + 1) * HEAD_SIZE, :]


def by_block(sz, parts, op):
    b = sz.block
    return [
        functools.reduce(op, [parts[j][:, b * (i - j) : b * (i - j + 1)] for j in range(i + 1)])
        for i in range(sz.blocks)
    ]


def plus(a, b):
    return a + b


def attention_forward(sz, x, gain, wqkv_t, wo, cos, sin, bias, a1, heads, lse, mixp, mix):
    b, half = sz.block, HEAD_SIZE // 2
    a1[...] = (x * inverse_rms(x, sz.width) * gain).astype(BF)
    step = max(k for k in (5, 4, 3, 2, 1) if sz.heads % k == 0)
    for c in range(0, sz.heads, step):
        part = nt(wqkv_t[c * HEAD_SIZE : (c + step) * HEAD_SIZE, :], a1[...])
        for h in range(c, c + step):
            lo = (h - c) * HEAD_SIZE
            first, second = part[lo : lo + half], part[lo + half : lo + HEAD_SIZE]
            if h < sz.hq + sz.kvh:
                first, second = (
                    first * cos[...] - second * sin[...],
                    second * cos[...] + first * sin[...],
                )
            if h < sz.hq:
                first, second = first * HEAD_SIZE ** (-0.5), second * HEAD_SIZE ** (-0.5)
            heads[h * HEAD_SIZE : h * HEAD_SIZE + half, :] = first.astype(BF)
            heads[h * HEAD_SIZE + half : (h + 1) * HEAD_SIZE, :] = second.astype(BF)
    if sz.lse > sz.hq:
        lse[...] = jnp.zeros(lse.shape, F32)
    for g in range(sz.kvh):
        k = head(heads, sz.hq + g).T
        vt = head(heads, sz.hq + sz.kvh + g)
        for r in range(sz.group):
            h = g * sz.group + r
            q = head(heads, h)
            ss = [
                nn(k[b * j : b * (j + 1)], q[:, b * j :]) + bias[b * j : b * (j + 1), b * j :]
                for j in range(sz.blocks)
            ]
            top = by_block(sz, [jnp.max(s, axis=0, keepdims=True) for s in ss], jnp.maximum)
            sums, out = [], None
            for j in range(sz.blocks):
                e = jnp.exp(ss[j] - join(top[j:], 1))
                sums.append(jnp.sum(e, axis=0, keepdims=True))
                part = nn(vt[:, b * j : b * (j + 1)], e.astype(BF))
                if j:
                    part = jnp.concatenate([jnp.zeros((HEAD_SIZE, b * j), F32), part], axis=1)
                out = part if out is None else out + part
            summed = join(by_block(sz, sums, plus), 1)
            mix[h * HEAD_SIZE : (h + 1) * HEAD_SIZE, :] = out * (1.0 / summed)
            lse[h : h + 1, :] = join(top, 1) + jnp.log(summed)
    row = lax.broadcasted_iota(jnp.int32, (sz.padded, sz.t), 0)
    for j in range(sz.n):
        part = mix[sz.real * j : sz.real * j + sz.padded, :]
        mixp[sz.padded * j : sz.padded * (j + 1), :] = jnp.where(row < sz.real, part, 0.0).astype(BF)
    return x + tn(mixp[...], wo[...])


def attention_backward(sz, gh, gl, x, gain, wqkv_t, wo, cos, sin, bias, heads, lse, gm, g_heads, gs_ref, p_ref, g_qkv, ready=None):
    b, half = sz.block, HEAD_SIZE // 2
    for j in range(sz.n):
        part = nt(wo[sz.padded * j : sz.padded * (j + 1), :], gl) if sz.n < 4 else None
        if part is not None:
            gm[sz.real * j : sz.real * j + sz.padded, :] = part
    if sz.n >= 4:
        quarter = sz.n // 4
        for c in range(4):
            part = nt(wo[sz.padded * quarter * c : sz.padded * quarter * (c + 1), :], gl)
            for j in range(quarter):
                at = sz.real * (quarter * c + j)
                gm[at : at + sz.padded, :] = part[sz.padded * j : sz.padded * (j + 1)]
    if ready is not None:
        ready(False)
    for g in range(sz.kvh):
        kt = head(heads, sz.hq + g)
        k = kt.T
        v = head(heads, sz.hq + sz.kvh + g).T
        gk = gv = None
        for r in range(sz.group):
            h = g * sz.group + r
            q, gmh = head(heads, h), head(gm, h).astype(BF)
            row = lse[h : h + 1, :]
            ps, gps, down = [], [], []
            for j in range(sz.blocks):
                lo = b * j
                s = nn(k[lo : lo + b], q[:, lo:]) + bias[lo : lo + b, lo:]
                p = jnp.exp(s - row[:, lo:])
                gp = nn(v[lo : lo + b], gmh[:, lo:])
                ps.append(p)
                gps.append(gp)
                down.append(jnp.sum(p * gp, axis=0, keepdims=True))
            d = by_block(sz, down, plus)
            for j in range(sz.blocks):
                lo = b * j
                gs_ref[r, lo : lo + b, lo:] = (ps[j] * (gps[j] - join(d[j:], 1))).astype(BF)
                p_ref[r, lo : lo + b, lo:] = ps[j].astype(BF)
            gq = join(
                [
                    nn(kt[:, : b * (i + 1)], gs_ref[r, : b * (i + 1), b * i : b * (i + 1)])
                    for i in range(sz.blocks)
                ],
                1,
            )
            part_k = join([nt(q[:, b * j :], gs_ref[r, b * j : b * (j + 1), b * j :]) for j in range(sz.blocks)], 1)
            part_v = join([nt(gmh[:, b * j :], p_ref[r, b * j : b * (j + 1), b * j :]) for j in range(sz.blocks)], 1)
            g_heads[h * HEAD_SIZE : (h + 1) * HEAD_SIZE, :] = gq * HEAD_SIZE ** (-0.5)
            gk = part_k if gk is None else gk + part_k
            gv = part_v if gv is None else gv + part_v
        at = (sz.hq + g) * HEAD_SIZE
        g_heads[at : at + HEAD_SIZE, :] = gk
        at = (sz.hq + sz.kvh + g) * HEAD_SIZE
        g_qkv[at : at + HEAD_SIZE, :] = gv.astype(BF)
    for h in range(sz.hq + sz.kvh):
        at = h * HEAD_SIZE
        first, second = g_heads[at : at + half, :], g_heads[at + half : at + HEAD_SIZE, :]
        g_qkv[at : at + half, :] = (first * cos[...] + second * sin[...]).astype(BF)
        g_qkv[at + half : at + HEAD_SIZE, :] = (second * cos[...] - first * sin[...]).astype(BF)
    if ready is not None:
        ready(True)
    gain_grad, back = norm_back(x[...], gain, tn(g_qkv[...], wqkv_t[...]), sz.width)
    return gain_grad, gh[...] + back


def ffn_up(sz, hidden, gain, a2, wg, wu, gate, up, inner):
    a2[...] = (hidden * inverse_rms(hidden, sz.width) * gain).astype(BF)
    for c in range(0, sz.ff, sz.tile):
        cols = slice(c, c + sz.tile)
        gate_part = nn(a2[...], wg[:, cols])
        up_part = nn(a2[...], wu[:, cols])
        gate[:, cols] = gate_part.astype(BF)
        up[:, cols] = up_part.astype(BF)
        inner[:, cols] = (gate_part * jax.nn.sigmoid(gate_part) * up_part).astype(BF)


def ffn_backward(sz, grad, cl, hidden, gain, wg, wu, wd, gate, up, gg, gu, ready=None):
    for i, c in enumerate(range(0, sz.ff, sz.tile)):
        cols = slice(c, c + sz.tile)
        if ready is not None:
            ready(i)
        g_inner = nt(cl[...], wd[cols, :])
        z = gate[:, cols].astype(F32)
        sg = jax.nn.sigmoid(z)
        silu = z * sg
        gg[:, cols] = (g_inner * up[:, cols].astype(F32) * (sg + silu * (1.0 - sg))).astype(BF)
        gu[:, cols] = (g_inner * silu).astype(BF)
    if ready is not None:
        ready(-1)
    g_a2 = nt(gg[...], wg[...]) + nt(gu[...], wu[...])
    gain_grad, back = norm_back(hidden[...], gain, g_a2, sz.width)
    return gain_grad, grad + back


def shape(*dims, dtype=BF):
    return jax.ShapeDtypeStruct(dims, dtype)


def halves(sz, half, cols):
    return [shape(sz.n, half, cols)] + [shape(sz.n // 2, half, cols)] * 2


def first_attention(sz, order, pieces, x, cot, rope, bias):
    t, wide = sz.t, sz.wide

    def body(order_ref, p0, p1, p2, p3, x_hbm, cot_hbm, cos, sin, bias_hbm,
             hidden_hbm, a1_hbm, heads_hbm, lse, mixp_hbm, wqkv_t_hbm, wo_hbm, gains, x_out, cot_out,
             x, cot, hidden, a1, heads, mixp, wqkv_t, wo, wqkv, mix, bias_ref, sem, out_sem):
        io = Copies(out_sem)
        wait(start(fetches(order_ref, (p0, p1, p2, p3), [(wqkv, sz.wide)], sem, 0)))
        loads = [io.start(x_hbm, x), io.start(bias_hbm, bias_ref), io.start(cot_hbm, cot)]
        loads += start(fetches(order_ref, (p0, p1, p2, p3), [(wo, 0)], sem, 2 * sz.n))
        rows = []
        for k in range(2):
            parts = []
            for j in range(sz.n):
                lo = sz.padded * (j + 1) - 16
                tile = wqkv[lo : lo + 16, 0:128].astype(F32)
                at = sz.real + k - (sz.padded - 16)
                parts.append(tile[at : at + 1, : sz.padded])
            rows.append(jnp.concatenate(parts, axis=1))
        gains[...] = jnp.concatenate(rows + [jnp.zeros((6, sz.wide), F32)], axis=0)
        wqkv_t[...] = wqkv[...].T
        wait(loads)
        for a, b in ((wqkv_t, wqkv_t_hbm), (wo, wo_hbm), (x, x_out), (cot, cot_out)):
            io.store(a, b)
        hidden[...] = x[...].astype(F32)
        hidden[...] = attention_forward(
            sz, hidden[...], gains[0:1, :], wqkv_t, wo, cos, sin, bias_ref, a1, heads, lse, mixp, mix
        )
        for a, b in ((hidden, hidden_hbm), (a1, a1_hbm), (heads, heads_hbm), (mixp, mixp_hbm)):
            io.store(a, b)
        io.close()

    v = pltpu.VMEM
    return call(
        body,
        [order, *pieces, x, cot, *rope, bias],
        [
            shape(t, wide, dtype=F32), shape(t, wide), shape(sz.feat, t), shape(sz.lse, t, dtype=F32),
            shape(wide, t), shape(sz.feat, wide), shape(wide, wide), shape(8, wide, dtype=F32),
            shape(t, wide), shape(t, wide),
        ],
        [
            v((t, wide), BF), v((t, wide), BF),
            v((t, wide), F32), v((t, wide), BF), v((sz.feat, t), BF), v((wide, t), BF), v((sz.feat, wide), BF),
            v((wide, wide), BF), v((wide, sz.feat), BF), v((sz.width + 16, t), F32), v((t, t), F32),
            pltpu.SemaphoreType.DMA((4 * sz.n,)), pltpu.SemaphoreType.DMA((12,)),
        ],
        6 * t * wide * sz.feat, 40,
        specs=[SMEM] + [ANY] * 6 + [VM] * 2 + [ANY],
        out_specs=[ANY] * 3 + [VM] + [ANY] * 3 + [VM] + [ANY] * 2,
    )


def first_gate(sz, order, pieces, hidden, gains):
    t, wide, ff = sz.t, sz.wide, sz.ff

    def body(order_ref, p0, p1, p2, p3, hidden_hbm, gains_ref, a2_hbm, gate_hbm, w_hbm, hidden_ref, a2, gate, w, sem, out_sem):
        out = Copies(out_sem)
        load = out.start(hidden_hbm, hidden_ref)
        wait([load])
        copies = start(fetches(order_ref, (p0, p1, p2, p3), [(w, 0)], sem, 0))
        hidden = hidden_ref[...]
        a2[...] = (hidden * inverse_rms(hidden, sz.width) * gains_ref[1:2, :]).astype(BF)
        wait(copies)
        out.store(w, w_hbm)
        out.store(a2, a2_hbm)
        for c in range(0, ff, sz.tile):
            cols = slice(c, c + sz.tile)
            gate[:, cols] = nn(a2[...], w[:, cols]).astype(BF)
        out.store(gate, gate_hbm)
        out.close()

    return call(
        body,
        [order, *pieces, hidden, gains],
        [shape(t, wide), shape(t, ff), shape(wide, ff)],
        [pltpu.VMEM((t, wide), F32), pltpu.VMEM((t, wide), BF), pltpu.VMEM((t, ff), BF), pltpu.VMEM((wide, ff), BF),
         pltpu.SemaphoreType.DMA((2 * sz.n,)), pltpu.SemaphoreType.DMA((4,))],
        2 * t * wide * ff, 40,
        specs=[SMEM] + [ANY] * 5 + [VM], out_specs=[ANY] * 3,
    )


def first_up(sz, order, pieces, a2, gate):
    t, wide, ff = sz.t, sz.wide, sz.ff

    def body(order_ref, p0, p1, p2, p3, a2_hbm, gate_hbm, up_hbm, inner_hbm, w_hbm, a2, gate, up, inner, w, sem, out_sem):
        copies = start(fetches(order_ref, (p0, p1, p2, p3), [(w, 0)], sem, 0))
        out = Copies(out_sem)
        copies += [out.start(a2_hbm, a2), out.start(gate_hbm, gate)]
        wait(copies)
        out.store(w, w_hbm)
        for c in range(0, ff, sz.tile):
            cols = slice(c, c + sz.tile)
            part = nn(a2[...], w[:, cols])
            up[:, cols] = part.astype(BF)
            z = gate[:, cols].astype(F32)
            inner[:, cols] = (z * jax.nn.sigmoid(z) * part).astype(BF)
        out.store(inner, inner_hbm)
        out.store(up, up_hbm)
        out.close()

    return call(
        body,
        [order, *pieces, a2, gate],
        [shape(t, ff), shape(t, ff), shape(wide, ff)],
        [pltpu.VMEM((t, wide), BF)] + [pltpu.VMEM((t, ff), BF)] * 3 + [pltpu.VMEM((wide, ff), BF),
         pltpu.SemaphoreType.DMA((2 * sz.n,)), pltpu.SemaphoreType.DMA((5,))],
        2 * t * wide * ff, 40,
        specs=[SMEM] + [ANY] * 6, out_specs=[ANY] * 3,
    )


def middle(sz, order, back, down_pieces, hidden1, inner1, wqkv_t, wo, wg, wu, gains, rope, bias, out_grad, half):
    aligned = isinstance(down_pieces, tuple)
    downs = list(down_pieces) if aligned else [down_pieces]
    t, wide, ff = sz.t, sz.wide, sz.ff

    def body(*refs):
        order_ref, back_ref, refs = refs[0], refs[1], refs[2:]
        down_refs, refs = refs[: len(downs)], refs[len(downs) :]
        (hidden1_hbm, inner1_hbm, wqkv_hbm, wo_hbm, wg_hbm, wu_hbm, gains_ref, cos, sin, bias_hbm, cl_hbm,
         second_hbm, carried_hbm, wd_hbm, a1_hbm, mixp_hbm, a2_hbm, gg_hbm, gu_hbm, gl_hbm, g_qkv_hbm, gain_grads,
         own, send0, send1,
         wd, wqkv_t, wo, wg, wu, inners, cls, x2, hidden, a1, heads, lse, mixp, a2, gate, up, gg, gu, gl, g_qkv,
         bias_ref, mix, g_heads, gs, probs, sem, piece_sem) = refs
        io = Copies(sem)
        if aligned:
            first = start(fetches(order_ref, down_refs, [(wd, 0)], piece_sem, 0))
        else:
            first = [io.start(down_refs[0], wd)]
        run1, run2 = pl.ds(0, t), pl.ds(t, t)
        first += [io.start(inner1_hbm, inners.at[run1, :]), io.start(hidden1_hbm, x2)]
        wait(first)
        loads = [io.start(wqkv_hbm, wqkv_t), io.start(bias_hbm, bias_ref), io.start(wo_hbm, wo)]
        inner1, inner2 = inners.at[run1, :], inners.at[run2, :]
        cl1, cl2 = cls.at[run1, :], cls.at[run2, :]
        x2[...] = x2[...] + nn(inner1[...], wd[...])
        wait(loads)
        sides = [io.start(wg_hbm, wg), io.start(wu_hbm, wu), io.start(cl_hbm, cls.at[run2, :])]
        hidden[...] = attention_forward(
            sz, x2[...], gains_ref[0:1, :], wqkv_t, wo, cos, sin, bias_ref, a1, heads, lse, mixp, mix
        )
        wait(sides)
        keep = io.start(wd, wd_hbm)
        io.store(a1, a1_hbm)
        io.store(mixp, mixp_hbm)
        ffn_up(sz, hidden[...], gains_ref[1:2, :], a2, wg, wu, gate, up, inner2)
        io.store(a2, a2_hbm)
        gl[...] = (hidden[...] + nn(inner2[...], wd[...])).astype(BF)
        out = io.start(gl, second_hbm)
        gain_f, gh = ffn_backward(
            sz, cl2[...].astype(F32), cl2, hidden[...], gains_ref[1:2, :], wg, wu, wd, gate, up, gg, gu
        )
        io.store(gg, gg_hbm)
        io.store(gu, gu_hbm)
        hidden[...] = gh
        wait([out])
        gl[...] = gh.astype(BF)
        io.store(gl, gl_hbm)
        gain_a, g_x = attention_backward(
            sz, hidden, gl[...], x2, gains_ref[0:1, :], wqkv_t, wo, cos, sin, bias_ref, heads, lse,
            mix, g_heads, gs, probs, g_qkv
        )
        io.store(g_qkv, g_qkv_hbm)
        hidden[...] = g_x
        io.store(hidden, carried_hbm)
        cl1[...] = g_x.astype(BF)
        gain_grads[...] = jnp.concatenate([gain_a, gain_f, jnp.zeros((6, wide), F32)], axis=0)
        wait([keep])
        tile = 640 if ff % 640 == 0 and 640 % half == 0 else ff
        for lo in range(0, ff, tile):
            wd[lo : lo + tile, :] = tn(inners[:, lo : lo + tile], cls[...]).astype(BF)
            if aligned:
                io.blocks(back_ref, wd, lo // half, tile // half, half, own, send0, send1)
        if not aligned:
            io.store(wd, own)
        io.close()

    ins = [order, back, *downs, hidden1, inner1, wqkv_t, wo, wg, wu, gains, *rope, bias, out_grad]
    specs = [SMEM] * 2 + [ANY] * len(downs) + [ANY] * 6 + [VM] * 3 + [ANY] * 2
    places = halves(sz, half, wide) if aligned else [shape(ff, wide), shape(8, 128), shape(8, 128)]
    outs = [
        shape(t, wide), shape(t, wide, dtype=F32), shape(ff, wide), shape(t, wide), shape(wide, t), shape(t, wide),
        shape(t, ff), shape(t, ff), shape(t, wide), shape(sz.feat, t), shape(8, wide, dtype=F32), *places,
    ]
    out_specs = [ANY] * 10 + [VM] + [ANY] * 3
    scratch = [
        pltpu.VMEM((ff, wide), BF), pltpu.VMEM((sz.feat, wide), BF), pltpu.VMEM((wide, wide), BF),
        pltpu.VMEM((wide, ff), BF), pltpu.VMEM((wide, ff), BF), pltpu.VMEM((2 * t, ff), BF), pltpu.VMEM((2 * t, wide), BF),
        pltpu.VMEM((t, wide), F32), pltpu.VMEM((t, wide), F32), pltpu.VMEM((t, wide), BF), pltpu.VMEM((sz.feat, t), BF),
        pltpu.VMEM((sz.lse, t), F32), pltpu.VMEM((wide, t), BF), pltpu.VMEM((t, wide), BF), pltpu.VMEM((t, ff), BF),
        pltpu.VMEM((t, ff), BF), pltpu.VMEM((t, ff), BF), pltpu.VMEM((t, ff), BF), pltpu.VMEM((t, wide), BF),
        pltpu.VMEM((sz.feat, t), BF), pltpu.VMEM((t, t), F32), pltpu.VMEM((sz.width + 16, t), F32),
        pltpu.VMEM((sz.feat, t), F32), pltpu.VMEM((sz.group, t, t), BF), pltpu.VMEM((sz.group, t, t), BF),
        pltpu.SemaphoreType.DMA((2 * sz.n + 24,)), pltpu.SemaphoreType.DMA((2 * sz.n,)),
    ]
    return call(body, ins, outs, scratch, 24 * t * wide * ff, 60, specs, out_specs)


def last_ffn(sz, back, grad, hidden, gains, wg, wu, wd, gate, up, a2s, gg2, half):
    t, wide, ff = sz.t, sz.wide, sz.ff

    def body(back_ref, grad_hbm, hidden_hbm, gains_ref, wg_hbm, wu_hbm, wd_hbm, gate_hbm, up_hbm, a2_1, a2_2, gg2_hbm,
             gh_hbm, gl_hbm, gu_hbm, gain_grad, own, send0, send1,
             grad_ref, hidden, cl, wg, wu, wd, gate, up, ggs, gu, gl, a2, sem):
        io = Copies(sem)
        count = ff // sz.tile
        run1, run2 = pl.ds(0, t), pl.ds(t, t)

        def step(i):
            part = pl.ds(i * sz.tile, sz.tile)
            return [
                io.start(wd_hbm.at[part, :], wd.at[part, :]), io.start(gate_hbm.at[:, part], gate.at[:, part]),
                io.start(up_hbm.at[:, part], up.at[:, part]),
            ]

        load = [io.start(grad_hbm, grad_ref)] + step(0)
        wait(load)
        steps, sides, rest = {}, [], []
        for i in range(1, count):
            steps[i] = step(i)
        cl[...] = grad_ref[...].astype(BF)

        def ready(i):
            if i > 0:
                wait(steps[i])
            if i == min(1, count - 1):
                sides.extend([io.start(wg_hbm, wg), io.start(wu_hbm, wu), io.start(hidden_hbm, hidden)])
            if i < 0:
                wait(sides)
                io.store(gu, gu_hbm)
                rest.extend([
                    io.start(a2_1, a2.at[run1, :]), io.start(a2_2, a2.at[run2, :]), io.start(gg2_hbm, ggs.at[run2, :])
                ])

        gain_f, gh = ffn_backward(
            sz, grad_ref[...], cl, hidden, gains_ref[1:2, :], wg, wu, wd, gate, up, ggs.at[run1, :], gu, ready
        )
        hidden[...] = gh
        gl[...] = gh.astype(BF)
        io.store(hidden, gh_hbm)
        io.store(gl, gl_hbm)
        gain_grad[...] = jnp.concatenate([gain_f, jnp.zeros((7, wide), F32)], axis=0)
        wait(rest)
        tile = 256 if wide % 256 == 0 else wide
        for lo in range(0, wide, tile):
            wg[lo : lo + tile, :] = tn(a2[:, lo : lo + tile], ggs[...]).astype(BF)
            io.blocks(back_ref, wg, lo // half, tile // half, half, own, send0, send1)
        io.close()

    v = pltpu.VMEM
    return call(
        body,
        [back, grad, hidden, gains, wg, wu, wd, gate, up, *a2s, gg2],
        [shape(t, wide, dtype=F32), shape(t, wide), shape(t, ff), shape(8, wide, dtype=F32), *halves(sz, half, ff)],
        [
            v((t, wide), F32), v((t, wide), F32), v((t, wide), BF), v((wide, ff), BF), v((wide, ff), BF), v((ff, wide), BF),
            v((t, ff), BF), v((t, ff), BF), v((2 * t, ff), BF), v((t, ff), BF), v((t, wide), BF), v((2 * t, wide), BF),
            pltpu.SemaphoreType.DMA((3 * (ff // sz.tile) + 2 * sz.n + 16,)),
        ],
        10 * t * wide * ff, 56,
        specs=[SMEM] + [ANY] * 2 + [VM] + [ANY] * 8, out_specs=[ANY] * 3 + [VM] + [ANY] * 3,
    )


def settle(*arrays):
    def body(*refs):
        for a, b in zip(refs[: len(arrays)], refs[len(arrays) :]):
            b[...] = a[...]

    return call(body, list(arrays), [shape(*a.shape, dtype=a.dtype) for a in arrays], [], 0, 20)


def last_attention(sz, back, gh, gl, x, gains, wqkv_t, wo, rope, bias, heads, lse, a2s, gus, mixps, gl2, half):
    t, wide, ff = sz.t, sz.wide, sz.ff
    cols = ff + wide

    def body(back_ref, gh_hbm, gl_hbm, x_hbm, gains_ref, wqkv_hbm, wo_hbm, cos, sin, bias_hbm, heads_hbm, lse_ref,
             a2_1, a2_2, gu_1, gu_2, m1, m2, gl_2,
             g_x_hbm, g_qkv_hbm, gain_grad, own, send0, send1,
             gh, gls, x_low, x, wqkv_t, wo, bias_ref, heads, g_qkv, mix, g_heads, gs, probs, a2, gu, mixp, out, sem):
        io = Copies(sem)
        run1, run2 = pl.ds(0, t), pl.ds(t, t)
        gl = gls.at[run1, :]
        first = [
            io.start(m1, mixp.at[:, run1]), io.start(m2, mixp.at[:, run2]),
            io.start(gl_hbm, gl), io.start(gl_2, gls.at[run2, :]),
        ]
        wait(first)
        second = [
            io.start(a2_1, a2.at[run1, :]), io.start(a2_2, a2.at[run2, :]),
            io.start(gu_1, gu.at[run1, :]), io.start(gu_2, gu.at[run2, :]),
        ]
        tile = 256 if wide % 256 == 0 else wide
        for lo in range(0, wide, tile):
            out[lo : lo + tile, ff:cols] = nn(mixp[lo : lo + tile, :], gls[...]).astype(BF)
        wait(second)
        third = [
            io.start(wo_hbm, wo), io.start(heads_hbm, heads), io.start(bias_hbm, bias_ref),
            io.start(wqkv_hbm, wqkv_t), io.start(gh_hbm, gh), io.start(x_hbm, x_low),
        ]
        for lo in range(0, wide, tile):
            out[lo : lo + tile, 0:ff] = tn(a2[:, lo : lo + tile], gu[...]).astype(BF)
            io.blocks(back_ref, out, lo // half, tile // half, half, own, send0, send1)
        wait(third)
        x[...] = x_low[...].astype(F32)
        gain_a, back_x = attention_backward(
            sz, gh, gl[...], x, gains_ref[0:1, :], wqkv_t, wo, cos, sin, bias_ref,
            heads, lse_ref, mix, g_heads, gs, probs, g_qkv
        )
        io.store(g_qkv, g_qkv_hbm)
        gl[...] = back_x.astype(BF)
        io.store(gl, g_x_hbm)
        gain_grad[...] = jnp.concatenate([gain_a, jnp.zeros((7, wide), F32)], axis=0)
        io.close()

    v = pltpu.VMEM
    return call(
        body,
        [back, gh, gl, x, gains, wqkv_t, wo, *rope, bias, heads, lse, *a2s, *gus, *mixps, gl2],
        [shape(t, wide), shape(sz.feat, t), shape(8, wide, dtype=F32), *halves(sz, half, cols)],
        [
            v((t, wide), F32), v((2 * t, wide), BF), v((t, wide), BF), v((t, wide), F32), v((sz.feat, wide), BF),
            v((wide, wide), BF), v((t, t), F32), v((sz.feat, t), BF), v((sz.feat, t), BF), v((sz.width + 16, t), F32),
            v((sz.feat, t), F32), v((sz.group, t, t), BF), v((sz.group, t, t), BF),
            v((2 * t, wide), BF), v((2 * t, ff), BF), v((wide, 2 * t), BF), v((wide, cols), BF),
            pltpu.SemaphoreType.DMA((2 * sz.n + 32,)),
        ],
        10 * t * wide * sz.feat, 56,
        specs=[SMEM] + [ANY] * 3 + [VM] + [ANY] * 2 + [VM] * 2 + [ANY] * 2 + [VM] + [ANY] * 7,
        out_specs=[ANY] * 2 + [VM] + [ANY] * 3,
    )


def qkv_grad(sz, back, a1s, g_qkv_runs, gain2, gain_f1, gain_a1, half):
    t, wide, cols = sz.t, sz.wide, sz.feat

    def body(back_ref, a_1, a_2, g1, g2, gain2_ref, gain_f_ref, gain_a_ref, own, send0, send1, a1, g_qkv, out, sem):
        io = Copies(sem)
        run1, run2 = pl.ds(0, t), pl.ds(t, t)
        wait([
            io.start(a_1, a1.at[run1, :]), io.start(a_2, a1.at[run2, :]),
            io.start(g1, g_qkv.at[:, run1]), io.start(g2, g_qkv.at[:, run2]),
        ])
        tile = 256 if wide % 256 == 0 else wide
        row = lax.broadcasted_iota(jnp.int32, (sz.padded, sz.padded), 0)
        for lo in range(0, wide, tile):
            into = tt(a1[:, lo : lo + tile], g_qkv[...])
            patches = []
            for s in range(lo, lo + tile, sz.padded):
                here = slice(s, s + sz.padded)
                attn_gain = gain_a_ref[0:1, here] + gain2_ref[0:1, here]
                ffn_gain = gain_f_ref[0:1, here] + gain2_ref[1:2, here]
                patches.append(
                    jnp.where(row == sz.real, attn_gain, jnp.where(row == sz.real + 1, ffn_gain, 0.0))
                )
            patch = jnp.concatenate([join(patches, 0), jnp.zeros((tile, 128 - sz.padded), F32)], axis=1)
            out[lo : lo + tile, 0:128] = (into[:, :128] + patch).astype(BF)
            out[lo : lo + tile, 128:cols] = into[:, 128:].astype(BF)
            io.blocks(back_ref, out, lo // half, tile // half, half, own, send0, send1)
        io.close()

    v = pltpu.VMEM
    return call(
        body,
        [back, *a1s, *g_qkv_runs, gain2, gain_f1, gain_a1],
        halves(sz, half, cols),
        [v((2 * t, wide), BF), v((cols, 2 * t), BF), v((wide, cols), BF), pltpu.SemaphoreType.DMA((2 * sz.n + 8,))],
        4 * t * wide * cols, 40,
        specs=[SMEM] + [ANY] * 4 + [VM] * 3, out_specs=[ANY] * 3,
    )


def spread(v, n, real, padded):
    lead = v.shape[:-1]
    v = v.reshape(lead + (n, real))
    v = jnp.pad(v, [(0, 0)] * len(lead) + [(0, 0), (0, padded - real)])
    return v.reshape(lead + (n * padded,))


def narrow(v, n, real, padded):
    lead = v.shape[:-1]
    return v.reshape(lead + (n, padded))[..., :real].reshape(lead + (n * real,))


def place_blocks(order, pieces):
    both = jnp.concatenate(pieces)
    spots = jnp.zeros(order.shape, jnp.int32).at[order].set(jnp.arange(order.shape[0], dtype=jnp.int32))
    return jnp.take(both, spots, axis=0).reshape(-1, both.shape[2])


def order_blocks(order, grad, half):
    spots = jnp.zeros(order.shape, jnp.int32).at[order].set(jnp.arange(order.shape[0], dtype=jnp.int32))
    both = jnp.take(grad.reshape(-1, half, grad.shape[1]), spots, axis=0)
    cut = order.shape[0] // 4
    return both[: 2 * cut], both[2 * cut : 3 * cut], both[3 * cut :]


def shards(mesh, tokens, lengths, w_query, key_weight, value_weight, output_weight, w_gate, w_up, w_down, gain_attn, gain_ffn, out_grad):
    at = Place(mesh)
    n = at.n
    real, width = w_query.shape
    padded = -(-(real + 2) // 16) * 16
    sz = Sizes(n, real, padded, w_gate.shape[1], tokens.shape[0], key_weight.shape[1])
    wide, ff = sz.wide, sz.ff
    half, down_half = padded // 2, w_down.shape[0] // 2
    aligned = down_half % 16 == 0
    order = Order()
    places, back = at.piece_order(), at.grad_order()

    def pad_rows(v):
        return jnp.pad(v, ((0, padded - v.shape[0]), (0, 0)))

    def attention_shard(w_query, key_weight, value_weight, output_weight, gain_attn, gain_ffn):
        qkv = jnp.concatenate([w_query, key_weight, value_weight], axis=1)
        gains = jnp.pad(jnp.stack([gain_attn, gain_ffn]), ((0, 0), (0, qkv.shape[1] - real)))
        qkv = pad_rows(jnp.concatenate([qkv, gains]))
        return jnp.concatenate([pad_rows(spread(output_weight, n, real, padded)), qkv], axis=1)

    def tables(lengths, tokens, out_grad):
        positions, allowed = layout(lengths, tokens.shape[0])
        bias = jnp.where(allowed[0], 0.0, -1e30).astype(F32).T
        return rotation(positions[0]), bias, spread(tokens, n, real, padded), spread(out_grad, n, real, padded)

    ga, gg, gu, gd = (Gather(at, order) for _ in range(4))
    ga.start(attention_shard, w_query, key_weight, value_weight, output_weight, gain_attn, gain_ffn)
    ga.ready()
    ga.along_z()
    gg.start(pad_rows, w_gate)
    gu.start(pad_rows, w_up)
    gd.start(lambda v: spread(v, n, real, padded), w_down)
    gu.ready()
    gd.ready()
    rope, bias, x1, cot = order.do(tables, lengths, tokens, out_grad)
    ga.come()
    ga.line_up()
    ga.first()
    gg.ready()
    gg.along_z()
    gg.come()
    gu.along_z()
    gg.line_up()
    ga.got_first()
    ga.join()
    ga.second()
    gg.first()
    x1, cot = order.do(settle, x1, cot)
    gu.come()
    gu.line_up()
    ga.got_second()
    ga.cores()
    gg.got_first()
    gg.join()
    gg.second()
    gu.first()
    gd.along_z()
    hidden1, a1_1, heads1, lse1, mixp1, wqkv_t, wo, gains, x1, cot = order.do(
        lambda *v: first_attention(sz, *v), places, ga.pieces(), x1, cot, rope, bias
    )
    gd.come()
    gd.line_up()
    gd.first()
    gg.got_second()
    gg.cores()
    gu.got_first()
    gu.join()
    gu.second()
    a2_1, gate1, wg = order.do(lambda *v: first_gate(sz, *v), places, gg.pieces(), hidden1, gains)
    gd.got_first()
    gd.join()
    gd.second()
    gu.got_second()
    gu.cores()
    up1, inner1, wu = order.do(lambda *v: first_up(sz, *v), places, gu.pieces(), a2_1, gate1)
    gd.got_second()
    gd.cores()
    down_pieces = gd.pieces()
    if not aligned:
        down_pieces = place_blocks(places, down_pieces)

    (second, carried, wd, a1_2, mixp2, a2_2, gg2, gu2, gl2, g_qkv2, gain2, own, *send) = order.do(
        lambda *v: middle(sz, *v, down_half),
        places, back, down_pieces, hidden1, inner1, wqkv_t, wo, wg, wu, gains, rope, bias, cot,
    )
    if not aligned:
        own, *send = order_blocks(back, own, down_half)
    sd = Scatter(at, order, own, *send)
    sd.first()
    sd.rest()
    gh1, gl1, gu1, gain_f1, own, *send = order.do(
        lambda *v: last_ffn(sz, *v, half), back, carried, hidden1, gains, wg, wu, wd, gate1, up1, (a2_1, a2_2), gg2
    )
    sd.come()
    sd.second()
    sg = Scatter(at, order, own, *send)
    sg.first()
    sg.rest()
    g_x, g_qkv1, gain_a1, own, *send = order.do(
        lambda *v: last_attention(sz, *v, half), back, gh1, gl1, x1, gains, wqkv_t, wo, rope, bias, heads1, lse1,
        (a2_1, a2_2), (gu1, gu2), (mixp1, mixp2), gl2
    )
    sd.come()
    sg.come()
    su = Scatter(at, order, own, *send)
    sg.second()
    su.first()
    su.rest()
    sd.along_z()
    own, *send = order.do(
        lambda *v: qkv_grad(sz, *v, half), back, (a1_1, a1_2), (g_qkv1, g_qkv2), gain2, gain_f1, gain_a1
    )
    sg.come()
    sa = Scatter(at, order, own, *send)
    sg.along_z()
    sa.first()
    sa.rest()
    su.come()
    su.second()
    second, g_x = order.do(lambda *v: tuple(narrow(a, n, real, padded) for a in v), second, g_x)
    sa.come()
    sa.second()
    sd.come_z()
    sd.along_x()
    su.come()
    su.along_z()
    sa.come()
    sa.along_z()
    sg.come_z()
    sg.along_x()
    sd.come()
    sd.cores()
    sg.come()
    sg.cores()
    sd.come()
    r_down = sd.result()
    sg.come()
    r_gate = sg.result()
    sa.come_z()
    sa.along_x()
    su.come_z()
    su.along_x()
    sa.come()
    sa.cores()
    su.come()
    su.cores()
    sa.come()
    r_in = sa.result()
    su.come()
    r_up = su.result()
    kv = key_weight.shape[1]
    return (
        second,
        g_x,
        r_in[:real, :width],
        r_in[:real, width : width + kv],
        r_in[:real, width + kv :],
        narrow(r_up[:real, ff:], n, real, padded),
        r_gate[:real],
        r_up[:real, :ff],
        narrow(r_down, n, real, padded),
        r_in[real, :real],
        r_in[real + 1, :real],
    )


def solution(mesh):
    rows, split, gain = P(("dp", "fsdp"), None), P("fsdp", None), P("fsdp")
    return jax.shard_map(
        functools.partial(shards, mesh),
        mesh=mesh,
        in_specs=(rows, rows) + (split,) * 7 + (gain, gain, rows),
        out_specs=(rows, rows) + (split,) * 7 + (gain, gain),
        check_vma=False,
    )
```

time: 602 us -> 391 us (0.65)
  matrix products: 190 us -> 0 us
  Pallas kernels: 23.7 us -> 133 us
  waiting for transfers between devices: 144 us -> 102 us
  starting transfers between devices: 107 us -> 66.8 us
  local copies, waits for them, and re-layouts: 78.9 us -> 40.7 us
  other arithmetic: 51.4 us -> 40 us
    dot_general x37 -> x0, matrix products: 190 us -> none  [the longest x10 38 us: product_back(): lax.dot_general(left, right, (((1,), (1,)), ((), ())), preferred_element_...]
    pallas_call x4 -> x8, Pallas kernels: 23.7 us -> 133 us  [call(): pl.pallas_call(body, in_specs=specs or [VM] * len(ins), out_specs=out_spe...]
    ppermute x16, waiting for transfers between devices: 108 us -> 44 us  [cross(): return lax.ppermute(v, ('dp', 'fsdp'), pairs)]
    ppermute x24, starting transfers between devices: 66.6 us -> 35.1 us  [shift_z(): lax.ppermute(v, 'fsdp', [(i, (i + 4 * k) % self.n) for i in range(self.n)])]
    another operation x23 -> x1, other arithmetic: 17.7 us -> 0.69 us  [attention_shard(): jnp.stack([gain_attn, gain_ffn])]
    convert_element_type x6 -> x0, local copies, waits for them, and re-layouts: 14.7 us -> none  [the longest x1 4.37 us: shards(): g_in = outer_sum(a1, g_qkv).astype(BF).reshape(n, padded, -1)]
    ppermute x16 -> x24, waiting for transfers between devices: 0.04 us -> 12.2 us  [swap_core(): return lax.ppermute(v, 'fsdp', [(i, i ^ 1) for i in range(self.n)])]
    convert_element_type x24 -> x20, other arithmetic: 21.2 us -> 32.3 us  [the longest x4 8.83 us: first(): add(a[:cut], b).astype(BF)]
  transfers between devices with their start and end apart: 60 -> 68, of which waited for: 21 -> 23; matrix products, arithmetic and copies ran while one was open for 17% -> 17% of each run, Pallas kernels for 3% -> 23%
where the time goes in v2:
time: 391 us; the launch traced here: 385 us
  Pallas kernels  133 us (34%)
  waiting for transfers between devices  102 us (26%)
  starting transfers between devices  66.8 us (17%)
  local copies, waits for them, and re-layouts  40.7 us (10%)
  other arithmetic  40 us (10%)
    pallas_call x8, Pallas kernels, call(): pl.pallas_call(body, in_specs=specs or [VM] * len(ins), out_specs=out_spe...  133 us
    ppermute x16, waiting for transfers between devices, cross(): return lax.ppermute(v, ('dp', 'fsdp'), pairs)  44 us
    ppermute x24, waiting for transfers between devices, shift_z(): lax.ppermute(v, 'fsdp', [(i, (i + 4 * k) % self.n) for i in range(self.n)])  39.1 us
    ppermute x24, starting transfers between devices, shift_z(): lax.ppermute(v, 'fsdp', [(i, (i + 4 * k) % self.n) for i in range(self.n)])  35.1 us
    ppermute x16, starting transfers between devices, cross(): return lax.ppermute(v, ('dp', 'fsdp'), pairs)  18.2 us
    unnamed x86, local copies, waits for them, and re-layouts  15.4 us
    ppermute x24, waiting for transfers between devices, swap_core(): return lax.ppermute(v, 'fsdp', [(i, i ^ 1) for i in range(self.n)])  12.2 us
    ppermute x24, starting transfers between devices, swap_core(): return lax.ppermute(v, 'fsdp', [(i, i ^ 1) for i in range(self.n)])  10.7 us
  transfers between devices with their start and end apart: 68, of which 23 were waited for; matrix products, arithmetic and copies ran while one was open for 17% of the time, Pallas kernels for 23%

profile of v2, /device:TPU:0, one launch (start us, length us, event | category | flops | bytes accessed | tf_op | source)
XLA Modules:
  0.0 385.1 jit_solution(2786834793963327185)
XLA Ops:
  5.5 4.8 %collective-permute-start.6 = (bf16[1,32,2624]{2,1,0:T(8,128)(2,1)S(1)}, bf16[1,32,2624]{2,1,0:T(8,128)(2,1)S(1)}, u32[]{:S(2)}, u32[]{:S(2)}) collective-permute-start(bf16[1,32,2624]{2,1,0:T(8,128)(2,1)S(1)} %select_bitcast_fusion), channel_id=1, source_target_pairs={{0,12},{1,13},{2,14},{3,15},{4,0},{5,1},{6,2},{7,3},{8,4},{9,5},{1... | collective-permute-start | bytes 503816 | tf_op jit(solution)/shard_map/ppermute | solution.py:57
  17.8 7.6 %collective-permute-done.5 = bf16[1,32,2624]{2,1,0:T(8,128)(2,1)S(1)} collective-permute-done((bf16[1,32,2624]{2,1,0:T(8,128)(2,1)S(1)}, bf16[1,32,2624]{2,1,0:T(8,128)(2,1)S(1)}, u32[]{:S(2)}, u32[]{:S(2)}) %collective-permute-start.5) | collective-permute-done | bytes 167968 | tf_op jit(solution)/shard_map/ppermute | solution.py:57
  33.2 10.4 %collective-permute-done.8 = bf16[1,32,2560]{2,1,0:T(8,128)(2,1)} collective-permute-done((bf16[1,32,2560]{2,1,0:T(8,128)(2,1)}, bf16[1,32,2560]{2,1,0:T(8,128)(2,1)}, u32[]{:S(2)}, u32[]{:S(2)}) %collective-permute-start.8) | collective-permute-done | bytes 163872 | tf_op jit(solution)/shard_map/ppermute | solution.py:57
  63.1 15.8 %collective-permute-done.12.p1 = bf16[8,32,2624]{2,1,0:T(8,128)(2,1)} collective-permute-done((bf16[8,32,2624]{2,1,0:T(8,128)(2,1)S(1)}, bf16[8,32,2624]{2,1,0:T(8,128)(2,1)}, u32[]{:S(2)}, u32[]{:S(2)}) %collective-permute-start.12) | collective-permute-done | bytes 1343520 | tf_op jit(solution)/shard_map/ppermute | solution.py:69
  89.3 15.6 %shard_map.204 = (f32[384,1024]{1,0:T(8,128)}, bf16[384,1024]{1,0:T(8,128)(2,1)}, bf16[1600,384]{1,0:T(8,128)(2,1)}, f32[16,384]{1,0:T(8,128)}, bf16[1024,384]{1...) custom-call(s32[32]{0:T(128)} %stack.239.order_ref.refs_0_, ...), custom_call_target="tpu_custom_call" | custom-call | flops 1000 | bytes 1000 | tf_op jit(solution)/shard_map/pallas_call | solution.py:263
  112.8 8.6 %shard_map.205 = (bf16[384,1024]{1,0:T(8,128)(2,1)}, bf16[384,2560]{1,0:T(8,128)(2,1)}, bf16[1024,2560]{1,0:T(8,128)(2,1)}) custom-call(s32[32]{0:T(128)} %stack.239.order_ref.refs_0_, bf16[8,32,2560]{2,1,0:T(8,128)(2,1)} %copy-done.3, bf16[8,32,2560]{2,1,0:T(8,128)(2,1)} %collective-permute-done.22.p1, bf16[8,32,2560]{2,1,0:T(8,128)(2,1)} %copy-done.12, ...), custom_call_target="tpu_custom_call" | custom-call | flops 1000 | bytes 1000 | tf_op jit(solution)/shard_map/pallas_call | solution.py:263
  121.5 6.5 %collective-permute-done.21 = bf16[4,80,1024]{2,1,0:T(8,128)(2,1)S(1)} collective-permute-done((bf16[4,80,1024]{2,1,0:T(8,128)(2,1)}, bf16[4,80,1024]{2,1,0:T(8,128)(2,1)S(1)}, u32[]{:S(2)}, u32[]{:S(2)}) %collective-permute-start.21) | collective-permute-done | bytes 655392 | tf_op jit(solution)/shard_map/ppermute | solution.py:69
  129.2 4.6 %collective-permute-done.27.p1 = bf16[8,32,2560]{2,1,0:T(8,128)(2,1)} collective-permute-done((bf16[8,32,2560]{2,1,0:T(8,128)(2,1)S(1)}, bf16[8,32,2560]{2,1,0:T(8,128)(2,1)}, u32[]{:S(2)}, u32[]{:S(2)}) %collective-permute-start.27) | collective-permute-done | bytes 1310752 | tf_op jit(solution)/shard_map/ppermute | solution.py:69
  137.2 8.5 %shard_map.206 = (bf16[384,2560]{1,0:T(8,128)(2,1)}, bf16[384,2560]{1,0:T(8,128)(2,1)}, bf16[1024,2560]{1,0:T(8,128)(2,1)}) custom-call(s32[32]{0:T(128)} %stack.239.order_ref.refs_0_, bf16[8,32,2560]{2,1,0:T(8,128)(2,1)} %copy-done.2, bf16[8,32,2560]{2,1,0:T(8,128)(2,1)} %collective-permute-done.27.p1, bf16[8,32,2560]{2,1,0:T(8,128)(2,1)} %collective-permute-done.28.p2, ...), custom_call_target="tpu_custom_call" | custom-call | flops 1000 | bytes 1000 | tf_op jit(solution)/shard_map/pallas_call | solution.py:263
  145.7 5.8 %collective-permute-done.26.refs_3_ = bf16[8,80,1024]{2,1,0:T(8,128)(2,1)} collective-permute-done((bf16[8,80,1024]{2,1,0:T(8,128)(2,1)S(1)}, bf16[8,80,1024]{2,1,0:T(8,128)(2,1)}, u32[]{:S(2)}, u32[]{:S(2)}) %collective-permute-start.26) | collective-permute-done | bytes 1310752 | tf_op jit(solution)/shard_map/ppermute | solution.py:69
  155.8 45.5 %shard_map.207 = (bf16[384,1024]{1,0:T(8,128)(2,1)}, f32[384,1024]{1,0:T(8,128)}, bf16[2560,1024]{1,0:T(8,128)(2,1)}, bf16[384,1024]{1,0:T(8,128)(2,1)}, bf16[10...) custom-call(s32[32]{0:T(128)} %stack.239.order_ref.refs_0_, ...), custom_call_target="tpu_custom_call" | custom-call | flops 1000 | bytes 1000 | tf_op jit(solution)/shard_map/pallas_call | solution.py:263
  204.6 3.0 add_convert_fusion.2
  209.2 21.0 %shard_map.208 = (f32[384,1024]{1,0:T(8,128)}, bf16[384,1024]{1,0:T(8,128)(2,1)}, bf16[384,2560]{1,0:T(8,128)(2,1)}, f32[8,1024]{1,0:T(8,128)}, bf16[16,32,2560]...) custom-call(s32[32]{0:T(128)} %stack.272.refs_1_.back_ref, ...), custom_call_target="tpu_custom_call" | custom-call | flops 1000 | bytes 1000 | tf_op jit(solution)/shard_map/pallas_call | solution.py:263
  232.6 2.8 collective-permute-done.36
  240.4 24.1 %shard_map.209 = (bf16[384,1024]{1,0:T(8,128)(2,1)}, bf16[1600,384]{1,0:T(8,128)(2,1)}, f32[8,1024]{1,0:T(8,128)}, bf16[16,32,3584]{2,1,0:T(8,128)(2,1)}, bf16[8...) custom-call(s32[32]{0:T(128)} %stack.272.refs_1_.back_ref, f32[384,1024]{1,0:T(8,128)} %get-tuple-element.532.gh_hbm, ...), custom_call_target="tpu_custom_call" | custom-call | flops 1000 | bytes 1000 | tf_op jit(solution)/shard_map/pallas_call | solution.py:263
  268.7 3.3 add_convert_fusion
  274.4 7.3 %shard_map.210 = (bf16[16,32,1600]{2,1,0:T(8,128)(2,1)}, bf16[8,32,1600]{2,1,0:T(8,128)(2,1)}, bf16[8,32,1600]{2,1,0:T(8,128)(2,1)}) custom-call(s32[32]{0:T(128)} %stack.272.refs_1_.back_ref, bf16[384,1024]{1,0:T(8,128)(2,1)} %get-tuple-element.577.a_1, bf16[384,1024]{1,0:T(8,128)(2,1)} %get-tuple-element.578.a_2, bf16[1600,384]{1,0:T(8,128)(2,1)} %get-tuple-element.579.g1, ...), custom_call_target="tpu_custom_call" | custom-call | flops 1000 | bytes 1000 | tf_op jit(solution)/shard_map/pallas_call | solution.py:263
  290.3 7.0 %collective-permute-done.41 = bf16[8,32,3584]{2,1,0:T(8,128)(2,1)} collective-permute-done((bf16[8,32,3584]{2,1,0:T(8,128)(2,1)}, bf16[8,32,3584]{2,1,0:T(8,128)(2,1)}, u32[]{:S(2)}, u32[]{:S(2)}) %collective-permute-start.41) | collective-permute-done | bytes 1835040 | tf_op jit(solution)/shard_map/ppermute | solution.py:69
  306.1 3.9 %collective-permute-done.45 = bf16[8,32,1600]{2,1,0:T(8,128)(2,1)} collective-permute-done((bf16[8,32,1600]{2,1,0:T(8,128)(2,1)}, bf16[8,32,1600]{2,1,0:T(8,128)(2,1)}, u32[]{:S(2)}, u32[]{:S(2)}) %collective-permute-start.45) | collective-permute-done | bytes 819232 | tf_op jit(solution)/shard_map/ppermute | solution.py:69
  332.7 5.5 %collective-permute-start.67 = (bf16[80,1024]{1,0:T(8,128)(2,1)S(1)}, bf16[80,1024]{1,0:T(8,128)(2,1)S(1)}, u32[]{:S(2)}, u32[]{:S(2)}) collective-permute-start(bf16[80,1024]{1,0:T(8,128)(2,1)S(1)} %get-tuple-element.695), channel_id=1, source_target_pairs={{0,1},{1,0},{2,3},{3,2},{4,5},{5,4},{6,7},{7,6},{8,9},{9,8},{10,11... | collective-permute-start | bytes 491528 | tf_op jit(solution)/shard_map/ppermute | solution.py:54
  338.1 3.5 collective-permute-start.53
  342.3 3.3 collective-permute-start.63
  355.0 16.4 %collective-permute-done.62 = bf16[32,3584]{1,0:T(8,128)(2,1)S(1)} collective-permute-done((bf16[32,3584]{1,0:T(8,128)(2,1)}, bf16[32,3584]{1,0:T(8,128)(2,1)S(1)}, u32[]{:S(2)}, u32[]{:S(2)}) %collective-permute-start.62) | collective-permute-done | bytes 229408 | tf_op jit(solution)/shard_map/ppermute | solution.py:57
  373.0 6.9 %collective-permute-done.65 = bf16[32,3584]{1,0:T(8,128)(2,1)S(1)} collective-permute-done((bf16[32,3584]{1,0:T(8,128)(2,1)S(1)}, bf16[32,3584]{1,0:T(8,128)(2,1)S(1)}, u32[]{:S(2)}, u32[]{:S(2)}) %collective-permute-start.65) | collective-permute-done | bytes 229408 | tf_op jit(solution)/shard_map/ppermute | solution.py:60
  (297 shorter events, 141.2 us)
Async XLA Ops:
  31.6 19.2 %collective-permute-start.10 = (bf16[4,32,2624]{2,1,0:T(8,128)(2,1)S(1)}, bf16[4,32,2624]{2,1,0:T(8,128)(2,1)S(1)}, u32[]{:S(2)}, u32[]{:S(2)}) collective-permute-start(bf16[4,32,2624]{2,1,0:T(8,128)(2,1)S(1)} %constant_dynamic-update-slice_fusion), channel_id=1, source_target_pairs={{0,2},{1,17},{2,0},{3,19},{4,6},{5,21},{6,4},{7,23},{8,10},{9,25},... | collective-permute-start | bytes 2015240 | tf_op jit(solution)/shard_map/ppermute | solution.py:69
  53.4 31.0 %collective-permute-start.19 = (bf16[8,32,2624]{2,1,0:T(8,128)(2,1)S(1)}, bf16[8,32,2624]{2,1,0:T(8,128)(2,1)}, u32[]{:S(2)}, u32[]{:S(2)}) collective-permute-start(bf16[8,32,2624]{2,1,0:T(8,128)(2,1)S(1)} %constant_dynamic-update-slice_fusion.8.p0), channel_id=1, source_target_pairs={{0,1},{1,0},{2,3},{3,2},{4,5},{5,4},{6,7},{7,6},{8,9},{9,8},{10,11... | collective-permute-start | bytes 4030472 | tf_op jit(solution)/shard_map/ppermute | solution.py:54
  53.4 25.5 %collective-permute-start.12 = (bf16[8,32,2624]{2,1,0:T(8,128)(2,1)S(1)}, bf16[8,32,2624]{2,1,0:T(8,128)(2,1)}, u32[]{:S(2)}, u32[]{:S(2)}) collective-permute-start(bf16[8,32,2624]{2,1,0:T(8,128)(2,1)S(1)} %constant_dynamic-update-slice_fusion.8.p0), channel_id=1, source_target_pairs={{0,16},{1,3},{2,18},{3,1},{4,20},{5,7},{6,22},{7,5},{8,24},{9,11},... | collective-permute-start | bytes 4030472 | tf_op jit(solution)/shard_map/ppermute | solution.py:69
  57.6 21.3 %collective-permute-start.11 = (bf16[4,32,2560]{2,1,0:T(8,128)(2,1)S(1)}, bf16[4,32,2560]{2,1,0:T(8,128)(2,1)S(1)}, u32[]{:S(2)}, u32[]{:S(2)}) collective-permute-start(bf16[4,32,2560]{2,1,0:T(8,128)(2,1)S(1)} %copy-done.17), channel_id=1, source_target_pairs={{0,2},{1,17},{2,0},{3,19},{4,6},{5,21},{6,4},{7,23},{8,10},{9,25},... | collective-permute-start | bytes 1966088 | tf_op jit(solution)/shard_map/ppermute | solution.py:69
  79.1 28.7 %collective-permute-start.22 = (bf16[8,32,2560]{2,1,0:T(8,128)(2,1)S(1)}, bf16[8,32,2560]{2,1,0:T(8,128)(2,1)}, u32[]{:S(2)}, u32[]{:S(2)}) collective-permute-start(bf16[8,32,2560]{2,1,0:T(8,128)(2,1)S(1)} %constant_dynamic-update-slice_fusion.14.p0), channel_id=1, source_target_pairs={{0,16},{1,3},{2,18},{3,1},{4,20},{5,7},{6,22},{7,5},{8,24},{9,11},... | collective-permute-start | bytes 3932168 | tf_op jit(solution)/shard_map/ppermute | solution.py:69
  81.9 23.0 %collective-permute-start.18 = (bf16[1,80,1024]{2,1,0:T(8,128)(2,1)S(1)}, bf16[1,80,1024]{2,1,0:T(8,128)(2,1)S(1)}, u32[]{:S(2)}, u32[]{:S(2)}) collective-permute-start(bf16[1,80,1024]{2,1,0:T(8,128)(2,1)S(1)} %copy-done.25), channel_id=1, source_target_pairs={{0,12},{1,13},{2,14},{3,15},{4,0},{5,1},{6,2},{7,3},{8,4},{9,5},{1... | collective-permute-start | bytes 491528 | tf_op jit(solution)/shard_map/ppermute | solution.py:57
  83.8 21.2 %collective-permute-start.17 = (bf16[1,80,1024]{2,1,0:T(8,128)(2,1)S(1)}, bf16[1,80,1024]{2,1,0:T(8,128)(2,1)S(1)}, u32[]{:S(2)}, u32[]{:S(2)}) collective-permute-start(bf16[1,80,1024]{2,1,0:T(8,128)(2,1)S(1)} %copy-done.25), channel_id=1, source_target_pairs={{0,8},{1,9},{2,10},{3,11},{4,12},{5,13},{6,14},{7,15},{8,0},{9,1},... | collective-permute-start | bytes 491528 | tf_op jit(solution)/shard_map/ppermute | solution.py:57
  84.4 20.6 %collective-permute-start.16 = (bf16[1,80,1024]{2,1,0:T(8,128)(2,1)S(1)}, bf16[1,80,1024]{2,1,0:T(8,128)(2,1)S(1)}, u32[]{:S(2)}, u32[]{:S(2)}) collective-permute-start(bf16[1,80,1024]{2,1,0:T(8,128)(2,1)S(1)} %copy-done.25), channel_id=1, source_target_pairs={{0,4},{1,5},{2,6},{3,7},{4,8},{5,9},{6,10},{7,11},{8,12},{9,13},{1... | collective-permute-start | bytes 491528 | tf_op jit(solution)/shard_map/ppermute | solution.py:57
  86.8 20.9 %collective-permute-start.25 = (bf16[4,32,2560]{2,1,0:T(8,128)(2,1)S(1)}, bf16[4,32,2560]{2,1,0:T(8,128)(2,1)}, u32[]{:S(2)}, u32[]{:S(2)}) collective-permute-start(bf16[4,32,2560]{2,1,0:T(8,128)(2,1)S(1)} %copy-done.20), channel_id=1, source_target_pairs={{0,2},{1,17},{2,0},{3,19},{4,6},{5,21},{6,4},{7,23},{8,10},{9,25},... | collective-permute-start | bytes 1966088 | tf_op jit(solution)/shard_map/ppermute | solution.py:69
  109.5 24.3 %collective-permute-start.27 = (bf16[8,32,2560]{2,1,0:T(8,128)(2,1)S(1)}, bf16[8,32,2560]{2,1,0:T(8,128)(2,1)}, u32[]{:S(2)}, u32[]{:S(2)}) collective-permute-start(bf16[8,32,2560]{2,1,0:T(8,128)(2,1)S(1)} %constant_dynamic-update-slice_fusion.20.p0), channel_id=1, source_target_pairs={{0,16},{1,3},{2,18},{3,1},{4,20},{5,7},{6,22},{7,5},{8,24},{9,11},... | collective-permute-start | bytes 3932168 | tf_op jit(solution)/shard_map/ppermute | solution.py:69
  110.1 17.9 %collective-permute-start.21 = (bf16[4,80,1024]{2,1,0:T(8,128)(2,1)}, bf16[4,80,1024]{2,1,0:T(8,128)(2,1)S(1)}, u32[]{:S(2)}, u32[]{:S(2)}) collective-permute-start(bf16[4,80,1024]{2,1,0:T(8,128)(2,1)} %constant_dynamic-update-slice_fusion.16), channel_id=1, source_target_pairs={{0,2},{1,17},{2,0},{3,19},{4,6},{5,21},{6,4},{7,23},{8,10},{9,25},... | collective-permute-start | bytes 1966088 | tf_op jit(solution)/shard_map/ppermute | solution.py:69
  110.6 24.4 %collective-permute-start.28 = (bf16[8,32,2560]{2,1,0:T(8,128)(2,1)S(1)}, bf16[8,32,2560]{2,1,0:T(8,128)(2,1)}, u32[]{:S(2)}, u32[]{:S(2)}) collective-permute-start(bf16[8,32,2560]{2,1,0:T(8,128)(2,1)S(1)} %constant_dynamic-update-slice_fusion.20.p0), channel_id=1, source_target_pairs={{0,1},{1,0},{2,3},{3,2},{4,5},{5,4},{6,7},{7,6},{8,9},{9,8},{10,11... | collective-permute-start | bytes 3932168 | tf_op jit(solution)/shard_map/ppermute | solution.py:54
  133.8 17.7 %collective-permute-start.26 = (bf16[8,80,1024]{2,1,0:T(8,128)(2,1)S(1)}, bf16[8,80,1024]{2,1,0:T(8,128)(2,1)}, u32[]{:S(2)}, u32[]{:S(2)}) collective-permute-start(bf16[8,80,1024]{2,1,0:T(8,128)(2,1)S(1)} %constant_dynamic-update-slice_fusion.22.refs_2_), channel_id=1, source_target_pairs={{0,16},{1,3},{2,18},{3,1},{4,20},{5,7},{6,22},{7,5},{8,24},{9,11},... | collective-permute-start | bytes 3932168 | tf_op jit(solution)/shard_map/ppermute | solution.py:69
  134.3 18.1 %collective-permute-start.30 = (bf16[8,80,1024]{2,1,0:T(8,128)(2,1)S(1)}, bf16[8,80,1024]{2,1,0:T(8,128)(2,1)}, u32[]{:S(2)}, u32[]{:S(2)}) collective-permute-start(bf16[8,80,1024]{2,1,0:T(8,128)(2,1)S(1)} %constant_dynamic-update-slice_fusion.22.refs_2_), channel_id=1, source_target_pairs={{0,1},{1,0},{2,3},{3,2},{4,5},{5,4},{6,7},{7,6},{8,9},{9,8},{10,11... | collective-permute-start | bytes 3932168 | tf_op jit(solution)/shard_map/ppermute | solution.py:54
  207.6 22.6 %collective-permute-start.34 = (bf16[8,80,1024]{2,1,0:T(8,128)(2,1)}, bf16[8,80,1024]{2,1,0:T(8,128)(2,1)}, u32[]{:S(2)}, u32[]{:S(2)}) collective-permute-start(bf16[8,80,1024]{2,1,0:T(8,128)(2,1)} %add_convert_fusion.2), channel_id=1, source_target_pairs={{0,16},{1,3},{2,18},{3,1},{4,20},{5,7},{6,22},{7,5},{8,24},{9,11},... | collective-permute-start | bytes 3932168 | tf_op jit(solution)/shard_map/ppermute | solution.py:69
  236.9 27.6 %collective-permute-start.37 = (bf16[8,32,2560]{2,1,0:T(8,128)(2,1)}, bf16[8,32,2560]{2,1,0:T(8,128)(2,1)}, u32[]{:S(2)}, u32[]{:S(2)}) collective-permute-start(bf16[8,32,2560]{2,1,0:T(8,128)(2,1)} %add_convert_fusion.1), channel_id=1, source_target_pairs={{0,16},{1,3},{2,18},{3,1},{4,20},{5,7},{6,22},{7,5},{8,24},{9,11},... | collective-permute-start | bytes 3932168 | tf_op jit(solution)/shard_map/ppermute | solution.py:69
  239.4 25.1 %collective-permute-start.38 = (bf16[4,80,1024]{2,1,0:T(8,128)(2,1)S(1)}, bf16[4,80,1024]{2,1,0:T(8,128)(2,1)}, u32[]{:S(2)}, u32[]{:S(2)}) collective-permute-start(bf16[4,80,1024]{2,1,0:T(8,128)(2,1)S(1)} %add_convert_fusion.9), channel_id=1, source_target_pairs={{0,2},{1,17},{2,0},{3,19},{4,6},{5,21},{6,4},{7,23},{8,10},{9,25},... | collective-permute-start | bytes 1966088 | tf_op jit(solution)/shard_map/ppermute | solution.py:69
  272.0 25.4 %collective-permute-start.41 = (bf16[8,32,3584]{2,1,0:T(8,128)(2,1)}, bf16[8,32,3584]{2,1,0:T(8,128)(2,1)}, u32[]{:S(2)}, u32[]{:S(2)}) collective-permute-start(bf16[8,32,3584]{2,1,0:T(8,128)(2,1)} %add_convert_fusion), channel_id=1, source_target_pairs={{0,16},{1,3},{2,18},{3,1},{4,20},{5,7},{6,22},{7,5},{8,24},{9,11},... | collective-permute-start | bytes 5505032 | tf_op jit(solution)/shard_map/ppermute | solution.py:69
  285.6 44.2 %collective-permute-start.56 = (bf16[32,2560]{1,0:T(8,128)(2,1)}, bf16[32,2560]{1,0:T(8,128)(2,1)S(1)}, u32[]{:S(2)}, u32[]{:S(2)}) collective-permute-start(bf16[32,2560]{1,0:T(8,128)(2,1)} %get-tuple-element.674), channel_id=1, source_target_pairs={{0,12},{1,13},{2,14},{3,15},{4,0},{5,1},{6,2},{7,3},{8,4},{9,5},{1... | collective-permute-start | bytes 491528 | tf_op jit(solution)/shard_map/ppermute | solution.py:57
  288.6 21.3 %collective-permute-start.45 = (bf16[8,32,1600]{2,1,0:T(8,128)(2,1)}, bf16[8,32,1600]{2,1,0:T(8,128)(2,1)}, u32[]{:S(2)}, u32[]{:S(2)}) collective-permute-start(bf16[8,32,1600]{2,1,0:T(8,128)(2,1)} %add_convert_fusion.5), channel_id=1, source_target_pairs={{0,16},{1,3},{2,18},{3,1},{4,20},{5,7},{6,22},{7,5},{8,24},{9,11},... | collective-permute-start | bytes 2457608 | tf_op jit(solution)/shard_map/ppermute | solution.py:69
  299.1 24.2 %collective-permute-start.47 = (bf16[4,32,3584]{2,1,0:T(8,128)(2,1)S(1)}, bf16[4,32,3584]{2,1,0:T(8,128)(2,1)}, u32[]{:S(2)}, u32[]{:S(2)}) collective-permute-start(bf16[4,32,3584]{2,1,0:T(8,128)(2,1)S(1)} %add_convert_fusion.4), channel_id=1, source_target_pairs={{0,2},{1,17},{2,0},{3,19},{4,6},{5,21},{6,4},{7,23},{8,10},{9,25},... | collective-permute-start | bytes 2752520 | tf_op jit(solution)/shard_map/ppermute | solution.py:69
  348.2 23.2 %collective-permute-start.62 = (bf16[32,3584]{1,0:T(8,128)(2,1)}, bf16[32,3584]{1,0:T(8,128)(2,1)S(1)}, u32[]{:S(2)}, u32[]{:S(2)}) collective-permute-start(bf16[32,3584]{1,0:T(8,128)(2,1)} %get-tuple-element.672), channel_id=1, source_target_pairs={{0,8},{1,9},{2,10},{3,11},{4,12},{5,13},{6,14},{7,15},{8,0},{9,1},... | collective-permute-start | bytes 688136 | tf_op jit(solution)/shard_map/ppermute | solution.py:57
  351.2 20.2 %collective-permute-start.61 = (bf16[32,3584]{1,0:T(8,128)(2,1)S(1)}, bf16[32,3584]{1,0:T(8,128)(2,1)S(1)}, u32[]{:S(2)}, u32[]{:S(2)}) collective-permute-start(bf16[32,3584]{1,0:T(8,128)(2,1)S(1)} %copy-done.29), channel_id=1, source_target_pairs={{0,4},{1,5},{2,6},{3,7},{4,8},{5,9},{6,10},{7,11},{8,12},{9,13},{1... | collective-permute-start | bytes 688136 | tf_op jit(solution)/shard_map/ppermute | solution.py:57
  353.2 19.6 %collective-permute-start.60 = (bf16[32,1600]{1,0:T(8,128)(2,1)S(1)}, bf16[32,1600]{1,0:T(8,128)(2,1)S(1)}, u32[]{:S(2)}, u32[]{:S(2)}) collective-permute-start(bf16[32,1600]{1,0:T(8,128)(2,1)S(1)} %fusion.21), channel_id=1, source_target_pairs={{0,16},{16,0},{1,17},{17,1},{2,18},{18,2},{3,19},{19,3},{4,20},{20... | collective-permute-start | bytes 307208 | tf_op jit(solution)/shard_map/ppermute | solution.py:60
  (79 other events, 668.9 us)

commit v3 on v2

v3 whole, which is shorter than its diff:
```python
import functools
import math

import jax
import jax.numpy as jnp
from jax import lax
from jax.experimental import pallas as pl
from jax.experimental.pallas import tpu as pltpu
from jax.sharding import PartitionSpec as P

HEAD_SIZE = 64
GROUP = 3
ROPE_BASE = 10000.0
EPS = 1e-05
BF = jnp.bfloat16
F32 = jnp.float32
MIB = 1024 * 1024


def layout(doc_lengths, token_count):
    ends = jnp.cumsum(doc_lengths, axis=1)
    starts = ends - doc_lengths
    place = jnp.arange(token_count, dtype=jnp.int32)
    document = jnp.sum((place[None, :, None] >= ends[:, None, :]).astype(jnp.int32), axis=2)
    inside = place[None, :] < ends[:, -1:]
    segment = jnp.where(inside, document, -1)
    chosen = (
        document[:, :, None] == jnp.arange(doc_lengths.shape[1], dtype=jnp.int32)[None, None, :]
    )
    begin = jnp.sum(jnp.where(chosen, starts[:, None, :], 0), axis=2)
    positions = jnp.where(inside, place[None, :] - begin, 0)
    causal = place[:, None] >= place[None, :]
    same = (segment[:, :, None] == segment[:, None, :]) & (segment[:, :, None] >= 0)
    allowed = same & causal[None] | (place[:, None] == place[None, :])[None]
    return (positions, allowed)


def rotation(positions):
    half = HEAD_SIZE // 2
    frequency = jnp.exp(jnp.arange(half, dtype=F32) * (-2.0 * math.log(ROPE_BASE) / HEAD_SIZE))
    angle = positions.astype(F32)[None, :] * frequency[:, None]
    return (jnp.cos(angle), jnp.sin(angle))


class Place:
    def __init__(self, mesh):
        self.n, self.groups = mesh.shape["fsdp"], mesh.shape["dp"]
        self.nz = self.n // 4
        i = lax.axis_index("fsdp")
        self.c, self.y, self.z = i % 2, (i // 2) % 2, i // 4
        self.p = lax.axis_index("dp") % 2

    def swap_core(self, v):
        return lax.ppermute(v, "fsdp", [(i, i ^ 1) for i in range(self.n)])

    def shift_z(self, v, k):
        return lax.ppermute(v, "fsdp", [(i, (i + 4 * k) % self.n) for i in range(self.n)])

    def swap_x(self, v):
        return lax.ppermute(v, "dp", [(d, d ^ 1) for d in range(self.groups)])

    def cross(self, v, first):
        pairs = []
        for d in range(self.groups):
            for i in range(self.n):
                along_x = (i % 2 == 0) == first
                e, j = (d ^ 1, i) if along_x else (d, i ^ 2)
                pairs.append((d * self.n + i, e * self.n + j))
        return lax.ppermute(v, ("dp", "fsdp"), pairs)

    def piece_order(self):
        order = []
        for h in (self.c, 1 - self.c):
            for j in range(4 * self.nz):
                dz, slot = j % self.nz, j // self.nz
                lo, hi = slot % 2, slot // 2
                dy, dc = jnp.where(h == 0, lo, hi), jnp.where(h == 0, hi, lo)
                z = (self.z - dz + self.nz) % self.nz
                order.append((((z * 2 + (self.y ^ dy)) * 2 + (self.p ^ dc)) * 2 + h).astype(jnp.int32))
        return jnp.stack(order)

    def grad_order(self):
        order = [(self.z + k) % self.nz for k in range(self.nz)]
        for h in (self.c, 1 - self.c):
            for hi in (0, 1):
                for lo in (0, 1):
                    of_c, of_y = jnp.where(h == 0, hi, lo), jnp.where(h == 0, lo, hi)
                    c = jnp.where(of_c == 1, self.p, 1 - self.p)
                    y = jnp.where(of_y == 1, self.y, 1 - self.y)
                    order.append((y * 2 + c) * 2 + h)
        return jnp.stack(order).astype(jnp.int32)


def pick(v, k, axis=0):
    return lax.dynamic_index_in_dim(v, k, axis, keepdims=False)


class Order:
    def __init__(self):
        self.last = ()

    def do(self, step, *inputs):
        leaves, tree = jax.tree.flatten(inputs)
        if self.last:
            leaves = lax.optimization_barrier((*leaves, *self.last))[: len(leaves)]
        out = step(*jax.tree.unflatten(tree, leaves))
        self.last = (jax.tree.leaves(out)[0],)
        return out

    def tie(self, v):
        return lax.optimization_barrier((v, *self.last))[0] if self.last else v

    def got(self, *received):
        out = lax.optimization_barrier((*received, *self.last))[: len(received)]
        self.last = (out[0],)
        return out[0] if len(out) == 1 else out


def add(*terms):
    return functools.reduce(lambda a, b: a + b, [t.astype(F32) for t in terms])


class Gather:
    def __init__(self, at, order):
        self.at, self.order = at, order

    def start(self, make, *inputs):
        def step(*inputs):
            shard = make(*inputs)
            halves = shard.reshape(2, shard.shape[0] // 2, shard.shape[1])
            return pick(halves, self.at.c), pick(halves, 1 - self.at.c)

        self.keep, send = self.order.do(step, *inputs)
        self.moving = self.at.swap_core(send)

    def ready(self):
        at = self.at
        got = self.order.got(self.moving)
        self.mine = self.order.do(lambda k, g: jnp.where(at.p == at.c, k, g)[None], self.keep, got)

    def along_z(self):
        mine = self.order.tie(self.mine)
        self.moving = [self.at.shift_z(mine, k) for k in range(1, self.at.nz)]

    def come(self):
        parts = self.order.got(*self.moving)
        self.parts = parts if isinstance(parts, tuple) else (parts,)

    def line_up(self):
        self.line = self.order.do(lambda *v: jnp.concatenate(v), self.mine, *self.parts)

    def first(self):
        self.moving = self.at.cross(self.order.tie(self.line), False)

    def got_first(self):
        self.got = self.order.got(self.moving)

    def second(self):
        self.both = self.order.do(lambda *v: jnp.concatenate(v), self.line, self.got)
        self.moving = self.at.cross(self.both, True)
        self.others = []

    def got_second(self):
        self.third = self.order.got(self.moving)

    def cores(self, *which):
        self.others += [self.at.swap_core(self.order.tie(v)) for v in which or (self.both, self.third)]

    def pieces(self):
        return (self.both, self.third, *self.order.got(*self.others))


class Scatter:
    def __init__(self, at, order, own, *send):
        self.at, self.order, self.own = at, order, own
        self.send, self.swaps, self.other = send, {}, {}

    def core(self, k):
        self.swaps[k] = self.at.swap_core(self.order.tie(self.send[k]))

    def sums(self, *terms):
        cuts = [(lo, lo + count) for _, lo, count in terms]

        def step(*v):
            return add(*[a[lo:hi] for a, (lo, hi) in zip(v, cuts)]).astype(BF)

        return self.order.do(step, *[a for a, _, _ in terms])

    def come(self):
        self.got = self.order.got(self.moving)

    def come_core(self, k):
        self.other[k] = self.order.got(self.swaps[k])

    def first(self):
        two = 2 * self.at.nz
        self.moving = self.at.cross(self.sums((self.own, 0, two), (self.other[0], 0, two)), True)

    def second(self):
        nz = self.at.nz
        self.crossed = self.got
        sent = self.sums((self.own, 2 * nz, nz), (self.other[1], 0, nz), (self.crossed, 0, nz))
        self.moving = self.at.cross(sent, False)

    def along_z(self):
        nz = self.at.nz
        self.low = self.sums((self.own, 3 * nz, nz), (self.other[1], nz, nz), (self.crossed, nz, nz), (self.got, 0, nz))
        self.moving = [self.at.shift_z(self.low[k : k + 1], k) for k in range(1, nz)]

    def come_z(self):
        parts = self.order.got(*self.moving)
        self.parts = parts if isinstance(parts, tuple) else (parts,)

    def along_x(self):
        total = self.sums((self.low, 0, 1), *[(p, 0, 1) for p in self.parts])[0]
        step = 2
        while step < self.at.groups:
            pairs = [(d, d ^ step) for d in range(self.at.groups)]
            total = add(total, lax.ppermute(total, "dp", pairs)).astype(BF)
            step *= 2
        self.total = total
        self.moving = self.at.swap_x(total)

    def cores(self):
        here = self.at.p == self.at.c
        self.keep, send = self.order.do(
            lambda a, b: (jnp.where(here, a, b), jnp.where(here, b, a)), self.total, self.got
        )
        self.moving = self.at.swap_core(send)

    def result(self):
        first = self.at.c == 0
        return self.order.do(
            lambda a, b: jnp.concatenate([jnp.where(first, a, b), jnp.where(first, b, a)]).astype(F32), self.keep, self.got
        )


VM = pl.BlockSpec(memory_space=pltpu.VMEM)
ANY = pl.BlockSpec(memory_space=pl.ANY)
SMEM = pl.BlockSpec(memory_space=pltpu.SMEM)


def nn(left, right):
    return jnp.dot(left, right, preferred_element_type=F32)


def nt(left, right):
    return lax.dot_general(left, right, (((1,), (1,)), ((), ())), preferred_element_type=F32)


def tn(left, right):
    return lax.dot_general(left, right, (((0,), (0,)), ((), ())), preferred_element_type=F32)


def tt(left, right):
    return lax.dot_general(left, right, (((0,), (1,)), ((), ())), preferred_element_type=F32)


def join(parts, axis):
    return jnp.concatenate(parts, axis=axis) if len(parts) > 1 else parts[0]


def call(body, ins, outs, scratch, flops, limit, specs=None, out_specs=None):
    return pl.pallas_call(
        body,
        in_specs=specs or [VM] * len(ins),
        out_specs=out_specs or [VM] * len(outs),
        out_shape=outs,
        scratch_shapes=scratch,
        compiler_params=pltpu.CompilerParams(vmem_limit_bytes=max(limit, 60) * MIB),
        cost_estimate=pl.CostEstimate(flops=1000, bytes_accessed=1000, transcendentals=0),
    )(*ins)


def fetches(order_ref, pieces, dests, sem, base):
    copies = []
    half = pieces[0].shape[1]
    at = 0
    for ref in pieces:
        for j in range(ref.shape[0]):
            row = pl.multiple_of(order_ref[at] * half, half)
            at += 1
            for dest, col in dests:
                whole = col == 0 and dest.shape[1] == ref.shape[2]
                src = ref.at[j] if whole else ref.at[j, :, pl.ds(col, dest.shape[1])]
                copies.append(
                    pltpu.make_async_copy(src, dest.at[pl.ds(row, half), :], sem.at[base + len(copies)])
                )
    return copies


class Copies:
    def __init__(self, sem):
        self.sem, self.used, self.open = sem, 0, []

    def start(self, source, dest):
        copy = pltpu.make_async_copy(source, dest, self.sem.at[self.used])
        self.used += 1
        copy.start()
        return copy

    def store(self, source, dest):
        self.open.append(self.start(source, dest))

    def blocks(self, order_ref, nz, k, source, base, half, own, sends):
        for quarter in range(4):
            place, part = quarter % 2 * nz + k, quarter // 2
            for first, dest in ((0, own.at[2 * nz * part + place]), (4, sends[part].at[place])):
                row = base + pl.multiple_of(order_ref[nz + first + quarter] * half, half)
                self.store(source.at[pl.ds(row, half), :], dest)

    def close(self):
        wait(self.open)
        self.open = []


def start(copies):
    for copy in copies:
        copy.start()
    return copies


def wait(copies):
    for copy in copies:
        copy.wait()


def inverse_rms(v, width):
    return lax.rsqrt(jnp.sum(v * v, axis=1, keepdims=True) * (1.0 / width) + EPS)


def norm_back(values, gain, grad, width):
    scale = inverse_rms(values, width)
    unit = values * scale
    gain_grad = jnp.sum(grad * unit, axis=0, keepdims=True)
    inner = grad * gain
    mean = jnp.sum(inner * unit, axis=1, keepdims=True) * (1.0 / width)
    return gain_grad, scale * (inner - unit * mean)


class Sizes:
    def __init__(self, n, real, padded, ff, t, kv):
        self.n, self.real, self.padded, self.ff, self.t = n, real, padded, ff, t
        self.width, self.wide = n * real, n * padded
        self.hq, self.kvh = self.width // HEAD_SIZE, kv // HEAD_SIZE
        self.heads = self.hq + 2 * self.kvh
        self.feat = self.heads * HEAD_SIZE
        self.group = self.hq // self.kvh
        self.lse = -(-self.hq // 8) * 8
        self.block = 128 if t % 128 == 0 else t
        self.blocks = t // self.block
        self.tile = 512 if ff % 512 == 0 else ff


def head(ref, h):
    return ref[h * HEAD_SIZE : (h + 1) * HEAD_SIZE, :]


def by_block(sz, parts, op):
    b = sz.block
    return [
        functools.reduce(op, [parts[j][:, b * (i - j) : b * (i - j + 1)] for j in range(i + 1)])
        for i in range(sz.blocks)
    ]


def plus(a, b):
    return a + b


def attention_forward(sz, x, gain, wqkv, wo, cos, sin, bias, a1, heads, lse, mixp, mix, done=lambda stage: None):
    b, half = sz.block, HEAD_SIZE // 2
    a1[...] = (x * inverse_rms(x, sz.width) * gain).astype(BF)
    for c in range(0, sz.heads, 4):
        end = min(c + 4, sz.heads)
        part = tt(wqkv[:, c * HEAD_SIZE : end * HEAD_SIZE], a1[...])
        for h in range(c, end):
            lo = (h - c) * HEAD_SIZE
            first, second = part[lo : lo + half], part[lo + half : lo + HEAD_SIZE]
            if h < sz.hq + sz.kvh:
                first, second = (
                    first * cos[...] - second * sin[...],
                    second * cos[...] + first * sin[...],
                )
            if h < sz.hq:
                first, second = first * HEAD_SIZE ** (-0.5), second * HEAD_SIZE ** (-0.5)
            heads[h * HEAD_SIZE : h * HEAD_SIZE + half, :] = first.astype(BF)
            heads[h * HEAD_SIZE + half : (h + 1) * HEAD_SIZE, :] = second.astype(BF)
    done(0)
    if sz.lse > sz.hq:
        lse[...] = jnp.zeros(lse.shape, F32)
    for g in range(sz.kvh):
        k = head(heads, sz.hq + g).T
        vt = head(heads, sz.hq + sz.kvh + g)
        for r in range(sz.group):
            h = g * sz.group + r
            q = head(heads, h)
            ss = [
                nn(k[b * j : b * (j + 1)], q[:, b * j :]) + bias[b * j : b * (j + 1), b * j :]
                for j in range(sz.blocks)
            ]
            top = by_block(sz, [jnp.max(s, axis=0, keepdims=True) for s in ss], jnp.maximum)
            sums, out = [], None
            for j in range(sz.blocks):
                e = jnp.exp(ss[j] - join(top[j:], 1))
                sums.append(jnp.sum(e, axis=0, keepdims=True))
                part = nn(vt[:, b * j : b * (j + 1)], e.astype(BF))
                if j:
                    part = jnp.concatenate([jnp.zeros((HEAD_SIZE, b * j), F32), part], axis=1)
                out = part if out is None else out + part
            summed = join(by_block(sz, sums, plus), 1)
            mix[h * HEAD_SIZE : (h + 1) * HEAD_SIZE, :] = out * (1.0 / summed)
            lse[h : h + 1, :] = join(top, 1) + jnp.log(summed)
    row = lax.broadcasted_iota(jnp.int32, (sz.padded, sz.t), 0)
    for j in range(sz.n):
        part = mix[sz.real * j : sz.real * j + sz.padded, :]
        mixp[sz.padded * j : sz.padded * (j + 1), :] = jnp.where(row < sz.real, part, 0.0).astype(BF)
    done(1)
    return x + tn(mixp[...], wo[...])


def attention_backward(sz, gh, gl, x, gain, wqkv, wo, cos, sin, bias, heads, lse, gm, g_heads, gs_ref, p_ref, g_qkv, ready=None):
    b, half = sz.block, HEAD_SIZE // 2
    for j in range(sz.n):
        part = nt(wo[sz.padded * j : sz.padded * (j + 1), :], gl) if sz.n < 4 else None
        if part is not None:
            gm[sz.real * j : sz.real * j + sz.padded, :] = part
    if sz.n >= 4:
        quarter = sz.n // 4
        for c in range(4):
            part = nt(wo[sz.padded * quarter * c : sz.padded * quarter * (c + 1), :], gl)
            for j in range(quarter):
                at = sz.real * (quarter * c + j)
                gm[at : at + sz.padded, :] = part[sz.padded * j : sz.padded * (j + 1)]
    if ready is not None:
        ready(False)
    for g in range(sz.kvh):
        kt = head(heads, sz.hq + g)
        k = kt.T
        v = head(heads, sz.hq + sz.kvh + g).T
        gk = gv = None
        for r in range(sz.group):
            h = g * sz.group + r
            q, gmh = head(heads, h), head(gm, h).astype(BF)
            row = lse[h : h + 1, :]
            ps, gps, down = [], [], []
            for j in range(sz.blocks):
                lo = b * j
                s = nn(k[lo : lo + b], q[:, lo:]) + bias[lo : lo + b, lo:]
                p = jnp.exp(s - row[:, lo:])
                gp = nn(v[lo : lo + b], gmh[:, lo:])
                ps.append(p)
                gps.append(gp)
                down.append(jnp.sum(p * gp, axis=0, keepdims=True))
            d = by_block(sz, down, plus)
            for j in range(sz.blocks):
                lo = b * j
                gs_ref[r, lo : lo + b, lo:] = (ps[j] * (gps[j] - join(d[j:], 1))).astype(BF)
                p_ref[r, lo : lo + b, lo:] = ps[j].astype(BF)
            gq = join(
                [
                    nn(kt[:, : b * (i + 1)], gs_ref[r, : b * (i + 1), b * i : b * (i + 1)])
                    for i in range(sz.blocks)
                ],
                1,
            )
            part_k = join([nt(q[:, b * j :], gs_ref[r, b * j : b * (j + 1), b * j :]) for j in range(sz.blocks)], 1)
            part_v = join([nt(gmh[:, b * j :], p_ref[r, b * j : b * (j + 1), b * j :]) for j in range(sz.blocks)], 1)
            g_heads[h * HEAD_SIZE : (h + 1) * HEAD_SIZE, :] = gq * HEAD_SIZE ** (-0.5)
            gk = part_k if gk is None else gk + part_k
            gv = part_v if gv is None else gv + part_v
        at = (sz.hq + g) * HEAD_SIZE
        g_heads[at : at + HEAD_SIZE, :] = gk
        at = (sz.hq + sz.kvh + g) * HEAD_SIZE
        g_qkv[at : at + HEAD_SIZE, :] = gv.astype(BF)
    for h in range(sz.hq + sz.kvh):
        at = h * HEAD_SIZE
        first, second = g_heads[at : at + half, :], g_heads[at + half : at + HEAD_SIZE, :]
        g_qkv[at : at + half, :] = (first * cos[...] + second * sin[...]).astype(BF)
        g_qkv[at + half : at + HEAD_SIZE, :] = (second * cos[...] - first * sin[...]).astype(BF)
    if ready is not None:
        ready(True)
    gain_grad, back = norm_back(x[...], gain, tt(g_qkv[...], wqkv[...]), sz.width)
    return gain_grad, gh[...] + back


def ffn_up(sz, hidden, gain, a2, wg, wu, gate, up, inner):
    a2[...] = (hidden * inverse_rms(hidden, sz.width) * gain).astype(BF)
    for c in range(0, sz.ff, sz.tile):
        cols = slice(c, c + sz.tile)
        gate_part = nn(a2[...], wg[:, cols])
        up_part = nn(a2[...], wu[:, cols])
        gate[:, cols] = gate_part.astype(BF)
        up[:, cols] = up_part.astype(BF)
        inner[:, cols] = (gate_part * jax.nn.sigmoid(gate_part) * up_part).astype(BF)


def ffn_back_tile(cl, wd, gate, up, gg, gu, cols):
    g_inner = nt(cl[...], wd[cols, :])
    z = gate[:, cols].astype(F32)
    sg = jax.nn.sigmoid(z)
    silu = z * sg
    gg[:, cols] = (g_inner * up[:, cols].astype(F32) * (sg + silu * (1.0 - sg))).astype(BF)
    gu[:, cols] = (g_inner * silu).astype(BF)


def ffn_backward(sz, grad, cl, hidden, gain, wg, wu, wd, gate, up, gg, gu):
    for c in range(0, sz.ff, sz.tile):
        ffn_back_tile(cl, wd, gate, up, gg, gu, slice(c, c + sz.tile))
    g_a2 = nt(gg[...], wg[...]) + nt(gu[...], wu[...])
    gain_grad, back = norm_back(hidden[...], gain, g_a2, sz.width)
    return gain_grad, grad + back


def shape(*dims, dtype=BF):
    return jax.ShapeDtypeStruct(dims, dtype)


def halves(sz, half, cols):
    return [shape(sz.n, half, cols)] + [shape(sz.n // 2, half, cols)] * 2


def first_attention(sz, order, pieces, x, rope, bias):
    t, wide = sz.t, sz.wide

    def body(order_ref, p0, p1, p2, p3, x_hbm, cos, sin, bias_hbm,
             hidden_hbm, a1_hbm, heads_hbm, lse, mixp_hbm, gains,
             x, hidden, a1, heads, mixp, wo, wqkv, mix, bias_ref, sem, out_sem):
        io = Copies(out_sem)
        first = start(fetches(order_ref, (p0, p1, p2, p3), [(wqkv, sz.wide)], sem, 0))
        loads = [io.start(x_hbm, x), io.start(bias_hbm, bias_ref)]
        loads += start(fetches(order_ref, (p0, p1, p2, p3), [(wo, 0)], sem, 2 * sz.n))
        wait(first)
        rows = []
        for k in range(2):
            parts = []
            for j in range(sz.n):
                lo = sz.padded * (j + 1) - 16
                tile = wqkv[lo : lo + 16, 0:128].astype(F32)
                at = sz.real + k - (sz.padded - 16)
                parts.append(tile[at : at + 1, : sz.padded])
            rows.append(jnp.concatenate(parts, axis=1))
        gains[...] = jnp.concatenate(rows + [jnp.zeros((6, sz.wide), F32)], axis=0)
        wait(loads)
        hidden[...] = x[...].astype(F32)

        def done(stage):
            for a, b in (((a1, a1_hbm), (heads, heads_hbm)), ((mixp, mixp_hbm),))[stage]:
                io.store(a, b)

        hidden[...] = attention_forward(
            sz, hidden[...], gains[0:1, :], wqkv, wo, cos, sin, bias_ref, a1, heads, lse, mixp, mix, done
        )
        io.store(hidden, hidden_hbm)
        io.close()

    v = pltpu.VMEM
    return call(
        body,
        [order, *pieces, x, *rope, bias],
        [
            shape(t, wide, dtype=F32), shape(t, wide), shape(sz.feat, t), shape(sz.lse, t, dtype=F32),
            shape(wide, t), shape(8, wide, dtype=F32),
        ],
        [
            v((t, wide), BF), v((t, wide), F32), v((t, wide), BF), v((sz.feat, t), BF), v((wide, t), BF),
            v((wide, wide), BF), v((wide, sz.feat), BF), v((sz.width + 16, t), F32), v((t, t), F32),
            pltpu.SemaphoreType.DMA((4 * sz.n,)), pltpu.SemaphoreType.DMA((8,)),
        ],
        6 * t * wide * sz.feat, 40,
        specs=[SMEM] + [ANY] * 5 + [VM] * 2 + [ANY],
        out_specs=[ANY] * 3 + [VM, ANY, VM],
    )


def first_gate(sz, order, pieces, hidden, gains):
    t, wide, ff = sz.t, sz.wide, sz.ff

    def body(order_ref, p0, p1, p2, p3, hidden_hbm, gains_ref, a2_hbm, gate_hbm, hidden_ref, a2, gate, w, sem, out_sem):
        out = Copies(out_sem)
        load = out.start(hidden_hbm, hidden_ref)
        copies = start(fetches(order_ref, (p0, p1, p2, p3), [(w, 0)], sem, 0))
        wait([load])
        hidden = hidden_ref[...]
        a2[...] = (hidden * inverse_rms(hidden, sz.width) * gains_ref[1:2, :]).astype(BF)
        wait(copies)
        out.store(a2, a2_hbm)
        for c in range(0, ff, sz.tile):
            cols = slice(c, c + sz.tile)
            gate[:, cols] = nn(a2[...], w[:, cols]).astype(BF)
            out.store(gate.at[:, pl.ds(c, sz.tile)], gate_hbm.at[:, pl.ds(c, sz.tile)])
        out.close()

    return call(
        body,
        [order, *pieces, hidden, gains],
        [shape(t, wide), shape(t, ff)],
        [pltpu.VMEM((t, wide), F32), pltpu.VMEM((t, wide), BF), pltpu.VMEM((t, ff), BF), pltpu.VMEM((wide, ff), BF),
         pltpu.SemaphoreType.DMA((2 * sz.n,)), pltpu.SemaphoreType.DMA((2 + ff // sz.tile,))],
        2 * t * wide * ff, 40,
        specs=[SMEM] + [ANY] * 5 + [VM], out_specs=[ANY] * 2,
    )


def first_up(sz, order, pieces, a2, gate):
    t, wide, ff = sz.t, sz.wide, sz.ff

    def body(order_ref, p0, p1, p2, p3, a2_hbm, gate_hbm, up_hbm, inner_hbm, a2, gate, up, inner, w, sem, out_sem):
        out = Copies(out_sem)
        loads = [out.start(a2_hbm, a2), out.start(gate_hbm, gate)]
        wait(start(fetches(order_ref, (p0, p1, p2, p3), [(w, 0)], sem, 0)))
        wait(loads)
        for c in range(0, ff, sz.tile):
            cols, part = slice(c, c + sz.tile), pl.ds(c, sz.tile)
            value = nn(a2[...], w[:, cols])
            up[:, cols] = value.astype(BF)
            z = gate[:, cols].astype(F32)
            inner[:, cols] = (z * jax.nn.sigmoid(z) * value).astype(BF)
            out.store(inner.at[:, part], inner_hbm.at[:, part])
            out.store(up.at[:, part], up_hbm.at[:, part])
        out.close()

    return call(
        body,
        [order, *pieces, a2, gate],
        [shape(t, ff), shape(t, ff)],
        [pltpu.VMEM((t, wide), BF)] + [pltpu.VMEM((t, ff), BF)] * 3 + [pltpu.VMEM((wide, ff), BF),
         pltpu.SemaphoreType.DMA((2 * sz.n,)), pltpu.SemaphoreType.DMA((2 + 2 * (ff // sz.tile),))],
        2 * t * wide * ff, 40,
        specs=[SMEM] + [ANY] * 6, out_specs=[ANY] * 2,
    )


def middle(sz, order, back, down_pieces, attn_pieces, gate_pieces, up_pieces, hidden1, inner1, gate1, up1, a2_1, gains, rope, bias,
           out_grad, half, down_half):
    aligned = isinstance(down_pieces, tuple)
    downs = list(down_pieces) if aligned else [down_pieces]
    t, wide, ff = sz.t, sz.wide, sz.ff

    def body(*refs):
        order_ref, back_ref, refs = refs[0], refs[1], refs[2:]
        down_refs, refs = refs[: len(downs)], refs[len(downs) :]
        attn_refs, gate_refs, up_refs, refs = refs[:4], refs[4:8], refs[8:12], refs[12:]
        (hidden1_hbm, inner1_hbm, gate1_hbm, up1_hbm, a2_1_hbm, gains_ref, cos, sin, bias_hbm, cl_hbm,
         second_hbm, wqkv_hbm, wo_hbm, a1_hbm, mixp_hbm, a2_hbm, gu_hbm, gl_hbm, g_qkv_hbm, gh1_hbm, gl1_hbm, gu1_hbm,
         gain_grads, *refs) = refs
        down_out, gate_out, refs = refs[:3], refs[3:6], refs[6:]
        (wd, wqkv, wo, wg, wu, inners, cls, x2, hidden, a1, heads, lse, mixp, a2s, gate, up, ggs, gu, gl, g_qkv,
         bias_ref, mix, g_heads, gs, probs, sem, piece_sem) = refs
        io = Copies(sem)
        if aligned:
            first = start(fetches(order_ref, down_refs, [(wd, 0)], piece_sem, 0))
        else:
            first = [io.start(down_refs[0], wd)]
        run1, run2 = pl.ds(0, t), pl.ds(t, t)
        inner1, inner2 = inners.at[run1, :], inners.at[run2, :]
        cl1, cl2 = cls.at[run1, :], cls.at[run2, :]
        a2, gg1, gg2 = a2s.at[run2, :], ggs.at[run1, :], ggs.at[run2, :]
        first += [io.start(inner1_hbm, inner1), io.start(hidden1_hbm, x2)]
        wait(first)
        loads = start(fetches(order_ref, attn_refs, [(wqkv, wide)], piece_sem, 2 * sz.n))
        loads += start(fetches(order_ref, attn_refs, [(wo, 0)], piece_sem, 4 * sz.n))
        loads += [io.start(bias_hbm, bias_ref)]
        x2[...] = x2[...] + nn(inner1[...], wd[...])
        wait(loads)
        sides = start(fetches(order_ref, gate_refs, [(wg, 0)], piece_sem, 6 * sz.n))
        sides += start(fetches(order_ref, up_refs, [(wu, 0)], piece_sem, 8 * sz.n))
        sides += [io.start(cl_hbm, cl2)]
        hidden[...] = attention_forward(
            sz, x2[...], gains_ref[0:1, :], wqkv, wo, cos, sin, bias_ref, a1, heads, lse, mixp, mix
        )
        wait(sides)
        for a, b in ((a1, a1_hbm), (mixp, mixp_hbm), (wqkv, wqkv_hbm), (wo, wo_hbm)):
            io.store(a, b)
        ffn_up(sz, hidden[...], gains_ref[1:2, :], a2, wg, wu, gate, up, inner2)
        io.store(a2, a2_hbm)
        gl[...] = (hidden[...] + nn(inner2[...], wd[...])).astype(BF)
        out = io.start(gl, second_hbm)
        gain_f, gh = ffn_backward(
            sz, cl2[...].astype(F32), cl2, hidden[...], gains_ref[1:2, :], wg, wu, wd, gate, up, gg2, gu
        )
        gus_out = io.start(gu, gu_hbm)
        loads = [io.start(gate1_hbm, gate), io.start(up1_hbm, up), io.start(a2_1_hbm, a2s.at[run1, :])]
        hidden[...] = gh
        wait([out])
        gl[...] = gh.astype(BF)
        out = io.start(gl, gl_hbm)
        gain_a, g_x = attention_backward(
            sz, hidden, gl[...], x2, gains_ref[0:1, :], wqkv, wo, cos, sin, bias_ref, heads, lse,
            mix, g_heads, gs, probs, g_qkv
        )
        io.store(g_qkv, g_qkv_hbm)
        hidden[...] = g_x
        loads.append(io.start(hidden1_hbm, x2))
        cl1[...] = g_x.astype(BF)
        wait(loads + [out, gus_out])
        gain_f1, gh = ffn_backward(
            sz, hidden[...], cl1, x2, gains_ref[1:2, :], wg, wu, wd, gate, up, gg1, gu
        )
        io.store(gu, gu1_hbm)
        hidden[...] = gh
        gl[...] = gh.astype(BF)
        io.store(hidden, gh1_hbm)
        io.store(gl, gl1_hbm)
        gain_grads[...] = jnp.concatenate([gain_a, gain_f + gain_f1, jnp.zeros((6, wide), F32)], axis=0)
        nz = sz.n // 4
        tile = ff // nz
        for k in range(nz):
            if aligned:
                rows = inners[:, pl.ds(pl.multiple_of(back_ref[k] * tile, tile), tile)]
                wd[k * tile : (k + 1) * tile, :] = tn(rows, cls[...]).astype(BF)
                io.blocks(back_ref, nz, k, wd, k * tile, down_half, down_out[0], down_out[1:])
        if not aligned:
            wd[...] = tn(inners[...], cls[...]).astype(BF)
            io.store(wd, down_out[0])
        tile = wide // nz
        for k in range(nz):
            rows = a2s[:, pl.ds(pl.multiple_of(back_ref[k] * tile, tile), tile)]
            wg[k * tile : (k + 1) * tile, :] = tn(rows, ggs[...]).astype(BF)
            io.blocks(back_ref, nz, k, wg, k * tile, half, gate_out[0], gate_out[1:])
        io.close()

    ins = [order, back, *downs, *attn_pieces, *gate_pieces, *up_pieces, hidden1, inner1, gate1, up1, a2_1, gains, *rope, bias,
           out_grad]
    specs = [SMEM] * 2 + [ANY] * (len(downs) + 17) + [VM] * 3 + [ANY] * 2
    places = halves(sz, down_half, wide) if aligned else [shape(ff, wide)] + [shape(8, 128)] * 2
    outs = [
        shape(t, wide), shape(wide, sz.feat), shape(wide, wide), shape(t, wide), shape(wide, t), shape(t, wide), shape(t, ff),
        shape(t, wide), shape(sz.feat, t), shape(t, wide, dtype=F32), shape(t, wide), shape(t, ff),
        shape(8, wide, dtype=F32), *places, *halves(sz, half, ff),
    ]
    out_specs = [ANY] * 12 + [VM] + [ANY] * 6
    v = pltpu.VMEM
    scratch = [
        v((ff, wide), BF), v((wide, sz.feat), BF), v((wide, wide), BF), v((wide, ff), BF), v((wide, ff), BF),
        v((2 * t, ff), BF), v((2 * t, wide), BF), v((t, wide), F32), v((t, wide), F32), v((t, wide), BF), v((sz.feat, t), BF),
        v((sz.lse, t), F32), v((wide, t), BF), v((2 * t, wide), BF), v((t, ff), BF), v((t, ff), BF), v((2 * t, ff), BF),
        v((t, ff), BF), v((t, wide), BF), v((sz.feat, t), BF), v((t, t), F32), v((sz.width + 16, t), F32),
        v((sz.feat, t), F32), v((sz.group, t, t), BF), v((sz.group, t, t), BF),
        pltpu.SemaphoreType.DMA((4 * sz.n + 40,)), pltpu.SemaphoreType.DMA((10 * sz.n,)),
    ]
    return call(body, ins, outs, scratch, 24 * t * wide * ff, 60, specs, out_specs)


def up_out_grad(sz, back, a2s, grads, mixps, gls, half):
    t, wide, ff = sz.t, sz.wide, sz.ff
    cols = ff + wide

    def body(back_ref, a_1, a_2, g_1, g_2, m1, m2, l1, l2, own, s0, s1, a, g, mixp, gl, out, sem):
        io = Copies(sem)
        run1, run2 = pl.ds(0, t), pl.ds(t, t)
        wait([
            io.start(m1, mixp.at[:, run1]), io.start(m2, mixp.at[:, run2]),
            io.start(l1, gl.at[run1, :]), io.start(l2, gl.at[run2, :]),
        ])
        later = [
            io.start(a_1, a.at[run1, :]), io.start(a_2, a.at[run2, :]),
            io.start(g_1, g.at[run1, :]), io.start(g_2, g.at[run2, :]),
        ]
        nz = sz.n // 4
        tile = wide // nz
        starts = [pl.multiple_of(back_ref[k] * tile, tile) for k in range(nz)]
        for k in range(nz):
            out[k * tile : (k + 1) * tile, ff:cols] = nn(mixp[pl.ds(starts[k], tile), :], gl[...]).astype(BF)
        wait(later)
        for k in range(nz):
            out[k * tile : (k + 1) * tile, 0:ff] = tn(a[:, pl.ds(starts[k], tile)], g[...]).astype(BF)
            io.blocks(back_ref, nz, k, out, k * tile, half, own, (s0, s1))
        io.close()

    v = pltpu.VMEM
    return call(
        body, [back, *a2s, *grads, *mixps, *gls], halves(sz, half, cols),
        [
            v((2 * t, wide), BF), v((2 * t, ff), BF), v((wide, 2 * t), BF), v((2 * t, wide), BF), v((wide, cols), BF),
            pltpu.SemaphoreType.DMA((2 * sz.n + 8,)),
        ],
        4 * t * wide * cols, 48,
        specs=[SMEM] + [ANY] * 8, out_specs=[ANY] * 3,
    )


def settle(*arrays):
    def body(*refs):
        for a, b in zip(refs[: len(arrays)], refs[len(arrays) :]):
            b[...] = a[...]

    return call(body, list(arrays), [shape(*a.shape, dtype=a.dtype) for a in arrays], [], 0, 20)


def last_attention(sz, gh, gl, x, gains, wqkv, wo, rope, bias, heads, lse):
    t, wide = sz.t, sz.wide

    def body(gh_hbm, gl_hbm, x_hbm, gains_ref, wqkv_hbm, wo_hbm, cos, sin, bias_hbm, heads_hbm, lse_ref,
             g_x_hbm, g_qkv_hbm, gain_grad,
             gh, gl, x_low, x, wqkv, wo, bias_ref, heads, g_qkv, mix, g_heads, gs, probs, sem):
        io = Copies(sem)
        first = [io.start(gl_hbm, gl), io.start(wo_hbm, wo)]
        second = [io.start(heads_hbm, heads), io.start(bias_hbm, bias_ref)]
        wait(first)
        later = []

        def ready(last):
            if last:
                wait(later)
                x[...] = x_low[...].astype(F32)
            else:
                wait(second)
                later.extend([io.start(wqkv_hbm, wqkv), io.start(gh_hbm, gh), io.start(x_hbm, x_low)])

        gain_a, back_x = attention_backward(
            sz, gh, gl[...], x, gains_ref[0:1, :], wqkv, wo, cos, sin, bias_ref,
            heads, lse_ref, mix, g_heads, gs, probs, g_qkv, ready
        )
        io.store(g_qkv, g_qkv_hbm)
        gl[...] = back_x.astype(BF)
        io.store(gl, g_x_hbm)
        gain_grad[...] = jnp.concatenate([gain_a, jnp.zeros((7, wide), F32)], axis=0)
        io.close()

    v = pltpu.VMEM
    return call(
        body,
        [gh, gl, x, gains, wqkv, wo, *rope, bias, heads, lse],
        [shape(t, wide), shape(sz.feat, t), shape(8, wide, dtype=F32)],
        [
            v((t, wide), F32), v((t, wide), BF), v((t, wide), BF), v((t, wide), F32), v((wide, sz.feat), BF),
            v((wide, wide), BF), v((t, t), F32), v((sz.feat, t), BF), v((sz.feat, t), BF), v((sz.width + 16, t), F32),
            v((sz.feat, t), F32), v((sz.group, t, t), BF), v((sz.group, t, t), BF), pltpu.SemaphoreType.DMA((16,)),
        ],
        10 * t * wide * sz.feat, 40,
        specs=[ANY] * 3 + [VM] + [ANY] * 2 + [VM] * 2 + [ANY] * 2 + [VM],
        out_specs=[ANY] * 2 + [VM],
    )


def qkv_grad(sz, back, a1s, g_qkv_runs, gain2, gain_a1, half):
    t, wide, cols = sz.t, sz.wide, sz.feat

    def body(back_ref, a_1, a_2, g1, g2, gain2_ref, gain_a_ref, own, s0, s1, a1, g_qkv, out, sem):
        io = Copies(sem)
        run1, run2 = pl.ds(0, t), pl.ds(t, t)
        wait([
            io.start(a_1, a1.at[run1, :]), io.start(a_2, a1.at[run2, :]),
            io.start(g1, g_qkv.at[:, run1]), io.start(g2, g_qkv.at[:, run2]),
        ])
        nz = sz.n // 4
        tile = wide // nz
        row = lax.broadcasted_iota(jnp.int32, (sz.padded, sz.padded), 0)
        for k in range(nz):
            here = pl.ds(pl.multiple_of(back_ref[k] * tile, tile), tile)
            into = tt(a1[:, here], g_qkv[...])
            attn_gain = gain_a_ref[0:1, here] + gain2_ref[0:1, here]
            ffn_gain = gain2_ref[1:2, here]
            patches = []
            for s in range(0, tile, sz.padded):
                a, f = attn_gain[:, s : s + sz.padded], ffn_gain[:, s : s + sz.padded]
                patches.append(jnp.where(row == sz.real, a, jnp.where(row == sz.real + 1, f, 0.0)))
            patch = jnp.concatenate([join(patches, 0), jnp.zeros((tile, 128 - sz.padded), F32)], axis=1)
            lo = k * tile
            out[lo : lo + tile, 0:128] = (into[:, :128] + patch).astype(BF)
            out[lo : lo + tile, 128:cols] = into[:, 128:].astype(BF)
            io.blocks(back_ref, nz, k, out, lo, half, own, (s0, s1))
        io.close()

    v = pltpu.VMEM
    return call(
        body,
        [back, *a1s, *g_qkv_runs, gain2, gain_a1],
        halves(sz, half, cols),
        [v((2 * t, wide), BF), v((cols, 2 * t), BF), v((wide, cols), BF), pltpu.SemaphoreType.DMA((2 * sz.n + 8,))],
        4 * t * wide * cols, 40,
        specs=[SMEM] + [ANY] * 4 + [VM] * 2, out_specs=[ANY] * 3,
    )


def spread(v, n, real, padded):
    lead = v.shape[:-1]
    v = v.reshape(lead + (n, real))
    v = jnp.pad(v, [(0, 0)] * len(lead) + [(0, 0), (0, padded - real)])
    return v.reshape(lead + (n * padded,))


def narrow(v, n, real, padded):
    lead = v.shape[:-1]
    return v.reshape(lead + (n, padded))[..., :real].reshape(lead + (n * real,))


def place_blocks(order, pieces):
    both = jnp.concatenate(pieces)
    spots = jnp.zeros(order.shape, jnp.int32).at[order].set(jnp.arange(order.shape[0], dtype=jnp.int32))
    return jnp.take(both, spots, axis=0).reshape(-1, both.shape[2])


def order_blocks(order, grad, half, nz):
    blocks = grad.reshape(nz, 8, half, grad.shape[1])
    at_z = jnp.take(blocks, order[:nz], axis=0)
    parts = [jnp.take(at_z, order[nz + k], axis=1) for k in range(8)]
    return jnp.concatenate(parts[:4]), jnp.concatenate(parts[4:6]), jnp.concatenate(parts[6:])


def shards(mesh, tokens, lengths, w_query, key_weight, value_weight, output_weight, w_gate, w_up, w_down, gain_attn, gain_ffn, out_grad):
    at = Place(mesh)
    n = at.n
    real, width = w_query.shape
    padded = -(-(real + 2) // 16) * 16
    sz = Sizes(n, real, padded, w_gate.shape[1], tokens.shape[0], key_weight.shape[1])
    wide, ff = sz.wide, sz.ff
    half, down_half = padded // 2, w_down.shape[0] // 2
    aligned = down_half % 16 == 0
    order = Order()
    places, back = at.piece_order(), at.grad_order()

    def pad_rows(v):
        return jnp.pad(v, ((0, padded - v.shape[0]), (0, 0)))

    def attention_shard(w_query, key_weight, value_weight, output_weight, gain_attn, gain_ffn):
        qkv = jnp.concatenate([w_query, key_weight, value_weight], axis=1)
        gains = jnp.pad(jnp.stack([gain_attn, gain_ffn]), ((0, 0), (0, qkv.shape[1] - real)))
        qkv = pad_rows(jnp.concatenate([qkv, gains]))
        return jnp.concatenate([pad_rows(spread(output_weight, n, real, padded)), qkv], axis=1)

    def tables(lengths, tokens, out_grad):
        positions, allowed = layout(lengths, tokens.shape[0])
        bias = jnp.where(allowed[0], 0.0, -1e30).astype(F32).T
        return rotation(positions[0]), bias, spread(tokens, n, real, padded), spread(out_grad, n, real, padded)

    ga, gg, gu, gd = (Gather(at, order) for _ in range(4))
    ga.start(attention_shard, w_query, key_weight, value_weight, output_weight, gain_attn, gain_ffn)
    ga.ready()
    ga.along_z()
    gg.start(pad_rows, w_gate)
    gu.start(pad_rows, w_up)
    gd.start(lambda v: spread(v, n, real, padded), w_down)
    gg.ready()
    gu.ready()
    gd.ready()
    rope, bias, x1, cot = order.do(tables, lengths, tokens, out_grad)
    ga.come()
    ga.line_up()
    ga.first()
    gg.along_z()
    ga.got_first()
    ga.second()
    gg.come()
    gg.line_up()
    gg.first()
    gu.along_z()
    x1, cot = order.do(settle, x1, cot)
    ga.got_second()
    gg.got_first()
    gu.come()
    ga.cores()
    gg.second()
    gu.line_up()
    gu.first()
    attn_pieces = ga.pieces()
    gd.along_z()
    hidden1, a1_1, heads1, lse1, mixp1, gains = order.do(
        lambda *v: first_attention(sz, *v), places, attn_pieces, x1, rope, bias
    )
    gd.come()
    gg.got_second()
    gg.cores()
    gu.got_first()
    gu.second()
    gd.line_up()
    gd.first()
    gate_pieces = gg.pieces()
    a2_1, gate1 = order.do(lambda *v: first_gate(sz, *v), places, gate_pieces, hidden1, gains)
    gd.got_first()
    gd.second()
    gu.got_second()
    gu.cores()
    up_pieces = gu.pieces()
    gd.cores(gd.both)
    up1, inner1 = order.do(lambda *v: first_up(sz, *v), places, up_pieces, a2_1, gate1)
    gd.got_second()
    gd.cores(gd.third)
    down_pieces = gd.pieces()
    if not aligned:
        down_pieces = place_blocks(places, down_pieces)

    (second, wqkv, wo, a1_2, mixp2, a2_2, gu2, gl2, g_qkv2, gh1, gl1, gu1, gain2, *grads) = order.do(
        lambda *v: middle(sz, *v, half, down_half),
        places, back, down_pieces, attn_pieces, gate_pieces, up_pieces, hidden1, inner1, gate1, up1, a2_1, gains, rope, bias, cot,
    )
    downs, gates = grads[:3], grads[3:]
    if not aligned:
        downs = order_blocks(back, downs[0], down_half, at.nz)
    sd = Scatter(at, order, *downs)
    sg = Scatter(at, order, *gates)
    sd.core(0)
    sg.core(0)
    sd.core(1)
    sg.core(1)
    sd.come_core(0)
    sd.first()
    sg.come_core(0)
    sg.first()
    sd.come_core(1)
    sg.come_core(1)
    own, *send = order.do(
        lambda *v: up_out_grad(sz, *v, half), back, (a2_1, a2_2), (gu1, gu2), (mixp1, mixp2), (gl1, gl2)
    )
    sd.come()
    su = Scatter(at, order, own, *send)
    su.core(0)
    su.core(1)
    sd.second()
    su.come_core(0)
    su.first()
    su.come_core(1)
    g_x, g_qkv1, gain_a1 = order.do(
        lambda *v: last_attention(sz, *v), gh1, gl1, x1, gains, wqkv, wo, rope, bias, heads1, lse1
    )
    sg.come()
    sd.come()
    sg.second()
    sd.along_z()
    own, *send = order.do(
        lambda *v: qkv_grad(sz, *v, half), back, (a1_1, a1_2), (g_qkv1, g_qkv2), gain2, gain_a1
    )
    sg.come()
    su.come()
    su.second()
    sd.come_z()
    sg.along_z()
    sa = Scatter(at, order, own, *send)
    sa.core(0)
    sa.core(1)
    sa.come_core(0)
    sa.first()
    sa.come_core(1)
    su.come()
    sg.come_z()
    su.along_z()
    sa.come()
    sa.second()
    sd.along_x()
    sg.along_x()
    second, g_x = order.do(settle, second, g_x)
    su.come_z()
    sa.come()
    sa.along_z()
    su.along_x()
    sd.come()
    sd.cores()
    sa.come_z()
    sa.along_x()
    sg.come()
    sg.cores()
    su.come()
    su.cores()
    sd.come()
    sg.come()
    su.come()
    r_up = su.result()
    r_gate = sg.result()
    r_down = sd.result()
    second, g_x = narrow(second, n, real, padded), narrow(g_x, n, real, padded)
    sa.come()
    sa.cores()
    sa.come()
    r_in = sa.result()
    kv = key_weight.shape[1]
    return (
        second,
        g_x,
        r_in[:real, :width],
        r_in[:real, width : width + kv],
        r_in[:real, width + kv :],
        narrow(r_up[:real, ff:], n, real, padded),
        r_gate[:real],
        r_up[:real, :ff],
        narrow(r_down, n, real, padded),
        r_in[real, :real],
        r_in[real + 1, :real],
    )


def solution(mesh):
    rows, split, gain = P(("dp", "fsdp"), None), P("fsdp", None), P("fsdp")
    return jax.shard_map(
        functools.partial(shards, mesh),
        mesh=mesh,
        in_specs=(rows, rows) + (split,) * 7 + (gain, gain, rows),
        out_specs=(rows, rows) + (split,) * 7 + (gain, gain),
        check_vma=False,
    )
```

time: 391 us -> 360 us (0.921)
  starting transfers between devices: 66.8 us -> 56.1 us
  other arithmetic: 40 us -> 33.7 us
  waiting for transfers between devices: 102 us -> 96.2 us
  Pallas kernels: 133 us -> 128 us
    ppermute x24, waiting for transfers between devices: 39.1 us -> 26.1 us  [shift_z(): lax.ppermute(v, 'fsdp', [(i, (i + 4 * k) % self.n) for i in range(self.n)])]
    ppermute x16, waiting for transfers between devices: 44 us -> 51.1 us  [cross(): return lax.ppermute(v, ('dp', 'fsdp'), pairs)]
    ppermute x24, starting transfers between devices: 10.7 us -> 5.45 us  [swap_core(): return lax.ppermute(v, 'fsdp', [(i, i ^ 1) for i in range(self.n)])]
    pallas_call x8 -> x9, Pallas kernels: 133 us -> 128 us  [call(): pl.pallas_call(body, in_specs=specs or [VM] * len(ins), out_specs=out_spe...]
    unnamed x86, local copies, waits for them, and re-layouts: 15.4 us -> 10.2 us
    ppermute x24, starting transfers between devices: 35.1 us -> 30.6 us  [shift_z(): lax.ppermute(v, 'fsdp', [(i, (i + 4 * k) % self.n) for i in range(self.n)])]
  transfers between devices with their start and end apart: 68 -> 68, of which waited for: 23 -> 26; matrix products, arithmetic and copies ran while one was open for 17% -> 16% of each run, Pallas kernels for 23% -> 19%
where the time goes in v3:
time: 360 us; the launch traced here: 354 us
  Pallas kernels  128 us (36%)
  waiting for transfers between devices  96.2 us (27%)
  starting transfers between devices  56.1 us (16%)
  local copies, waits for them, and re-layouts  37.8 us (10%)
  other arithmetic  33.7 us (9%)
    pallas_call x9, Pallas kernels, call(): pl.pallas_call(body, in_specs=specs or [VM] * len(ins), out_specs=out_spe...  128 us
    ppermute x16, waiting for transfers between devices, cross(): return lax.ppermute(v, ('dp', 'fsdp'), pairs)  51.1 us
    ppermute x24, starting transfers between devices, shift_z(): lax.ppermute(v, 'fsdp', [(i, (i + 4 * k) % self.n) for i in range(self.n)])  30.6 us
    convert_element_type x16, other arithmetic, step(): return add(*[a[lo:hi] for a, (lo, hi) in zip(v, cuts)]).astype(BF)  26.4 us
    ppermute x24, waiting for transfers between devices, shift_z(): lax.ppermute(v, 'fsdp', [(i, (i + 4 * k) % self.n) for i in range(self.n)])  26.1 us
    ppermute x16, starting transfers between devices, cross(): return lax.ppermute(v, ('dp', 'fsdp'), pairs)  16.4 us
    ppermute x24, waiting for transfers between devices, swap_core(): return lax.ppermute(v, 'fsdp', [(i, i ^ 1) for i in range(self.n)])  15.4 us
    unnamed x86, local copies, waits for them, and re-layouts  10.2 us
  transfers between devices with their start and end apart: 68, of which 26 were waited for; matrix products, arithmetic and copies ran while one was open for 16% of the time, Pallas kernels for 19%

profile of v3, /device:TPU:0, one launch (start us, length us, event | category | flops | bytes accessed | tf_op | source)
XLA Modules:
  0.0 353.9 jit_solution(15455435843315365203)
XLA Ops:
  4.9 5.0 %collective-permute-start.6 = (bf16[1,32,2624]{2,1,0:T(8,128)(2,1)S(1)}, bf16[1,32,2624]{2,1,0:T(8,128)(2,1)S(1)}, u32[]{:S(2)}, u32[]{:S(2)}) collective-permute-start(bf16[1,32,2624]{2,1,0:T(8,128)(2,1)S(1)} %select_bitcast_fusion), channel_id=1, source_target_pairs={{0,12},{1,13},{2,14},{3,15},{4,0},{5,1},{6,2},{7,3},{8,4},{9,5},{1... | collective-permute-start | bytes 503816 | tf_op jit(solution)/shard_map/ppermute | solution.py:57
  17.6 7.3 %collective-permute-done.5 = bf16[1,32,2624]{2,1,0:T(8,128)(2,1)S(1)} collective-permute-done((bf16[1,32,2624]{2,1,0:T(8,128)(2,1)S(1)}, bf16[1,32,2624]{2,1,0:T(8,128)(2,1)S(1)}, u32[]{:S(2)}, u32[]{:S(2)}) %collective-permute-start.5) | collective-permute-done | bytes 167968 | tf_op jit(solution)/shard_map/ppermute | solution.py:57
  31.3 4.6 %collective-permute-done.7 = bf16[4,32,2624]{2,1,0:T(8,128)(2,1)S(1)} collective-permute-done((bf16[4,32,2624]{2,1,0:T(8,128)(2,1)S(1)}, bf16[4,32,2624]{2,1,0:T(8,128)(2,1)S(1)}, u32[]{:S(2)}, u32[]{:S(2)}) %collective-permute-start.7) | collective-permute-done | bytes 671776 | tf_op jit(solution)/shard_map/ppermute | solution.py:69
  37.6 5.5 %collective-permute-done.9 = bf16[1,32,2560]{2,1,0:T(8,128)(2,1)S(1)} collective-permute-done((bf16[1,32,2560]{2,1,0:T(8,128)(2,1)S(1)}, bf16[1,32,2560]{2,1,0:T(8,128)(2,1)S(1)}, u32[]{:S(2)}, u32[]{:S(2)}) %collective-permute-start.9) | collective-permute-done | bytes 163872 | tf_op jit(solution)/shard_map/ppermute | solution.py:57
  78.2 13.6 %shard_map.204 = (f32[384,1024]{1,0:T(8,128)}, bf16[384,1024]{1,0:T(8,128)(2,1)}, bf16[1600,384]{1,0:T(8,128)(2,1)}, f32[16,384]{1,0:T(8,128)}, bf16[1024,384]{1,0:T(8,128)(2,1)}, /*index=5*/f32[8,1024]{1,0:T(8,128)}) custom-call(s32[32]{0:T(128)} %stack.179.order_ref.refs_0_, bf16[8,32,2624]{2,1,0:T(8,128)(2,1)} %copy-done, ...), custom_call_target="tpu_custom_call" | custom-call | flops 1000 | bytes 1000 | tf_op jit(solution)/shard_map/pallas_call | solution.py:264
  98.2 7.5 %shard_map.205 = (bf16[384,1024]{1,0:T(8,128)(2,1)}, bf16[384,2560]{1,0:T(8,128)(2,1)}) custom-call(s32[32]{0:T(128)} %stack.179.order_ref.refs_0_, bf16[8,32,2560]{2,1,0:T(8,128)(2,1)} %copy-done.2, bf16[8,32,2560]{2,1,0:T(8,128)(2,1)} %collective-permute-done.22.p1.refs_11_, bf16[8,32,2560]{2,1,0:T(8,128)(2,1)} %copy-done.4, ...), custom_call_target="tpu_custom_call" | custom-call | flops 1000 | bytes 1000 | tf_op jit(solution)/shard_map/pallas_call | solution.py:264
  105.7 6.5 %collective-permute-done.23 = bf16[4,80,1024]{2,1,0:T(8,128)(2,1)} collective-permute-done((bf16[4,80,1024]{2,1,0:T(8,128)(2,1)S(1)}, bf16[4,80,1024]{2,1,0:T(8,128)(2,1)}, u32[]{:S(2)}, u32[]{:S(2)}) %collective-permute-start.23) | collective-permute-done | bytes 655392 | tf_op jit(solution)/shard_map/ppermute | solution.py:69
  114.5 3.6 %collective-permute-done.27.p1.refs_15_ = bf16[8,32,2560]{2,1,0:T(8,128)(2,1)} collective-permute-done((bf16[8,32,2560]{2,1,0:T(8,128)(2,1)S(1)}, bf16[8,32,2560]{2,1,0:T(8,128)(2,1)}, u32[]{:S(2)}, u32[]{:S(2)}) %collective-permute-start.27) | collective-permute-done | bytes 1310752 | tf_op jit(solution)/shard_map/ppermute | solution.py:69
  119.1 3.8 %collective-permute-done.28.p2.refs_16_ = bf16[8,32,2560]{2,1,0:T(8,128)(2,1)S(1)} collective-permute-done((bf16[8,32,2560]{2,1,0:T(8,128)(2,1)S(1)}, bf16[8,32,2560]{2,1,0:T(8,128)(2,1)S(1)}, u32[]{:S(2)}, u32[]{:S(2)}) %collective-permute-start.28) | collective-permute-done | bytes 1310752 | tf_op jit(solution)/shard_map/ppermute | solution.py:54
  124.0 7.7 %shard_map.206 = (bf16[384,2560]{1,0:T(8,128)(2,1)}, bf16[384,2560]{1,0:T(8,128)(2,1)}) custom-call(s32[32]{0:T(128)} %stack.179.order_ref.refs_0_, bf16[8,32,2560]{2,1,0:T(8,128)(2,1)} %copy-done.1, bf16[8,32,2560]{2,1,0:T(8,128)(2,1)} %collective-permute-done.27.p1.refs_15_, bf16[8,32,2560]{2,1,0:T(8,128)(2,1)} %copy-done.3, ...), custom_call_target="tpu_custom_call" | custom-call | flops 1000 | bytes 1000 | tf_op jit(solution)/shard_map/pallas_call | solution.py:264
  131.7 4.6 %collective-permute-done.26.refs_3_ = bf16[8,80,1024]{2,1,0:T(8,128)(2,1)} collective-permute-done((bf16[8,80,1024]{2,1,0:T(8,128)(2,1)S(1)}, bf16[8,80,1024]{2,1,0:T(8,128)(2,1)}, u32[]{:S(2)}, u32[]{:S(2)}) %collective-permute-start.26) | collective-permute-done | bytes 1310752 | tf_op jit(solution)/shard_map/ppermute | solution.py:69
  140.6 60.2 %shard_map.207 = (bf16[384,1024]{1,0:T(8,128)(2,1)}, bf16[1024,1600]{1,0:T(8,128)(2,1)}, bf16[1024,1024]{1,0:T(8,128)(2,1)}, bf16[384,1024]{1,0:T(8,128)(2,1)}, ...) custom-call(s32[32]{0:T(128)} %stack.179.order_ref.refs_0_, ...), custom_call_target="tpu_custom_call" | custom-call | flops 1000 | bytes 1000 | tf_op jit(solution)/shard_map/pallas_call | solution.py:264
  204.1 3.2 add_convert_fusion.2
  209.8 11.5 %shard_map.208 = (bf16[16,32,3584]{2,1,0:T(8,128)(2,1)}, bf16[8,32,3584]{2,1,0:T(8,128)(2,1)}, bf16[8,32,3584]{2,1,0:T(8,128)(2,1)}) custom-call(s32[12]{0:T(128)} %stack.192.refs_1_.back_ref, bf16[384,1024]{1,0:T(8,128)(2,1)} %get-tuple-element.511.a2_hbm.refs_22_.a_1, bf16[384,1024]{1,0:T(8,128)(2,1)} %get-tuple-element.512.a_2, ...), custom_call_target="tpu_custom_call" | custom-call | flops 1000 | bytes 1000 | tf_op jit(solution)/shard_map/pallas_call | solution.py:264
  221.2 4.0 %collective-permute-done.36 = bf16[8,80,1024]{2,1,0:T(8,128)(2,1)} collective-permute-done((bf16[8,80,1024]{2,1,0:T(8,128)(2,1)}, bf16[8,80,1024]{2,1,0:T(8,128)(2,1)}, u32[]{:S(2)}, u32[]{:S(2)}) %collective-permute-start.36) | collective-permute-done | bytes 1310752 | tf_op jit(solution)/shard_map/ppermute | solution.py:69
  231.8 3.2 add_convert_fusion
  235.6 15.1 %shard_map.209 = (bf16[384,1024]{1,0:T(8,128)(2,1)}, bf16[1600,384]{1,0:T(8,128)(2,1)}, f32[8,1024]{1,0:T(8,128)}) custom-call(f32[384,1024]{1,0:T(8,128)} %get-tuple-element.532.gh_hbm, bf16[384,1024]{1,0:T(8,128)(2,1)} %get-tuple-element.533.l1.gl_hbm, bf16[384,1024]{1,0:T(8,128)(2,1)} %get-tuple-element.534.x_hbm, ...), custom_call_target="tpu_custom_call" | custom-call | flops 1000 | bytes 1000 | tf_op jit(solution)/shard_map/pallas_call | solution.py:264
  260.1 7.3 %shard_map.210 = (bf16[16,32,1600]{2,1,0:T(8,128)(2,1)}, bf16[8,32,1600]{2,1,0:T(8,128)(2,1)}, bf16[8,32,1600]{2,1,0:T(8,128)(2,1)}) custom-call(s32[12]{0:T(128)} %stack.192.refs_1_.back_ref, bf16[384,1024]{1,0:T(8,128)(2,1)} %get-tuple-element.560.a_1, bf16[384,1024]{1,0:T(8,128)(2,1)} %get-tuple-element.561.a_2, bf16[1600,384]{1,0:T(8,128)(2,1)} %get-tuple-element.562.g1, ...), custom_call_target="tpu_custom_call" | custom-call | flops 1000 | bytes 1000 | tf_op jit(solution)/shard_map/pallas_call | solution.py:264
  267.4 3.5 collective-permute-done.41
  270.9 6.5 %collective-permute-done.45 = bf16[8,32,3584]{2,1,0:T(8,128)(2,1)} collective-permute-done((bf16[8,32,3584]{2,1,0:T(8,128)(2,1)}, bf16[8,32,3584]{2,1,0:T(8,128)(2,1)}, u32[]{:S(2)}, u32[]{:S(2)}) %collective-permute-start.45) | collective-permute-done | bytes 1835040 | tf_op jit(solution)/shard_map/ppermute | solution.py:69
  286.8 14.7 %collective-permute-done.49 = bf16[4,32,3584]{2,1,0:T(8,128)(2,1)S(1)} collective-permute-done((bf16[4,32,3584]{2,1,0:T(8,128)(2,1)S(1)}, bf16[4,32,3584]{2,1,0:T(8,128)(2,1)S(1)}, u32[]{:S(2)}, u32[]{:S(2)}) %collective-permute-start.49) | collective-permute-done | bytes 917536 | tf_op jit(solution)/shard_map/ppermute | solution.py:69
  317.9 6.6 %collective-permute-done.55 = bf16[1,32,3584]{2,1,0:T(8,128)(2,1)} collective-permute-done((bf16[1,32,3584]{2,1,0:T(8,128)(2,1)}, bf16[1,32,3584]{2,1,0:T(8,128)(2,1)}, u32[]{:S(2)}, u32[]{:S(2)}) %collective-permute-start.55) | collective-permute-done | bytes 229408 | tf_op jit(solution)/shard_map/ppermute | solution.py:57
  335.0 5.1 %collective-permute-done.58 = bf16[1,32,1600]{2,1,0:T(8,128)(2,1)S(1)} collective-permute-done((bf16[1,32,1600]{2,1,0:T(8,128)(2,1)S(1)}, bf16[1,32,1600]{2,1,0:T(8,128)(2,1)S(1)}, u32[]{:S(2)}, u32[]{:S(2)}) %collective-permute-start.58) | collective-permute-done | bytes 102432 | tf_op jit(solution)/shard_map/ppermute | solution.py:57
  341.4 3.6 %collective-permute-done.61 = bf16[32,1600]{1,0:T(8,128)(2,1)S(1)} collective-permute-done((bf16[32,1600]{1,0:T(8,128)(2,1)S(1)}, bf16[32,1600]{1,0:T(8,128)(2,1)S(1)}, u32[]{:S(2)}, u32[]{:S(2)}) %collective-permute-start.61) | collective-permute-done | bytes 102432 | tf_op jit(solution)/shard_map/ppermute | solution.py:60
  (299 shorter events, 137.6 us)
Async XLA Ops:
  36.1 25.5 %collective-permute-start.15 = (bf16[8,32,2624]{2,1,0:T(8,128)(2,1)S(1)}, bf16[8,32,2624]{2,1,0:T(8,128)(2,1)}, u32[]{:S(2)}, u32[]{:S(2)}) collective-permute-start(bf16[8,32,2624]{2,1,0:T(8,128)(2,1)S(1)} %constant_dynamic-update-slice_fusion.4.p0.refs_6_), channel_id=1, source_target_pairs={{0,16},{1,3},{2,18},{3,1},{4,20},{5,7},{6,22},{7,5},{8,24},{9,11},... | collective-permute-start | bytes 4030472 | tf_op jit(solution)/shard_map/ppermute | solution.py:69
  64.2 27.7 %collective-permute-start.22 = (bf16[8,32,2560]{2,1,0:T(8,128)(2,1)S(1)}, bf16[8,32,2560]{2,1,0:T(8,128)(2,1)}, u32[]{:S(2)}, u32[]{:S(2)}) collective-permute-start(bf16[8,32,2560]{2,1,0:T(8,128)(2,1)S(1)} %constant_dynamic-update-slice_fusion.10.p0.refs_10_), channel_id=1, source_target_pairs={{0,16},{1,3},{2,18},{3,1},{4,20},{5,7},{6,22},{7,5},{8,24},{9,11},... | collective-permute-start | bytes 3932168 | tf_op jit(solution)/shard_map/ppermute | solution.py:69
  69.4 22.5 %collective-permute-start.21 = (bf16[4,32,2560]{2,1,0:T(8,128)(2,1)S(1)}, bf16[4,32,2560]{2,1,0:T(8,128)(2,1)}, u32[]{:S(2)}, u32[]{:S(2)}) collective-permute-start(bf16[4,32,2560]{2,1,0:T(8,128)(2,1)S(1)} %constant_dynamic-update-slice_fusion.12), channel_id=1, source_target_pairs={{0,2},{1,17},{2,0},{3,19},{4,6},{5,21},{6,4},{7,23},{8,10},{9,25},... | collective-permute-start | bytes 1966088 | tf_op jit(solution)/shard_map/ppermute | solution.py:69
  72.0 19.8 %collective-permute-start.20 = (bf16[1,80,1024]{2,1,0:T(8,128)(2,1)S(1)}, bf16[1,80,1024]{2,1,0:T(8,128)(2,1)S(1)}, u32[]{:S(2)}, u32[]{:S(2)}) collective-permute-start(bf16[1,80,1024]{2,1,0:T(8,128)(2,1)S(1)} %select_bitcast_fusion.1), channel_id=1, source_target_pairs={{0,12},{1,13},{2,14},{3,15},{4,0},{5,1},{6,2},{7,3},{8,4},{9,5},{1... | collective-permute-start | bytes 491528 | tf_op jit(solution)/shard_map/ppermute | solution.py:57
  72.8 19.0 %collective-permute-start.19 = (bf16[1,80,1024]{2,1,0:T(8,128)(2,1)S(1)}, bf16[1,80,1024]{2,1,0:T(8,128)(2,1)S(1)}, u32[]{:S(2)}, u32[]{:S(2)}) collective-permute-start(bf16[1,80,1024]{2,1,0:T(8,128)(2,1)S(1)} %select_bitcast_fusion.1), channel_id=1, source_target_pairs={{0,8},{1,9},{2,10},{3,11},{4,12},{5,13},{6,14},{7,15},{8,0},{9,1},... | collective-permute-start | bytes 491528 | tf_op jit(solution)/shard_map/ppermute | solution.py:57
  93.6 24.4 %collective-permute-start.27 = (bf16[8,32,2560]{2,1,0:T(8,128)(2,1)S(1)}, bf16[8,32,2560]{2,1,0:T(8,128)(2,1)}, u32[]{:S(2)}, u32[]{:S(2)}) collective-permute-start(bf16[8,32,2560]{2,1,0:T(8,128)(2,1)S(1)} %constant_dynamic-update-slice_fusion.16.p0.refs_14_), channel_id=1, source_target_pairs={{0,16},{1,3},{2,18},{3,1},{4,20},{5,7},{6,22},{7,5},{8,24},{9,11},... | collective-permute-start | bytes 3932168 | tf_op jit(solution)/shard_map/ppermute | solution.py:69
  94.3 17.8 %collective-permute-start.23 = (bf16[4,80,1024]{2,1,0:T(8,128)(2,1)S(1)}, bf16[4,80,1024]{2,1,0:T(8,128)(2,1)}, u32[]{:S(2)}, u32[]{:S(2)}) collective-permute-start(bf16[4,80,1024]{2,1,0:T(8,128)(2,1)S(1)} %constant_dynamic-update-slice_fusion.18), channel_id=1, source_target_pairs={{0,2},{1,17},{2,0},{3,19},{4,6},{5,21},{6,4},{7,23},{8,10},{9,25},... | collective-permute-start | bytes 1966088 | tf_op jit(solution)/shard_map/ppermute | solution.py:69
  118.6 17.7 %collective-permute-start.26 = (bf16[8,80,1024]{2,1,0:T(8,128)(2,1)S(1)}, bf16[8,80,1024]{2,1,0:T(8,128)(2,1)}, u32[]{:S(2)}, u32[]{:S(2)}) collective-permute-start(bf16[8,80,1024]{2,1,0:T(8,128)(2,1)S(1)} %constant_dynamic-update-slice_fusion.22.refs_2_), channel_id=1, source_target_pairs={{0,16},{1,3},{2,18},{3,1},{4,20},{5,7},{6,22},{7,5},{8,24},{9,11},... | collective-permute-start | bytes 3932168 | tf_op jit(solution)/shard_map/ppermute | solution.py:69
  207.3 17.9 %collective-permute-start.36 = (bf16[8,80,1024]{2,1,0:T(8,128)(2,1)}, bf16[8,80,1024]{2,1,0:T(8,128)(2,1)}, u32[]{:S(2)}, u32[]{:S(2)}) collective-permute-start(bf16[8,80,1024]{2,1,0:T(8,128)(2,1)} %add_convert_fusion.2), channel_id=1, source_target_pairs={{0,16},{1,3},{2,18},{3,1},{4,20},{5,7},{6,22},{7,5},{8,24},{9,11},... | collective-permute-start | bytes 3932168 | tf_op jit(solution)/shard_map/ppermute | solution.py:69
  225.8 25.0 %collective-permute-start.39 = (bf16[8,32,2560]{2,1,0:T(8,128)(2,1)}, bf16[8,32,2560]{2,1,0:T(8,128)(2,1)}, u32[]{:S(2)}, u32[]{:S(2)}) collective-permute-start(bf16[8,32,2560]{2,1,0:T(8,128)(2,1)} %add_convert_fusion.1), channel_id=1, source_target_pairs={{0,16},{1,3},{2,18},{3,1},{4,20},{5,7},{6,22},{7,5},{8,24},{9,11},... | collective-permute-start | bytes 3932168 | tf_op jit(solution)/shard_map/ppermute | solution.py:69
  229.0 21.8 %collective-permute-start.40 = (bf16[4,80,1024]{2,1,0:T(8,128)(2,1)}, bf16[4,80,1024]{2,1,0:T(8,128)(2,1)}, u32[]{:S(2)}, u32[]{:S(2)}) collective-permute-start(bf16[4,80,1024]{2,1,0:T(8,128)(2,1)} %add_convert_fusion.9), channel_id=1, source_target_pairs={{0,2},{1,17},{2,0},{3,19},{4,6},{5,21},{6,4},{7,23},{8,10},{9,25},... | collective-permute-start | bytes 1966088 | tf_op jit(solution)/shard_map/ppermute | solution.py:69
  235.0 42.3 %collective-permute-start.45 = (bf16[8,32,3584]{2,1,0:T(8,128)(2,1)}, bf16[8,32,3584]{2,1,0:T(8,128)(2,1)}, u32[]{:S(2)}, u32[]{:S(2)}) collective-permute-start(bf16[8,32,3584]{2,1,0:T(8,128)(2,1)} %add_convert_fusion), channel_id=1, source_target_pairs={{0,16},{1,3},{2,18},{3,1},{4,20},{5,7},{6,22},{7,5},{8,24},{9,11},... | collective-permute-start | bytes 5505032 | tf_op jit(solution)/shard_map/ppermute | solution.py:69
  252.9 18.0 %collective-permute-start.41 = (bf16[4,32,2560]{2,1,0:T(8,128)(2,1)}, bf16[4,32,2560]{2,1,0:T(8,128)(2,1)}, u32[]{:S(2)}, u32[]{:S(2)}) collective-permute-start(bf16[4,32,2560]{2,1,0:T(8,128)(2,1)} %add_convert_fusion.8), channel_id=1, source_target_pairs={{0,2},{1,17},{2,0},{3,19},{4,6},{5,21},{6,4},{7,23},{8,10},{9,25},... | collective-permute-start | bytes 1966088 | tf_op jit(solution)/shard_map/ppermute | solution.py:69
  257.0 22.2 %collective-permute-start.44 = (bf16[1,80,1024]{2,1,0:T(8,128)(2,1)}, bf16[1,80,1024]{2,1,0:T(8,128)(2,1)S(1)}, u32[]{:S(2)}, u32[]{:S(2)}) collective-permute-start(bf16[1,80,1024]{2,1,0:T(8,128)(2,1)} %get-tuple-element.661), channel_id=1, source_target_pairs={{0,12},{1,13},{2,14},{3,15},{4,0},{5,1},{6,2},{7,3},{8,4},{9,5},{1... | collective-permute-start | bytes 491528 | tf_op jit(solution)/shard_map/ppermute | solution.py:57
  258.7 20.5 %collective-permute-start.43 = (bf16[1,80,1024]{2,1,0:T(8,128)(2,1)}, bf16[1,80,1024]{2,1,0:T(8,128)(2,1)S(1)}, u32[]{:S(2)}, u32[]{:S(2)}) collective-permute-start(bf16[1,80,1024]{2,1,0:T(8,128)(2,1)} %get-tuple-element.662), channel_id=1, source_target_pairs={{0,8},{1,9},{2,10},{3,11},{4,12},{5,13},{6,14},{7,15},{8,0},{9,1},... | collective-permute-start | bytes 491528 | tf_op jit(solution)/shard_map/ppermute | solution.py:57
  258.7 20.5 %collective-permute-start.42 = (bf16[1,80,1024]{2,1,0:T(8,128)(2,1)}, bf16[1,80,1024]{2,1,0:T(8,128)(2,1)}, u32[]{:S(2)}, u32[]{:S(2)}) collective-permute-start(bf16[1,80,1024]{2,1,0:T(8,128)(2,1)} %get-tuple-element.663), channel_id=1, source_target_pairs={{0,4},{1,5},{2,6},{3,7},{4,8},{5,9},{6,10},{7,11},{8,12},{9,13},{1... | collective-permute-start | bytes 491528 | tf_op jit(solution)/shard_map/ppermute | solution.py:57
  281.3 20.2 %collective-permute-start.49 = (bf16[4,32,3584]{2,1,0:T(8,128)(2,1)S(1)}, bf16[4,32,3584]{2,1,0:T(8,128)(2,1)S(1)}, u32[]{:S(2)}, u32[]{:S(2)}) collective-permute-start(bf16[4,32,3584]{2,1,0:T(8,128)(2,1)S(1)} %add_convert_fusion.4), channel_id=1, source_target_pairs={{0,2},{1,17},{2,0},{3,19},{4,6},{5,21},{6,4},{7,23},{8,10},{9,25},... | collective-permute-start | bytes 2752520 | tf_op jit(solution)/shard_map/ppermute | solution.py:69
  282.4 19.1 %collective-permute-start.48 = (bf16[1,32,2560]{2,1,0:T(8,128)(2,1)S(1)}, bf16[1,32,2560]{2,1,0:T(8,128)(2,1)S(1)}, u32[]{:S(2)}, u32[]{:S(2)}) collective-permute-start(bf16[1,32,2560]{2,1,0:T(8,128)(2,1)S(1)} %get-tuple-element.658), channel_id=1, source_target_pairs={{0,12},{1,13},{2,14},{3,15},{4,0},{5,1},{6,2},{7,3},{8,4},{9,5},{1... | collective-permute-start | bytes 491528 | tf_op jit(solution)/shard_map/ppermute | solution.py:57
  284.2 17.3 %collective-permute-start.47 = (bf16[1,32,2560]{2,1,0:T(8,128)(2,1)S(1)}, bf16[1,32,2560]{2,1,0:T(8,128)(2,1)S(1)}, u32[]{:S(2)}, u32[]{:S(2)}) collective-permute-start(bf16[1,32,2560]{2,1,0:T(8,128)(2,1)S(1)} %get-tuple-element.659), channel_id=1, source_target_pairs={{0,8},{1,9},{2,10},{3,11},{4,12},{5,13},{6,14},{7,15},{8,0},{9,1},... | collective-permute-start | bytes 491528 | tf_op jit(solution)/shard_map/ppermute | solution.py:57
  285.7 20.7 %collective-permute-start.52 = (bf16[8,32,1600]{2,1,0:T(8,128)(2,1)S(1)}, bf16[8,32,1600]{2,1,0:T(8,128)(2,1)S(1)}, u32[]{:S(2)}, u32[]{:S(2)}) collective-permute-start(bf16[8,32,1600]{2,1,0:T(8,128)(2,1)S(1)} %add_convert_fusion.5), channel_id=1, source_target_pairs={{0,16},{1,3},{2,18},{3,1},{4,20},{5,7},{6,22},{7,5},{8,24},{9,11},... | collective-permute-start | bytes 2457608 | tf_op jit(solution)/shard_map/ppermute | solution.py:69
  304.7 19.8 %collective-permute-start.55 = (bf16[1,32,3584]{2,1,0:T(8,128)(2,1)}, bf16[1,32,3584]{2,1,0:T(8,128)(2,1)}, u32[]{:S(2)}, u32[]{:S(2)}) collective-permute-start(bf16[1,32,3584]{2,1,0:T(8,128)(2,1)} %get-tuple-element.656), channel_id=1, source_target_pairs={{0,8},{1,9},{2,10},{3,11},{4,12},{5,13},{6,14},{7,15},{8,0},{9,1},... | collective-permute-start | bytes 688136 | tf_op jit(solution)/shard_map/ppermute | solution.py:57
  304.7 19.8 %collective-permute-start.54 = (bf16[1,32,3584]{2,1,0:T(8,128)(2,1)}, bf16[1,32,3584]{2,1,0:T(8,128)(2,1)}, u32[]{:S(2)}, u32[]{:S(2)}) collective-permute-start(bf16[1,32,3584]{2,1,0:T(8,128)(2,1)} %get-tuple-element.657), channel_id=1, source_target_pairs={{0,4},{1,5},{2,6},{3,7},{4,8},{5,9},{6,10},{7,11},{8,12},{9,13},{1... | collective-permute-start | bytes 688136 | tf_op jit(solution)/shard_map/ppermute | solution.py:57
  307.5 18.0 %collective-permute-start.53 = (bf16[4,32,1600]{2,1,0:T(8,128)(2,1)}, bf16[4,32,1600]{2,1,0:T(8,128)(2,1)}, u32[]{:S(2)}, u32[]{:S(2)}) collective-permute-start(bf16[4,32,1600]{2,1,0:T(8,128)(2,1)} %add_convert_fusion.11), channel_id=1, source_target_pairs={{0,2},{1,17},{2,0},{3,19},{4,6},{5,21},{6,4},{7,23},{8,10},{9,25},... | collective-permute-start | bytes 1228808 | tf_op jit(solution)/shard_map/ppermute | solution.py:69
  315.5 24.7 %collective-permute-start.64 = (bf16[32,2560]{1,0:T(8,128)(2,1)S(1)}, bf16[32,2560]{1,0:T(8,128)(2,1)}, u32[]{:S(2)}, u32[]{:S(2)}) collective-permute-start(bf16[32,2560]{1,0:T(8,128)(2,1)S(1)} %bitcast.112), channel_id=1, source_target_pairs={{0,16},{16,0},{1,17},{17,1},{2,18},{18,2},{3,19},{19,3},{4,20},{20... | collective-permute-start | bytes 491528 | tf_op jit(solution)/shard_map/ppermute | solution.py:60
  (79 other events, 729.3 us)

commit v4 on v3

--- a/solution.py
+++ b/solution.py
@@ -366,6 +366,16 @@
 
 def plus(a, b):
     return a + b
+
+
+def block_product(sz, left, parts):
+    b, out = sz.block, None
+    for j in range(sz.blocks):
+        part = nn(left[:, b * j : b * (j + 1)], parts[j])
+        if j:
+            part = jnp.concatenate([jnp.zeros((left.shape[0], b * j), F32), part], axis=1)
+        out = part if out is None else out + part
+    return out
 
 
 def attention_forward(sz, x, gain, wqkv, wo, cos, sin, bias, a1, heads, lse, mixp, mix, done=lambda stage: None):
@@ -389,26 +399,26 @@
     done(0)
     if sz.lse > sz.hq:
         lse[...] = jnp.zeros(lse.shape, F32)
-    for g in range(sz.kvh):
-        k = head(heads, sz.hq + g).T
-        vt = head(heads, sz.hq + sz.kvh + g)
-        for r in range(sz.group):
-            h = g * sz.group + r
+    for first in range(0, sz.kvh, 3):
+        groups = range(first, min(first + 3, sz.kvh))
+        keys = {g: head(heads, sz.hq + g).T for g in groups}
+        values = {g: head(heads, sz.hq + sz.kvh + g) for g in groups}
+        pairs = [(g, g * sz.group + r) for g in groups for r in range(sz.group)]
+        scores = []
+        for g, h in pairs:
             q = head(heads, h)
-            ss = [
-                nn(k[b * j : b * (j + 1)], q[:, b * j :]) + bias[b * j : b * (j + 1), b * j :]
+            scores.append([
+                nn(keys[g][b * j : b * (j + 1)], q[:, b * j :]) + bias[b * j : b * (j + 1), b * j :]
                 for j in range(sz.blocks)
-            ]
-            top = by_block(sz, [jnp.max(s, axis=0, keepdims=True) for s in ss], jnp.maximum)
-            sums, out = [], None
-            for j in range(sz.blocks):
-                e = jnp.exp(ss[j] - join(top[j:], 1))
-                sums.append(jnp.sum(e, axis=0, keepdims=True))
-                part = nn(vt[:, b * j : b * (j + 1)], e.astype(BF))
-                if j:
-                    part = jnp.concatenate([jnp.zeros((HEAD_SIZE, b * j), F32), part], axis=1)
-                out = part if out is None else out + part
-            summed = join(by_block(sz, sums, plus), 1)
+            ])
+        tops = [by_block(sz, [jnp.max(s, axis=0, keepdims=True) for s in ss], jnp.maximum) for ss in scores]
+        powers, sums = [], []
+        for ss, top in zip(scores, tops):
+            e = [jnp.exp(ss[j] - join(top[j:], 1)) for j in range(sz.blocks)]
+            sums.append(join(by_block(sz, [jnp.sum(v, axis=0, keepdims=True) for v in e], plus), 1))
+            powers.append([v.astype(BF) for v in e])
+        for (g, h), e, top, summed in zip(pairs, powers, tops, sums):
+            out = block_product(sz, values[g], e)
             mix[h * HEAD_SIZE : (h + 1) * HEAD_SIZE, :] = out * (1.0 / summed)
             lse[h : h + 1, :] = join(top, 1) + jnp.log(summed)
     row = lax.broadcasted_iota(jnp.int32, (sz.padded, sz.t), 0)
@@ -419,7 +429,7 @@
     return x + tn(mixp[...], wo[...])
 
 
-def attention_backward(sz, gh, gl, x, gain, wqkv, wo, cos, sin, bias, heads, lse, gm, g_heads, gs_ref, p_ref, g_qkv, ready=None):
+def attention_backward(sz, gh, gl, x, gain, wqkv, wo, cos, sin, bias, heads, lse, gm, g_heads, g_qkv, ready=None):
     b, half = sz.block, HEAD_SIZE // 2
     for j in range(sz.n):
         part = nt(wo[sz.padded * j : sz.padded * (j + 1), :], gl) if sz.n < 4 else None
@@ -438,35 +448,20 @@
         kt = head(heads, sz.hq + g)
         k = kt.T
         v = head(heads, sz.hq + sz.kvh + g).T
+        hs = range(g * sz.group, (g + 1) * sz.group)
+        qs, gms = [head(heads, h) for h in hs], [head(gm, h).astype(BF) for h in hs]
+        cut = [(b * j, b * (j + 1)) for j in range(sz.blocks)]
+        scores = [[nn(k[lo:hi], q[:, lo:]) + bias[lo:hi, lo:] for lo, hi in cut] for q in qs]
+        gps = [[nn(v[lo:hi], m[:, lo:]) for lo, hi in cut] for m in gms]
+        ps = [[jnp.exp(s - lse[h : h + 1, :][:, lo:]) for s, (lo, _) in zip(ss, cut)] for ss, h in zip(scores, hs)]
         gk = gv = None
-        for r in range(sz.group):
-            h = g * sz.group + r
-            q, gmh = head(heads, h), head(gm, h).astype(BF)
-            row = lse[h : h + 1, :]
-            ps, gps, down = [], [], []
-            for j in range(sz.blocks):
-                lo = b * j
-                s = nn(k[lo : lo + b], q[:, lo:]) + bias[lo : lo + b, lo:]
-                p = jnp.exp(s - row[:, lo:])
-                gp = nn(v[lo : lo + b], gmh[:, lo:])
-                ps.append(p)
-                gps.append(gp)
-                down.append(jnp.sum(p * gp, axis=0, keepdims=True))
-            d = by_block(sz, down, plus)
-            for j in range(sz.blocks):
-                lo = b * j
-                gs_ref[r, lo : lo + b, lo:] = (ps[j] * (gps[j] - join(d[j:], 1))).astype(BF)
-                p_ref[r, lo : lo + b, lo:] = ps[j].astype(BF)
-            gq = join(
-                [
-                    nn(kt[:, : b * (i + 1)], gs_ref[r, : b * (i + 1), b * i : b * (i + 1)])
-                    for i in range(sz.blocks)
-                ],
-                1,
-            )
-            part_k = join([nt(q[:, b * j :], gs_ref[r, b * j : b * (j + 1), b * j :]) for j in range(sz.blocks)], 1)
-            part_v = join([nt(gmh[:, b * j :], p_ref[r, b * j : b * (j + 1), b * j :]) for j in range(sz.blocks)], 1)
-            g_heads[h * HEAD_SIZE : (h + 1) * HEAD_SIZE, :] = gq * HEAD_SIZE ** (-0.5)
+        for h, q, m, p, gp in zip(hs, qs, gms, ps, gps):
+            d = by_block(sz, [jnp.sum(a * c, axis=0, keepdims=True) for a, c in zip(p, gp)], plus)
+            g_s = [(p[j] * (gp[j] - join(d[j:], 1))).astype(BF) for j in range(sz.blocks)]
+            low = [a.astype(BF) for a in p]
+            part_k = join([nt(q[:, lo:], a) for (lo, _), a in zip(cut, g_s)], 1)
+            part_v = join([nt(m[:, lo:], a) for (lo, _), a in zip(cut, low)], 1)
+            g_heads[h * HEAD_SIZE : (h + 1) * HEAD_SIZE, :] = block_product(sz, kt, g_s) * HEAD_SIZE ** (-0.5)
             gk = part_k if gk is None else gk + part_k
             gv = part_v if gv is None else gv + part_v
         at = (sz.hq + g) * HEAD_SIZE
@@ -646,7 +641,7 @@
          gain_grads, *refs) = refs
         down_out, gate_out, refs = refs[:3], refs[3:6], refs[6:]
         (wd, wqkv, wo, wg, wu, inners, cls, x2, hidden, a1, heads, lse, mixp, a2s, gate, up, ggs, gu, gl, g_qkv,
-         bias_ref, mix, g_heads, gs, probs, sem, piece_sem) = refs
+         bias_ref, mix, g_heads, sem, piece_sem) = refs
         io = Copies(sem)
         if aligned:
             first = start(fetches(order_ref, down_refs, [(wd, 0)], piece_sem, 0))
@@ -687,7 +682,7 @@
         out = io.start(gl, gl_hbm)
         gain_a, g_x = attention_backward(
             sz, hidden, gl[...], x2, gains_ref[0:1, :], wqkv, wo, cos, sin, bias_ref, heads, lse,
-            mix, g_heads, gs, probs, g_qkv
+            mix, g_heads, g_qkv
         )
         io.store(g_qkv, g_qkv_hbm)
         hidden[...] = g_x
@@ -736,7 +731,7 @@
         v((2 * t, ff), BF), v((2 * t, wide), BF), v((t, wide), F32), v((t, wide), F32), v((t, wide), BF), v((sz.feat, t), BF),
         v((sz.lse, t), F32), v((wide, t), BF), v((2 * t, wide), BF), v((t, ff), BF), v((t, ff), BF), v((2 * t, ff), BF),
         v((t, ff), BF), v((t, wide), BF), v((sz.feat, t), BF), v((t, t), F32), v((sz.width + 16, t), F32),
-        v((sz.feat, t), F32), v((sz.group, t, t), BF), v((sz.group, t, t), BF),
+        v((sz.feat, t), F32),
         pltpu.SemaphoreType.DMA((4 * sz.n + 40,)), pltpu.SemaphoreType.DMA((10 * sz.n,)),
     ]
     return call(body, ins, outs, scratch, 24 * t * wide * ff, 60, specs, out_specs)
@@ -793,7 +788,7 @@
 
     def body(gh_hbm, gl_hbm, x_hbm, gains_ref, wqkv_hbm, wo_hbm, cos, sin, bias_hbm, heads_hbm, lse_ref,
              g_x_hbm, g_qkv_hbm, gain_grad,
-             gh, gl, x_low, x, wqkv, wo, bias_ref, heads, g_qkv, mix, g_heads, gs, probs, sem):
+             gh, gl, x_low, x, wqkv, wo, bias_ref, heads, g_qkv, mix, g_heads, sem):
         io = Copies(sem)
         first = [io.start(gl_hbm, gl), io.start(wo_hbm, wo)]
         second = [io.start(heads_hbm, heads), io.start(bias_hbm, bias_ref)]
@@ -810,7 +805,7 @@
 
         gain_a, back_x = attention_backward(
             sz, gh, gl[...], x, gains_ref[0:1, :], wqkv, wo, cos, sin, bias_ref,
-            heads, lse_ref, mix, g_heads, gs, probs, g_qkv, ready
+            heads, lse_ref, mix, g_heads, g_qkv, ready
         )
         io.store(g_qkv, g_qkv_hbm)
         gl[...] = back_x.astype(BF)
@@ -826,7 +821,7 @@
         [
             v((t, wide), F32), v((t, wide), BF), v((t, wide), BF), v((t, wide), F32), v((wide, sz.feat), BF),
             v((wide, wide), BF), v((t, t), F32), v((sz.feat, t), BF), v((sz.feat, t), BF), v((sz.width + 16, t), F32),
-            v((sz.feat, t), F32), v((sz.group, t, t), BF), v((sz.group, t, t), BF), pltpu.SemaphoreType.DMA((16,)),
+            v((sz.feat, t), F32), pltpu.SemaphoreType.DMA((16,)),
         ],
         10 * t * wide * sz.feat, 40,
         specs=[ANY] * 3 + [VM] + [ANY] * 2 + [VM] * 2 + [ANY] * 2 + [VM],
@@ -1022,10 +1017,10 @@
         lambda *v: qkv_grad(sz, *v, half), back, (a1_1, a1_2), (g_qkv1, g_qkv2), gain2, gain_a1
     )
     sg.come()
+    sd.come_z()
+    sg.along_z()
     su.come()
     su.second()
-    sd.come_z()
-    sg.along_z()
     sa = Scatter(at, order, own, *send)
     sa.core(0)
     sa.core(1)
@@ -1050,14 +1045,14 @@
     sa.along_x()
     sg.come()
     sg.cores()
+    sd.come()
+    r_down = sd.result()
     su.come()
     su.cores()
-    sd.come()
     sg.come()
+    r_gate = sg.result()
     su.come()
     r_up = su.result()
-    r_gate = sg.result()
-    r_down = sd.result()
     second, g_x = narrow(second, n, real, padded), narrow(g_x, n, real, padded)
     sa.come()
     sa.cores()

time: 360 us -> 350 us (0.972)
  waiting for transfers between devices: 96.2 us -> 84 us
  starting transfers between devices: 56.1 us -> 64.8 us
  Pallas kernels: 128 us -> 121 us
    ppermute x16, waiting for transfers between devices: 51.1 us -> 43.5 us  [cross(): return lax.ppermute(v, ('dp', 'fsdp'), pairs)]
    pallas_call x9, Pallas kernels: 128 us -> 121 us  [call(): pl.pallas_call(body, in_specs=specs or [VM] * len(ins), out_specs=out_spe...]
    ppermute x24, starting transfers between devices: 30.6 us -> 34.3 us  [shift_z(): lax.ppermute(v, 'fsdp', [(i, (i + 4 * k) % self.n) for i in range(self.n)])]
    ppermute x4, waiting for transfers between devices: 3.63 us -> 0.01 us  [swap_x(): return lax.ppermute(v, 'dp', [(d, d ^ 1) for d in range(self.groups)])]
    unnamed x86 -> x88, local copies, waits for them, and re-layouts: 10.2 us -> 11.2 us
  transfers between devices with their start and end apart: 68 -> 68, of which waited for: 26 -> 25; matrix products, arithmetic and copies ran while one was open for 16% -> 17% of each run, Pallas kernels for 19% -> 19%
where the time goes in v4:
time: 350 us; the launch traced here: 344 us
  Pallas kernels  121 us (35%)
  waiting for transfers between devices  84 us (24%)
  starting transfers between devices  64.8 us (19%)
  local copies, waits for them, and re-layouts  38.8 us (11%)
  other arithmetic  33.5 us (10%)
    pallas_call x9, Pallas kernels, call(): pl.pallas_call(body, in_specs=specs or [VM] * len(ins), out_specs=out_spe...  121 us
    ppermute x16, waiting for transfers between devices, cross(): return lax.ppermute(v, ('dp', 'fsdp'), pairs)  43.5 us
    ppermute x24, starting transfers between devices, shift_z(): lax.ppermute(v, 'fsdp', [(i, (i + 4 * k) % self.n) for i in range(self.n)])  34.3 us
    ppermute x24, waiting for transfers between devices, shift_z(): lax.ppermute(v, 'fsdp', [(i, (i + 4 * k) % self.n) for i in range(self.n)])  28.1 us
    convert_element_type x16, other arithmetic, step(): return add(*[a[lo:hi] for a, (lo, hi) in zip(v, cuts)]).astype(BF)  26.5 us
    ppermute x16, starting transfers between devices, cross(): return lax.ppermute(v, ('dp', 'fsdp'), pairs)  19.3 us
    ppermute x24, waiting for transfers between devices, swap_core(): return lax.ppermute(v, 'fsdp', [(i, i ^ 1) for i in range(self.n)])  12.5 us
    unnamed x88, local copies, waits for them, and re-layouts  11.2 us
  transfers between devices with their start and end apart: 68, of which 25 were waited for; matrix products, arithmetic and copies ran while one was open for 17% of the time, Pallas kernels for 19%

profile of v4, /device:TPU:0, one launch (start us, length us, event | category | flops | bytes accessed | tf_op | source)
XLA Modules:
  0.0 344.1 jit_solution(5301542628186124774)
XLA Ops:
  4.9 5.0 %collective-permute-start.6 = (bf16[1,32,2624]{2,1,0:T(8,128)(2,1)S(1)}, bf16[1,32,2624]{2,1,0:T(8,128)(2,1)S(1)}, u32[]{:S(2)}, u32[]{:S(2)}) collective-permute-start(bf16[1,32,2624]{2,1,0:T(8,128)(2,1)S(1)} %select_bitcast_fusion), channel_id=1, source_target_pairs={{0,12},{1,13},{2,14},{3,15},{4,0},{5,1},{6,2},{7,3},{8,4},{9,5},{1... | collective-permute-start | bytes 503816 | tf_op jit(solution)/shard_map/ppermute | solution.py:57
  17.5 7.3 %collective-permute-done.5 = bf16[1,32,2624]{2,1,0:T(8,128)(2,1)S(1)} collective-permute-done((bf16[1,32,2624]{2,1,0:T(8,128)(2,1)S(1)}, bf16[1,32,2624]{2,1,0:T(8,128)(2,1)S(1)}, u32[]{:S(2)}, u32[]{:S(2)}) %collective-permute-start.5) | collective-permute-done | bytes 167968 | tf_op jit(solution)/shard_map/ppermute | solution.py:57
  31.3 4.6 %collective-permute-done.7 = bf16[4,32,2624]{2,1,0:T(8,128)(2,1)S(1)} collective-permute-done((bf16[4,32,2624]{2,1,0:T(8,128)(2,1)S(1)}, bf16[4,32,2624]{2,1,0:T(8,128)(2,1)S(1)}, u32[]{:S(2)}, u32[]{:S(2)}) %collective-permute-start.7) | collective-permute-done | bytes 671776 | tf_op jit(solution)/shard_map/ppermute | solution.py:69
  37.6 5.5 %collective-permute-done.9 = bf16[1,32,2560]{2,1,0:T(8,128)(2,1)S(1)} collective-permute-done((bf16[1,32,2560]{2,1,0:T(8,128)(2,1)S(1)}, bf16[1,32,2560]{2,1,0:T(8,128)(2,1)S(1)}, u32[]{:S(2)}, u32[]{:S(2)}) %collective-permute-start.9) | collective-permute-done | bytes 163872 | tf_op jit(solution)/shard_map/ppermute | solution.py:57
  58.5 3.1 collective-permute-done.15.p1.refs_7_
  77.9 11.7 %shard_map.204 = (f32[384,1024]{1,0:T(8,128)}, bf16[384,1024]{1,0:T(8,128)(2,1)}, bf16[1600,384]{1,0:T(8,128)(2,1)}, f32[16,384]{1,0:T(8,128)}, bf16[1024,384]{1,0:T(8,128)(2,1)}, /*index=5*/f32[8,1024]{1,0:T(8,128)}) custom-call(s32[32]{0:T(128)} %stack.179.order_ref.refs_0_, bf16[8,32,2624]{2,1,0:T(8,128)(2,1)} %copy-done, ...), custom_call_target="tpu_custom_call" | custom-call | flops 1000 | bytes 1000 | tf_op jit(solution)/shard_map/pallas_call | solution.py:264
  96.0 7.5 %shard_map.205 = (bf16[384,1024]{1,0:T(8,128)(2,1)}, bf16[384,2560]{1,0:T(8,128)(2,1)}) custom-call(s32[32]{0:T(128)} %stack.179.order_ref.refs_0_, bf16[8,32,2560]{2,1,0:T(8,128)(2,1)} %copy-done.2, bf16[8,32,2560]{2,1,0:T(8,128)(2,1)} %collective-permute-done.22.p1.refs_11_, bf16[8,32,2560]{2,1,0:T(8,128)(2,1)} %copy-done.4, ...), custom_call_target="tpu_custom_call" | custom-call | flops 1000 | bytes 1000 | tf_op jit(solution)/shard_map/pallas_call | solution.py:264
  103.5 7.0 %collective-permute-done.23 = bf16[4,80,1024]{2,1,0:T(8,128)(2,1)} collective-permute-done((bf16[4,80,1024]{2,1,0:T(8,128)(2,1)S(1)}, bf16[4,80,1024]{2,1,0:T(8,128)(2,1)}, u32[]{:S(2)}, u32[]{:S(2)}) %collective-permute-start.23) | collective-permute-done | bytes 655392 | tf_op jit(solution)/shard_map/ppermute | solution.py:69
  112.8 3.5 %collective-permute-done.27.p1.refs_15_ = bf16[8,32,2560]{2,1,0:T(8,128)(2,1)} collective-permute-done((bf16[8,32,2560]{2,1,0:T(8,128)(2,1)S(1)}, bf16[8,32,2560]{2,1,0:T(8,128)(2,1)}, u32[]{:S(2)}, u32[]{:S(2)}) %collective-permute-start.27) | collective-permute-done | bytes 1310752 | tf_op jit(solution)/shard_map/ppermute | solution.py:69
  117.8 3.3 collective-permute-done.28.p2.refs_16_
  122.2 7.7 %shard_map.206 = (bf16[384,2560]{1,0:T(8,128)(2,1)}, bf16[384,2560]{1,0:T(8,128)(2,1)}) custom-call(s32[32]{0:T(128)} %stack.179.order_ref.refs_0_, bf16[8,32,2560]{2,1,0:T(8,128)(2,1)} %copy-done.1, bf16[8,32,2560]{2,1,0:T(8,128)(2,1)} %collective-permute-done.27.p1.refs_15_, bf16[8,32,2560]{2,1,0:T(8,128)(2,1)} %copy-done.3, ...), custom_call_target="tpu_custom_call" | custom-call | flops 1000 | bytes 1000 | tf_op jit(solution)/shard_map/pallas_call | solution.py:264
  129.9 4.6 %collective-permute-done.26.refs_3_ = bf16[8,80,1024]{2,1,0:T(8,128)(2,1)} collective-permute-done((bf16[8,80,1024]{2,1,0:T(8,128)(2,1)S(1)}, bf16[8,80,1024]{2,1,0:T(8,128)(2,1)}, u32[]{:S(2)}, u32[]{:S(2)}) %collective-permute-start.26) | collective-permute-done | bytes 1310752 | tf_op jit(solution)/shard_map/ppermute | solution.py:69
  135.1 2.6 collective-permute-done.31.refs_5_
  138.8 56.4 %shard_map.207 = (bf16[384,1024]{1,0:T(8,128)(2,1)}, bf16[1024,1600]{1,0:T(8,128)(2,1)}, bf16[1024,1024]{1,0:T(8,128)(2,1)}, bf16[384,1024]{1,0:T(8,128)(2,1)}, ...) custom-call(s32[32]{0:T(128)} %stack.179.order_ref.refs_0_, ...), custom_call_target="tpu_custom_call" | custom-call | flops 1000 | bytes 1000 | tf_op jit(solution)/shard_map/pallas_call | solution.py:264
  198.7 3.1 add_convert_fusion.2
  205.4 11.5 %shard_map.208 = (bf16[16,32,3584]{2,1,0:T(8,128)(2,1)}, bf16[8,32,3584]{2,1,0:T(8,128)(2,1)}, bf16[8,32,3584]{2,1,0:T(8,128)(2,1)}) custom-call(s32[12]{0:T(128)} %stack.192.refs_1_.back_ref, bf16[384,1024]{1,0:T(8,128)(2,1)} %get-tuple-element.511.a2_hbm.refs_22_.a_1, bf16[384,1024]{1,0:T(8,128)(2,1)} %get-tuple-element.512.a_2, ...), custom_call_target="tpu_custom_call" | custom-call | flops 1000 | bytes 1000 | tf_op jit(solution)/shard_map/pallas_call | solution.py:264
  216.9 2.8 collective-permute-done.36
  221.3 2.7 add_convert_fusion.9
  226.3 3.2 add_convert_fusion
  230.6 13.4 %shard_map.209 = (bf16[384,1024]{1,0:T(8,128)(2,1)}, bf16[1600,384]{1,0:T(8,128)(2,1)}, f32[8,1024]{1,0:T(8,128)}) custom-call(f32[384,1024]{1,0:T(8,128)} %get-tuple-element.532.gh_hbm, bf16[384,1024]{1,0:T(8,128)(2,1)} %get-tuple-element.533.l1.gl_hbm, bf16[384,1024]{1,0:T(8,128)(2,1)} %get-tuple-element.534.x_hbm, ...), custom_call_target="tpu_custom_call" | custom-call | flops 1000 | bytes 1000 | tf_op jit(solution)/shard_map/pallas_call | solution.py:264
  255.3 7.7 %shard_map.210 = (bf16[16,32,1600]{2,1,0:T(8,128)(2,1)}, bf16[8,32,1600]{2,1,0:T(8,128)(2,1)}, bf16[8,32,1600]{2,1,0:T(8,128)(2,1)}) custom-call(s32[12]{0:T(128)} %stack.192.refs_1_.back_ref, bf16[384,1024]{1,0:T(8,128)(2,1)} %get-tuple-element.560.a_1, bf16[384,1024]{1,0:T(8,128)(2,1)} %get-tuple-element.561.a_2, bf16[1600,384]{1,0:T(8,128)(2,1)} %get-tuple-element.562.g1, ...), custom_call_target="tpu_custom_call" | custom-call | flops 1000 | bytes 1000 | tf_op jit(solution)/shard_map/pallas_call | solution.py:264
  280.8 12.1 %collective-permute-done.49 = bf16[4,32,3584]{2,1,0:T(8,128)(2,1)S(1)} collective-permute-done((bf16[4,32,3584]{2,1,0:T(8,128)(2,1)S(1)}, bf16[4,32,3584]{2,1,0:T(8,128)(2,1)S(1)}, u32[]{:S(2)}, u32[]{:S(2)}) %collective-permute-start.49) | collective-permute-done | bytes 917536 | tf_op jit(solution)/shard_map/ppermute | solution.py:69
  312.3 6.0 %collective-permute-done.55 = bf16[1,32,3584]{2,1,0:T(8,128)(2,1)} collective-permute-done((bf16[1,32,3584]{2,1,0:T(8,128)(2,1)}, bf16[1,32,3584]{2,1,0:T(8,128)(2,1)}, u32[]{:S(2)}, u32[]{:S(2)}) %collective-permute-start.55) | collective-permute-done | bytes 229408 | tf_op jit(solution)/shard_map/ppermute | solution.py:57
  328.3 4.2 %collective-permute-done.58 = bf16[1,32,1600]{2,1,0:T(8,128)(2,1)S(1)} collective-permute-done((bf16[1,32,1600]{2,1,0:T(8,128)(2,1)S(1)}, bf16[1,32,1600]{2,1,0:T(8,128)(2,1)S(1)}, u32[]{:S(2)}, u32[]{:S(2)}) %collective-permute-start.58) | collective-permute-done | bytes 102432 | tf_op jit(solution)/shard_map/ppermute | solution.py:57
  (301 shorter events, 145.8 us)
Async XLA Ops:
  27.4 15.8 %collective-permute-start.9 = (bf16[1,32,2560]{2,1,0:T(8,128)(2,1)S(1)}, bf16[1,32,2560]{2,1,0:T(8,128)(2,1)S(1)}, u32[]{:S(2)}, u32[]{:S(2)}) collective-permute-start(bf16[1,32,2560]{2,1,0:T(8,128)(2,1)S(1)} %select_bitcast_fusion.3), channel_id=1, source_target_pairs={{0,8},{1,9},{2,10},{3,11},{4,12},{5,13},{6,14},{7,15},{8,0},{9,1},... | collective-permute-start | bytes 491528 | tf_op jit(solution)/shard_map/ppermute | solution.py:57
  36.1 25.5 %collective-permute-start.15 = (bf16[8,32,2624]{2,1,0:T(8,128)(2,1)S(1)}, bf16[8,32,2624]{2,1,0:T(8,128)(2,1)}, u32[]{:S(2)}, u32[]{:S(2)}) collective-permute-start(bf16[8,32,2624]{2,1,0:T(8,128)(2,1)S(1)} %constant_dynamic-update-slice_fusion.4.p0.refs_6_), channel_id=1, source_target_pairs={{0,16},{1,3},{2,18},{3,1},{4,20},{5,7},{6,22},{7,5},{8,24},{9,11},... | collective-permute-start | bytes 4030472 | tf_op jit(solution)/shard_map/ppermute | solution.py:69
  45.9 15.7 %collective-permute-start.14 = (bf16[4,32,2560]{2,1,0:T(8,128)(2,1)}, bf16[4,32,2560]{2,1,0:T(8,128)(2,1)}, u32[]{:S(2)}, u32[]{:S(2)}) collective-permute-start(bf16[4,32,2560]{2,1,0:T(8,128)(2,1)} %constant_dynamic-update-slice_fusion.6), channel_id=1, source_target_pairs={{0,2},{1,17},{2,0},{3,19},{4,6},{5,21},{6,4},{7,23},{8,10},{9,25},... | collective-permute-start | bytes 1966088 | tf_op jit(solution)/shard_map/ppermute | solution.py:69
  64.2 25.5 %collective-permute-start.22 = (bf16[8,32,2560]{2,1,0:T(8,128)(2,1)S(1)}, bf16[8,32,2560]{2,1,0:T(8,128)(2,1)}, u32[]{:S(2)}, u32[]{:S(2)}) collective-permute-start(bf16[8,32,2560]{2,1,0:T(8,128)(2,1)S(1)} %constant_dynamic-update-slice_fusion.10.p0.refs_10_), channel_id=1, source_target_pairs={{0,16},{1,3},{2,18},{3,1},{4,20},{5,7},{6,22},{7,5},{8,24},{9,11},... | collective-permute-start | bytes 3932168 | tf_op jit(solution)/shard_map/ppermute | solution.py:69
  69.4 20.3 %collective-permute-start.21 = (bf16[4,32,2560]{2,1,0:T(8,128)(2,1)S(1)}, bf16[4,32,2560]{2,1,0:T(8,128)(2,1)}, u32[]{:S(2)}, u32[]{:S(2)}) collective-permute-start(bf16[4,32,2560]{2,1,0:T(8,128)(2,1)S(1)} %constant_dynamic-update-slice_fusion.12), channel_id=1, source_target_pairs={{0,2},{1,17},{2,0},{3,19},{4,6},{5,21},{6,4},{7,23},{8,10},{9,25},... | collective-permute-start | bytes 1966088 | tf_op jit(solution)/shard_map/ppermute | solution.py:69
  72.0 17.6 %collective-permute-start.20 = (bf16[1,80,1024]{2,1,0:T(8,128)(2,1)S(1)}, bf16[1,80,1024]{2,1,0:T(8,128)(2,1)S(1)}, u32[]{:S(2)}, u32[]{:S(2)}) collective-permute-start(bf16[1,80,1024]{2,1,0:T(8,128)(2,1)S(1)} %select_bitcast_fusion.1), channel_id=1, source_target_pairs={{0,12},{1,13},{2,14},{3,15},{4,0},{5,1},{6,2},{7,3},{8,4},{9,5},{1... | collective-permute-start | bytes 491528 | tf_op jit(solution)/shard_map/ppermute | solution.py:57
  72.8 16.8 %collective-permute-start.19 = (bf16[1,80,1024]{2,1,0:T(8,128)(2,1)S(1)}, bf16[1,80,1024]{2,1,0:T(8,128)(2,1)S(1)}, u32[]{:S(2)}, u32[]{:S(2)}) collective-permute-start(bf16[1,80,1024]{2,1,0:T(8,128)(2,1)S(1)} %select_bitcast_fusion.1), channel_id=1, source_target_pairs={{0,8},{1,9},{2,10},{3,11},{4,12},{5,13},{6,14},{7,15},{8,0},{9,1},... | collective-permute-start | bytes 491528 | tf_op jit(solution)/shard_map/ppermute | solution.py:57
  91.4 24.8 %collective-permute-start.27 = (bf16[8,32,2560]{2,1,0:T(8,128)(2,1)S(1)}, bf16[8,32,2560]{2,1,0:T(8,128)(2,1)}, u32[]{:S(2)}, u32[]{:S(2)}) collective-permute-start(bf16[8,32,2560]{2,1,0:T(8,128)(2,1)S(1)} %constant_dynamic-update-slice_fusion.16.p0.refs_14_), channel_id=1, source_target_pairs={{0,16},{1,3},{2,18},{3,1},{4,20},{5,7},{6,22},{7,5},{8,24},{9,11},... | collective-permute-start | bytes 3932168 | tf_op jit(solution)/shard_map/ppermute | solution.py:69
  92.7 17.8 %collective-permute-start.23 = (bf16[4,80,1024]{2,1,0:T(8,128)(2,1)S(1)}, bf16[4,80,1024]{2,1,0:T(8,128)(2,1)}, u32[]{:S(2)}, u32[]{:S(2)}) collective-permute-start(bf16[4,80,1024]{2,1,0:T(8,128)(2,1)S(1)} %constant_dynamic-update-slice_fusion.18), channel_id=1, source_target_pairs={{0,2},{1,17},{2,0},{3,19},{4,6},{5,21},{6,4},{7,23},{8,10},{9,25},... | collective-permute-start | bytes 1966088 | tf_op jit(solution)/shard_map/ppermute | solution.py:69
  116.8 17.7 %collective-permute-start.26 = (bf16[8,80,1024]{2,1,0:T(8,128)(2,1)S(1)}, bf16[8,80,1024]{2,1,0:T(8,128)(2,1)}, u32[]{:S(2)}, u32[]{:S(2)}) collective-permute-start(bf16[8,80,1024]{2,1,0:T(8,128)(2,1)S(1)} %constant_dynamic-update-slice_fusion.22.refs_2_), channel_id=1, source_target_pairs={{0,16},{1,3},{2,18},{3,1},{4,20},{5,7},{6,22},{7,5},{8,24},{9,11},... | collective-permute-start | bytes 3932168 | tf_op jit(solution)/shard_map/ppermute | solution.py:69
  201.8 17.9 %collective-permute-start.36 = (bf16[8,80,1024]{2,1,0:T(8,128)(2,1)}, bf16[8,80,1024]{2,1,0:T(8,128)(2,1)}, u32[]{:S(2)}, u32[]{:S(2)}) collective-permute-start(bf16[8,80,1024]{2,1,0:T(8,128)(2,1)} %add_convert_fusion.2), channel_id=1, source_target_pairs={{0,16},{1,3},{2,18},{3,1},{4,20},{5,7},{6,22},{7,5},{8,24},{9,11},... | collective-permute-start | bytes 3932168 | tf_op jit(solution)/shard_map/ppermute | solution.py:69
  220.2 24.9 %collective-permute-start.39 = (bf16[8,32,2560]{2,1,0:T(8,128)(2,1)}, bf16[8,32,2560]{2,1,0:T(8,128)(2,1)}, u32[]{:S(2)}, u32[]{:S(2)}) collective-permute-start(bf16[8,32,2560]{2,1,0:T(8,128)(2,1)} %add_convert_fusion.1), channel_id=1, source_target_pairs={{0,16},{1,3},{2,18},{3,1},{4,20},{5,7},{6,22},{7,5},{8,24},{9,11},... | collective-permute-start | bytes 3932168 | tf_op jit(solution)/shard_map/ppermute | solution.py:69
  224.0 21.2 %collective-permute-start.40 = (bf16[4,80,1024]{2,1,0:T(8,128)(2,1)}, bf16[4,80,1024]{2,1,0:T(8,128)(2,1)}, u32[]{:S(2)}, u32[]{:S(2)}) collective-permute-start(bf16[4,80,1024]{2,1,0:T(8,128)(2,1)} %add_convert_fusion.9), channel_id=1, source_target_pairs={{0,2},{1,17},{2,0},{3,19},{4,6},{5,21},{6,4},{7,23},{8,10},{9,25},... | collective-permute-start | bytes 1966088 | tf_op jit(solution)/shard_map/ppermute | solution.py:69
  229.5 42.3 %collective-permute-start.48 = (bf16[8,32,3584]{2,1,0:T(8,128)(2,1)}, bf16[8,32,3584]{2,1,0:T(8,128)(2,1)}, u32[]{:S(2)}, u32[]{:S(2)}) collective-permute-start(bf16[8,32,3584]{2,1,0:T(8,128)(2,1)} %add_convert_fusion), channel_id=1, source_target_pairs={{0,16},{1,3},{2,18},{3,1},{4,20},{5,7},{6,22},{7,5},{8,24},{9,11},... | collective-permute-start | bytes 5505032 | tf_op jit(solution)/shard_map/ppermute | solution.py:69
  247.5 18.0 %collective-permute-start.41 = (bf16[4,32,2560]{2,1,0:T(8,128)(2,1)}, bf16[4,32,2560]{2,1,0:T(8,128)(2,1)}, u32[]{:S(2)}, u32[]{:S(2)}) collective-permute-start(bf16[4,32,2560]{2,1,0:T(8,128)(2,1)} %add_convert_fusion.8), channel_id=1, source_target_pairs={{0,2},{1,17},{2,0},{3,19},{4,6},{5,21},{6,4},{7,23},{8,10},{9,25},... | collective-permute-start | bytes 1966088 | tf_op jit(solution)/shard_map/ppermute | solution.py:69
  273.9 19.0 %collective-permute-start.49 = (bf16[4,32,3584]{2,1,0:T(8,128)(2,1)S(1)}, bf16[4,32,3584]{2,1,0:T(8,128)(2,1)S(1)}, u32[]{:S(2)}, u32[]{:S(2)}) collective-permute-start(bf16[4,32,3584]{2,1,0:T(8,128)(2,1)S(1)} %add_convert_fusion.4), channel_id=1, source_target_pairs={{0,2},{1,17},{2,0},{3,19},{4,6},{5,21},{6,4},{7,23},{8,10},{9,25},... | collective-permute-start | bytes 2752520 | tf_op jit(solution)/shard_map/ppermute | solution.py:69
  275.2 17.7 %collective-permute-start.47 = (bf16[1,32,2560]{2,1,0:T(8,128)(2,1)S(1)}, bf16[1,32,2560]{2,1,0:T(8,128)(2,1)S(1)}, u32[]{:S(2)}, u32[]{:S(2)}) collective-permute-start(bf16[1,32,2560]{2,1,0:T(8,128)(2,1)S(1)} %get-tuple-element.658), channel_id=1, source_target_pairs={{0,12},{1,13},{2,14},{3,15},{4,0},{5,1},{6,2},{7,3},{8,4},{9,5},{1... | collective-permute-start | bytes 491528 | tf_op jit(solution)/shard_map/ppermute | solution.py:57
  276.5 16.4 %collective-permute-start.46 = (bf16[1,32,2560]{2,1,0:T(8,128)(2,1)S(1)}, bf16[1,32,2560]{2,1,0:T(8,128)(2,1)S(1)}, u32[]{:S(2)}, u32[]{:S(2)}) collective-permute-start(bf16[1,32,2560]{2,1,0:T(8,128)(2,1)S(1)} %get-tuple-element.659), channel_id=1, source_target_pairs={{0,8},{1,9},{2,10},{3,11},{4,12},{5,13},{6,14},{7,15},{8,0},{9,1},... | collective-permute-start | bytes 491528 | tf_op jit(solution)/shard_map/ppermute | solution.py:57
  279.9 21.0 %collective-permute-start.52 = (bf16[8,32,1600]{2,1,0:T(8,128)(2,1)S(1)}, bf16[8,32,1600]{2,1,0:T(8,128)(2,1)S(1)}, u32[]{:S(2)}, u32[]{:S(2)}) collective-permute-start(bf16[8,32,1600]{2,1,0:T(8,128)(2,1)S(1)} %add_convert_fusion.5), channel_id=1, source_target_pairs={{0,16},{1,3},{2,18},{3,1},{4,20},{5,7},{6,22},{7,5},{8,24},{9,11},... | collective-permute-start | bytes 2457608 | tf_op jit(solution)/shard_map/ppermute | solution.py:69
  295.8 16.3 %collective-permute-start.56 = (bf16[1,32,3584]{2,1,0:T(8,128)(2,1)}, bf16[1,32,3584]{2,1,0:T(8,128)(2,1)}, u32[]{:S(2)}, u32[]{:S(2)}) collective-permute-start(bf16[1,32,3584]{2,1,0:T(8,128)(2,1)} %get-tuple-element.655), channel_id=1, source_target_pairs={{0,12},{1,13},{2,14},{3,15},{4,0},{5,1},{6,2},{7,3},{8,4},{9,5},{1... | collective-permute-start | bytes 688136 | tf_op jit(solution)/shard_map/ppermute | solution.py:57
  296.5 21.8 %collective-permute-start.55 = (bf16[1,32,3584]{2,1,0:T(8,128)(2,1)}, bf16[1,32,3584]{2,1,0:T(8,128)(2,1)}, u32[]{:S(2)}, u32[]{:S(2)}) collective-permute-start(bf16[1,32,3584]{2,1,0:T(8,128)(2,1)} %get-tuple-element.656), channel_id=1, source_target_pairs={{0,8},{1,9},{2,10},{3,11},{4,12},{5,13},{6,14},{7,15},{8,0},{9,1},... | collective-permute-start | bytes 688136 | tf_op jit(solution)/shard_map/ppermute | solution.py:57
  298.8 19.5 %collective-permute-start.54 = (bf16[1,32,3584]{2,1,0:T(8,128)(2,1)}, bf16[1,32,3584]{2,1,0:T(8,128)(2,1)}, u32[]{:S(2)}, u32[]{:S(2)}) collective-permute-start(bf16[1,32,3584]{2,1,0:T(8,128)(2,1)} %get-tuple-element.657), channel_id=1, source_target_pairs={{0,4},{1,5},{2,6},{3,7},{4,8},{5,9},{6,10},{7,11},{8,12},{9,13},{1... | collective-permute-start | bytes 688136 | tf_op jit(solution)/shard_map/ppermute | solution.py:57
  301.9 17.4 %collective-permute-start.53 = (bf16[4,32,1600]{2,1,0:T(8,128)(2,1)}, bf16[4,32,1600]{2,1,0:T(8,128)(2,1)}, u32[]{:S(2)}, u32[]{:S(2)}) collective-permute-start(bf16[4,32,1600]{2,1,0:T(8,128)(2,1)} %add_convert_fusion.11), channel_id=1, source_target_pairs={{0,2},{1,17},{2,0},{3,19},{4,6},{5,21},{6,4},{7,23},{8,10},{9,25},... | collective-permute-start | bytes 1228808 | tf_op jit(solution)/shard_map/ppermute | solution.py:69
  309.8 22.7 %collective-permute-start.64 = (bf16[32,2560]{1,0:T(8,128)(2,1)S(1)}, bf16[32,2560]{1,0:T(8,128)(2,1)}, u32[]{:S(2)}, u32[]{:S(2)}) collective-permute-start(bf16[32,2560]{1,0:T(8,128)(2,1)S(1)} %bitcast.112), channel_id=1, source_target_pairs={{0,16},{16,0},{1,17},{17,1},{2,18},{18,2},{3,19},{19,3},{4,20},{20... | collective-permute-start | bytes 491528 | tf_op jit(solution)/shard_map/ppermute | solution.py:60
  (80 other events, 717.8 us)

commit v5 on v4

--- a/solution.py
+++ b/solution.py
@@ -524,7 +524,7 @@
         io = Copies(out_sem)
         first = start(fetches(order_ref, (p0, p1, p2, p3), [(wqkv, sz.wide)], sem, 0))
         loads = [io.start(x_hbm, x), io.start(bias_hbm, bias_ref)]
-        loads += start(fetches(order_ref, (p0, p1, p2, p3), [(wo, 0)], sem, 2 * sz.n))
+        last = start(fetches(order_ref, (p0, p1, p2, p3), [(wo, 0)], sem, 2 * sz.n))
         wait(first)
         rows = []
         for k in range(2):
@@ -542,6 +542,8 @@
         def done(stage):
             for a, b in (((a1, a1_hbm), (heads, heads_hbm)), ((mixp, mixp_hbm),))[stage]:
                 io.store(a, b)
+            if stage == 1:
+                wait(last)
 
         hidden[...] = attention_forward(
             sz, hidden[...], gains[0:1, :], wqkv, wo, cos, sin, bias_ref, a1, heads, lse, mixp, mix, done
@@ -654,15 +656,16 @@
         first += [io.start(inner1_hbm, inner1), io.start(hidden1_hbm, x2)]
         wait(first)
         loads = start(fetches(order_ref, attn_refs, [(wqkv, wide)], piece_sem, 2 * sz.n))
-        loads += start(fetches(order_ref, attn_refs, [(wo, 0)], piece_sem, 4 * sz.n))
         loads += [io.start(bias_hbm, bias_ref)]
+        last = start(fetches(order_ref, attn_refs, [(wo, 0)], piece_sem, 4 * sz.n))
         x2[...] = x2[...] + nn(inner1[...], wd[...])
         wait(loads)
         sides = start(fetches(order_ref, gate_refs, [(wg, 0)], piece_sem, 6 * sz.n))
         sides += start(fetches(order_ref, up_refs, [(wu, 0)], piece_sem, 8 * sz.n))
         sides += [io.start(cl_hbm, cl2)]
         hidden[...] = attention_forward(
-            sz, x2[...], gains_ref[0:1, :], wqkv, wo, cos, sin, bias_ref, a1, heads, lse, mixp, mix
+            sz, x2[...], gains_ref[0:1, :], wqkv, wo, cos, sin, bias_ref, a1, heads, lse, mixp, mix,
+            lambda stage: wait(last) if stage == 1 else None
         )
         wait(sides)
         for a, b in ((a1, a1_hbm), (mixp, mixp_hbm), (wqkv, wqkv_hbm), (wo, wo_hbm)):
@@ -797,6 +800,7 @@
 
         def ready(last):
             if last:
+                io.store(g_qkv, g_qkv_hbm)
                 wait(later)
                 x[...] = x_low[...].astype(F32)
             else:
@@ -807,7 +811,6 @@
             sz, gh, gl[...], x, gains_ref[0:1, :], wqkv, wo, cos, sin, bias_ref,
             heads, lse_ref, mix, g_heads, g_qkv, ready
         )
-        io.store(g_qkv, g_qkv_hbm)
         gl[...] = back_x.astype(BF)
         io.store(gl, g_x_hbm)
         gain_grad[...] = jnp.concatenate([gain_a, jnp.zeros((7, wide), F32)], axis=0)

time: 350 us -> 350 us (level)
  transfers between devices with their start and end apart: 68 -> 68, of which waited for: 25 -> 26; matrix products, arithmetic and copies ran while one was open for 17% -> 17% of each run, Pallas kernels for 19% -> 19%
where the time goes in v5:
time: 350 us; the launch traced here: 344 us
  Pallas kernels  121 us (35%)
  waiting for transfers between devices  84.9 us (24%)
  starting transfers between devices  63.6 us (18%)
  local copies, waits for them, and re-layouts  38.8 us (11%)
  other arithmetic  33.5 us (10%)
    pallas_call x9, Pallas kernels, call(): pl.pallas_call(body, in_specs=specs or [VM] * len(ins), out_specs=out_spe...  121 us
    ppermute x16, waiting for transfers between devices, cross(): return lax.ppermute(v, ('dp', 'fsdp'), pairs)  43.8 us
    ppermute x24, starting transfers between devices, shift_z(): lax.ppermute(v, 'fsdp', [(i, (i + 4 * k) % self.n) for i in range(self.n)])  33.8 us
    ppermute x24, waiting for transfers between devices, shift_z(): lax.ppermute(v, 'fsdp', [(i, (i + 4 * k) % self.n) for i in range(self.n)])  28.5 us
    convert_element_type x16, other arithmetic, step(): return add(*[a[lo:hi] for a, (lo, hi) in zip(v, cuts)]).astype(BF)  26.5 us
    ppermute x16, starting transfers between devices, cross(): return lax.ppermute(v, ('dp', 'fsdp'), pairs)  18.9 us
    ppermute x24, waiting for transfers between devices, swap_core(): return lax.ppermute(v, 'fsdp', [(i, i ^ 1) for i in range(self.n)])  12.6 us
    unnamed x88, local copies, waits for them, and re-layouts  11.2 us
  transfers between devices with their start and end apart: 68, of which 26 were waited for; matrix products, arithmetic and copies ran while one was open for 17% of the time, Pallas kernels for 19%

profile of v5, /device:TPU:0, one launch (start us, length us, event | category | flops | bytes accessed | tf_op | source)
XLA Modules:
  0.0 344.1 jit_solution(17481670499106157934)
XLA Ops:
  4.9 5.0 %collective-permute-start.6 = (bf16[1,32,2624]{2,1,0:T(8,128)(2,1)S(1)}, bf16[1,32,2624]{2,1,0:T(8,128)(2,1)S(1)}, u32[]{:S(2)}, u32[]{:S(2)}) collective-permute-start(bf16[1,32,2624]{2,1,0:T(8,128)(2,1)S(1)} %select_bitcast_fusion), channel_id=1, source_target_pairs={{0,12},{1,13},{2,14},{3,15},{4,0},{5,1},{6,2},{7,3},{8,4},{9,5},{1... | collective-permute-start | bytes 503816 | tf_op jit(solution)/shard_map/ppermute | solution.py:57
  17.5 7.3 %collective-permute-done.5 = bf16[1,32,2624]{2,1,0:T(8,128)(2,1)S(1)} collective-permute-done((bf16[1,32,2624]{2,1,0:T(8,128)(2,1)S(1)}, bf16[1,32,2624]{2,1,0:T(8,128)(2,1)S(1)}, u32[]{:S(2)}, u32[]{:S(2)}) %collective-permute-start.5) | collective-permute-done | bytes 167968 | tf_op jit(solution)/shard_map/ppermute | solution.py:57
  31.3 4.6 %collective-permute-done.7 = bf16[4,32,2624]{2,1,0:T(8,128)(2,1)S(1)} collective-permute-done((bf16[4,32,2624]{2,1,0:T(8,128)(2,1)S(1)}, bf16[4,32,2624]{2,1,0:T(8,128)(2,1)S(1)}, u32[]{:S(2)}, u32[]{:S(2)}) %collective-permute-start.7) | collective-permute-done | bytes 671776 | tf_op jit(solution)/shard_map/ppermute | solution.py:69
  37.6 5.5 %collective-permute-done.9 = bf16[1,32,2560]{2,1,0:T(8,128)(2,1)S(1)} collective-permute-done((bf16[1,32,2560]{2,1,0:T(8,128)(2,1)S(1)}, bf16[1,32,2560]{2,1,0:T(8,128)(2,1)S(1)}, u32[]{:S(2)}, u32[]{:S(2)}) %collective-permute-start.9) | collective-permute-done | bytes 163872 | tf_op jit(solution)/shard_map/ppermute | solution.py:57
  58.5 3.1 collective-permute-done.15.p1.refs_7_
  77.9 11.9 %shard_map.204 = (f32[384,1024]{1,0:T(8,128)}, bf16[384,1024]{1,0:T(8,128)(2,1)}, bf16[1600,384]{1,0:T(8,128)(2,1)}, f32[16,384]{1,0:T(8,128)}, bf16[1024,384]{1,0:T(8,128)(2,1)}, /*index=5*/f32[8,1024]{1,0:T(8,128)}) custom-call(s32[32]{0:T(128)} %stack.179.order_ref.refs_0_, bf16[8,32,2624]{2,1,0:T(8,128)(2,1)} %copy-done, ...), custom_call_target="tpu_custom_call" | custom-call | flops 1000 | bytes 1000 | tf_op jit(solution)/shard_map/pallas_call | solution.py:264
  96.2 7.5 %shard_map.205 = (bf16[384,1024]{1,0:T(8,128)(2,1)}, bf16[384,2560]{1,0:T(8,128)(2,1)}) custom-call(s32[32]{0:T(128)} %stack.179.order_ref.refs_0_, bf16[8,32,2560]{2,1,0:T(8,128)(2,1)} %copy-done.2, bf16[8,32,2560]{2,1,0:T(8,128)(2,1)} %collective-permute-done.22.p1.refs_11_, bf16[8,32,2560]{2,1,0:T(8,128)(2,1)} %copy-done.4, ...), custom_call_target="tpu_custom_call" | custom-call | flops 1000 | bytes 1000 | tf_op jit(solution)/shard_map/pallas_call | solution.py:264
  103.7 6.8 %collective-permute-done.23 = bf16[4,80,1024]{2,1,0:T(8,128)(2,1)} collective-permute-done((bf16[4,80,1024]{2,1,0:T(8,128)(2,1)S(1)}, bf16[4,80,1024]{2,1,0:T(8,128)(2,1)}, u32[]{:S(2)}, u32[]{:S(2)}) %collective-permute-start.23) | collective-permute-done | bytes 655392 | tf_op jit(solution)/shard_map/ppermute | solution.py:69
  112.8 3.5 %collective-permute-done.27.p1.refs_15_ = bf16[8,32,2560]{2,1,0:T(8,128)(2,1)} collective-permute-done((bf16[8,32,2560]{2,1,0:T(8,128)(2,1)S(1)}, bf16[8,32,2560]{2,1,0:T(8,128)(2,1)}, u32[]{:S(2)}, u32[]{:S(2)}) %collective-permute-start.27) | collective-permute-done | bytes 1310752 | tf_op jit(solution)/shard_map/ppermute | solution.py:69
  117.8 3.4 collective-permute-done.28.p2.refs_16_
  122.3 7.7 %shard_map.206 = (bf16[384,2560]{1,0:T(8,128)(2,1)}, bf16[384,2560]{1,0:T(8,128)(2,1)}) custom-call(s32[32]{0:T(128)} %stack.179.order_ref.refs_0_, bf16[8,32,2560]{2,1,0:T(8,128)(2,1)} %copy-done.1, bf16[8,32,2560]{2,1,0:T(8,128)(2,1)} %collective-permute-done.27.p1.refs_15_, bf16[8,32,2560]{2,1,0:T(8,128)(2,1)} %copy-done.3, ...), custom_call_target="tpu_custom_call" | custom-call | flops 1000 | bytes 1000 | tf_op jit(solution)/shard_map/pallas_call | solution.py:264
  130.0 4.6 %collective-permute-done.26.refs_3_ = bf16[8,80,1024]{2,1,0:T(8,128)(2,1)} collective-permute-done((bf16[8,80,1024]{2,1,0:T(8,128)(2,1)S(1)}, bf16[8,80,1024]{2,1,0:T(8,128)(2,1)}, u32[]{:S(2)}, u32[]{:S(2)}) %collective-permute-start.26) | collective-permute-done | bytes 1310752 | tf_op jit(solution)/shard_map/ppermute | solution.py:69
  138.8 56.6 %shard_map.207 = (bf16[384,1024]{1,0:T(8,128)(2,1)}, bf16[1024,1600]{1,0:T(8,128)(2,1)}, bf16[1024,1024]{1,0:T(8,128)(2,1)}, bf16[384,1024]{1,0:T(8,128)(2,1)}, ...) custom-call(s32[32]{0:T(128)} %stack.179.order_ref.refs_0_, ...), custom_call_target="tpu_custom_call" | custom-call | flops 1000 | bytes 1000 | tf_op jit(solution)/shard_map/pallas_call | solution.py:264
  198.8 3.1 add_convert_fusion.2
  205.4 11.5 %shard_map.208 = (bf16[16,32,3584]{2,1,0:T(8,128)(2,1)}, bf16[8,32,3584]{2,1,0:T(8,128)(2,1)}, bf16[8,32,3584]{2,1,0:T(8,128)(2,1)}) custom-call(s32[12]{0:T(128)} %stack.192.refs_1_.back_ref, bf16[384,1024]{1,0:T(8,128)(2,1)} %get-tuple-element.511.a2_hbm.refs_22_.a_1, bf16[384,1024]{1,0:T(8,128)(2,1)} %get-tuple-element.512.a_2, ...), custom_call_target="tpu_custom_call" | custom-call | flops 1000 | bytes 1000 | tf_op jit(solution)/shard_map/pallas_call | solution.py:264
  216.9 2.9 collective-permute-done.36
  221.3 2.7 add_convert_fusion.9
  226.4 3.2 add_convert_fusion
  230.6 13.4 %shard_map.209 = (bf16[384,1024]{1,0:T(8,128)(2,1)}, bf16[1600,384]{1,0:T(8,128)(2,1)}, f32[8,1024]{1,0:T(8,128)}) custom-call(f32[384,1024]{1,0:T(8,128)} %get-tuple-element.532.gh_hbm, bf16[384,1024]{1,0:T(8,128)(2,1)} %get-tuple-element.533.l1.gl_hbm, bf16[384,1024]{1,0:T(8,128)(2,1)} %get-tuple-element.534.x_hbm, ...), custom_call_target="tpu_custom_call" | custom-call | flops 1000 | bytes 1000 | tf_op jit(solution)/shard_map/pallas_call | solution.py:264
  255.2 7.7 %shard_map.210 = (bf16[16,32,1600]{2,1,0:T(8,128)(2,1)}, bf16[8,32,1600]{2,1,0:T(8,128)(2,1)}, bf16[8,32,1600]{2,1,0:T(8,128)(2,1)}) custom-call(s32[12]{0:T(128)} %stack.192.refs_1_.back_ref, bf16[384,1024]{1,0:T(8,128)(2,1)} %get-tuple-element.560.a_1, bf16[384,1024]{1,0:T(8,128)(2,1)} %get-tuple-element.561.a_2, bf16[1600,384]{1,0:T(8,128)(2,1)} %get-tuple-element.562.g1, ...), custom_call_target="tpu_custom_call" | custom-call | flops 1000 | bytes 1000 | tf_op jit(solution)/shard_map/pallas_call | solution.py:264
  280.8 12.3 %collective-permute-done.49 = bf16[4,32,3584]{2,1,0:T(8,128)(2,1)S(1)} collective-permute-done((bf16[4,32,3584]{2,1,0:T(8,128)(2,1)S(1)}, bf16[4,32,3584]{2,1,0:T(8,128)(2,1)S(1)}, u32[]{:S(2)}, u32[]{:S(2)}) %collective-permute-start.49) | collective-permute-done | bytes 917536 | tf_op jit(solution)/shard_map/ppermute | solution.py:69
  312.2 6.3 %collective-permute-done.55 = bf16[1,32,3584]{2,1,0:T(8,128)(2,1)} collective-permute-done((bf16[1,32,3584]{2,1,0:T(8,128)(2,1)}, bf16[1,32,3584]{2,1,0:T(8,128)(2,1)}, u32[]{:S(2)}, u32[]{:S(2)}) %collective-permute-start.55) | collective-permute-done | bytes 229408 | tf_op jit(solution)/shard_map/ppermute | solution.py:57
  324.8 2.6 collective-permute-done.59
  328.3 4.3 %collective-permute-done.58 = bf16[1,32,1600]{2,1,0:T(8,128)(2,1)S(1)} collective-permute-done((bf16[1,32,1600]{2,1,0:T(8,128)(2,1)S(1)}, bf16[1,32,1600]{2,1,0:T(8,128)(2,1)S(1)}, u32[]{:S(2)}, u32[]{:S(2)}) %collective-permute-start.58) | collective-permute-done | bytes 102432 | tf_op jit(solution)/shard_map/ppermute | solution.py:57
  (301 shorter events, 144.9 us)
Async XLA Ops:
  27.4 15.8 %collective-permute-start.9 = (bf16[1,32,2560]{2,1,0:T(8,128)(2,1)S(1)}, bf16[1,32,2560]{2,1,0:T(8,128)(2,1)S(1)}, u32[]{:S(2)}, u32[]{:S(2)}) collective-permute-start(bf16[1,32,2560]{2,1,0:T(8,128)(2,1)S(1)} %select_bitcast_fusion.3), channel_id=1, source_target_pairs={{0,8},{1,9},{2,10},{3,11},{4,12},{5,13},{6,14},{7,15},{8,0},{9,1},... | collective-permute-start | bytes 491528 | tf_op jit(solution)/shard_map/ppermute | solution.py:57
  36.1 25.5 %collective-permute-start.15 = (bf16[8,32,2624]{2,1,0:T(8,128)(2,1)S(1)}, bf16[8,32,2624]{2,1,0:T(8,128)(2,1)}, u32[]{:S(2)}, u32[]{:S(2)}) collective-permute-start(bf16[8,32,2624]{2,1,0:T(8,128)(2,1)S(1)} %constant_dynamic-update-slice_fusion.4.p0.refs_6_), channel_id=1, source_target_pairs={{0,16},{1,3},{2,18},{3,1},{4,20},{5,7},{6,22},{7,5},{8,24},{9,11},... | collective-permute-start | bytes 4030472 | tf_op jit(solution)/shard_map/ppermute | solution.py:69
  45.9 15.7 %collective-permute-start.14 = (bf16[4,32,2560]{2,1,0:T(8,128)(2,1)}, bf16[4,32,2560]{2,1,0:T(8,128)(2,1)}, u32[]{:S(2)}, u32[]{:S(2)}) collective-permute-start(bf16[4,32,2560]{2,1,0:T(8,128)(2,1)} %constant_dynamic-update-slice_fusion.6), channel_id=1, source_target_pairs={{0,2},{1,17},{2,0},{3,19},{4,6},{5,21},{6,4},{7,23},{8,10},{9,25},... | collective-permute-start | bytes 1966088 | tf_op jit(solution)/shard_map/ppermute | solution.py:69
  64.2 25.6 %collective-permute-start.22 = (bf16[8,32,2560]{2,1,0:T(8,128)(2,1)S(1)}, bf16[8,32,2560]{2,1,0:T(8,128)(2,1)}, u32[]{:S(2)}, u32[]{:S(2)}) collective-permute-start(bf16[8,32,2560]{2,1,0:T(8,128)(2,1)S(1)} %constant_dynamic-update-slice_fusion.10.p0.refs_10_), channel_id=1, source_target_pairs={{0,16},{1,3},{2,18},{3,1},{4,20},{5,7},{6,22},{7,5},{8,24},{9,11},... | collective-permute-start | bytes 3932168 | tf_op jit(solution)/shard_map/ppermute | solution.py:69
  69.4 20.4 %collective-permute-start.21 = (bf16[4,32,2560]{2,1,0:T(8,128)(2,1)S(1)}, bf16[4,32,2560]{2,1,0:T(8,128)(2,1)}, u32[]{:S(2)}, u32[]{:S(2)}) collective-permute-start(bf16[4,32,2560]{2,1,0:T(8,128)(2,1)S(1)} %constant_dynamic-update-slice_fusion.12), channel_id=1, source_target_pairs={{0,2},{1,17},{2,0},{3,19},{4,6},{5,21},{6,4},{7,23},{8,10},{9,25},... | collective-permute-start | bytes 1966088 | tf_op jit(solution)/shard_map/ppermute | solution.py:69
  72.0 17.8 %collective-permute-start.20 = (bf16[1,80,1024]{2,1,0:T(8,128)(2,1)S(1)}, bf16[1,80,1024]{2,1,0:T(8,128)(2,1)S(1)}, u32[]{:S(2)}, u32[]{:S(2)}) collective-permute-start(bf16[1,80,1024]{2,1,0:T(8,128)(2,1)S(1)} %select_bitcast_fusion.1), channel_id=1, source_target_pairs={{0,12},{1,13},{2,14},{3,15},{4,0},{5,1},{6,2},{7,3},{8,4},{9,5},{1... | collective-permute-start | bytes 491528 | tf_op jit(solution)/shard_map/ppermute | solution.py:57
  72.8 17.0 %collective-permute-start.19 = (bf16[1,80,1024]{2,1,0:T(8,128)(2,1)S(1)}, bf16[1,80,1024]{2,1,0:T(8,128)(2,1)S(1)}, u32[]{:S(2)}, u32[]{:S(2)}) collective-permute-start(bf16[1,80,1024]{2,1,0:T(8,128)(2,1)S(1)} %select_bitcast_fusion.1), channel_id=1, source_target_pairs={{0,8},{1,9},{2,10},{3,11},{4,12},{5,13},{6,14},{7,15},{8,0},{9,1},... | collective-permute-start | bytes 491528 | tf_op jit(solution)/shard_map/ppermute | solution.py:57
  91.6 24.7 %collective-permute-start.27 = (bf16[8,32,2560]{2,1,0:T(8,128)(2,1)S(1)}, bf16[8,32,2560]{2,1,0:T(8,128)(2,1)}, u32[]{:S(2)}, u32[]{:S(2)}) collective-permute-start(bf16[8,32,2560]{2,1,0:T(8,128)(2,1)S(1)} %constant_dynamic-update-slice_fusion.16.p0.refs_14_), channel_id=1, source_target_pairs={{0,16},{1,3},{2,18},{3,1},{4,20},{5,7},{6,22},{7,5},{8,24},{9,11},... | collective-permute-start | bytes 3932168 | tf_op jit(solution)/shard_map/ppermute | solution.py:69
  92.7 17.8 %collective-permute-start.23 = (bf16[4,80,1024]{2,1,0:T(8,128)(2,1)S(1)}, bf16[4,80,1024]{2,1,0:T(8,128)(2,1)}, u32[]{:S(2)}, u32[]{:S(2)}) collective-permute-start(bf16[4,80,1024]{2,1,0:T(8,128)(2,1)S(1)} %constant_dynamic-update-slice_fusion.18), channel_id=1, source_target_pairs={{0,2},{1,17},{2,0},{3,19},{4,6},{5,21},{6,4},{7,23},{8,10},{9,25},... | collective-permute-start | bytes 1966088 | tf_op jit(solution)/shard_map/ppermute | solution.py:69
  116.8 17.7 %collective-permute-start.26 = (bf16[8,80,1024]{2,1,0:T(8,128)(2,1)S(1)}, bf16[8,80,1024]{2,1,0:T(8,128)(2,1)}, u32[]{:S(2)}, u32[]{:S(2)}) collective-permute-start(bf16[8,80,1024]{2,1,0:T(8,128)(2,1)S(1)} %constant_dynamic-update-slice_fusion.22.refs_2_), channel_id=1, source_target_pairs={{0,16},{1,3},{2,18},{3,1},{4,20},{5,7},{6,22},{7,5},{8,24},{9,11},... | collective-permute-start | bytes 3932168 | tf_op jit(solution)/shard_map/ppermute | solution.py:69
  201.9 17.9 %collective-permute-start.36 = (bf16[8,80,1024]{2,1,0:T(8,128)(2,1)}, bf16[8,80,1024]{2,1,0:T(8,128)(2,1)}, u32[]{:S(2)}, u32[]{:S(2)}) collective-permute-start(bf16[8,80,1024]{2,1,0:T(8,128)(2,1)} %add_convert_fusion.2), channel_id=1, source_target_pairs={{0,16},{1,3},{2,18},{3,1},{4,20},{5,7},{6,22},{7,5},{8,24},{9,11},... | collective-permute-start | bytes 3932168 | tf_op jit(solution)/shard_map/ppermute | solution.py:69
  220.3 24.9 %collective-permute-start.39 = (bf16[8,32,2560]{2,1,0:T(8,128)(2,1)}, bf16[8,32,2560]{2,1,0:T(8,128)(2,1)}, u32[]{:S(2)}, u32[]{:S(2)}) collective-permute-start(bf16[8,32,2560]{2,1,0:T(8,128)(2,1)} %add_convert_fusion.1), channel_id=1, source_target_pairs={{0,16},{1,3},{2,18},{3,1},{4,20},{5,7},{6,22},{7,5},{8,24},{9,11},... | collective-permute-start | bytes 3932168 | tf_op jit(solution)/shard_map/ppermute | solution.py:69
  224.0 21.3 %collective-permute-start.40 = (bf16[4,80,1024]{2,1,0:T(8,128)(2,1)}, bf16[4,80,1024]{2,1,0:T(8,128)(2,1)}, u32[]{:S(2)}, u32[]{:S(2)}) collective-permute-start(bf16[4,80,1024]{2,1,0:T(8,128)(2,1)} %add_convert_fusion.9), channel_id=1, source_target_pairs={{0,2},{1,17},{2,0},{3,19},{4,6},{5,21},{6,4},{7,23},{8,10},{9,25},... | collective-permute-start | bytes 1966088 | tf_op jit(solution)/shard_map/ppermute | solution.py:69
  229.6 42.3 %collective-permute-start.48 = (bf16[8,32,3584]{2,1,0:T(8,128)(2,1)}, bf16[8,32,3584]{2,1,0:T(8,128)(2,1)}, u32[]{:S(2)}, u32[]{:S(2)}) collective-permute-start(bf16[8,32,3584]{2,1,0:T(8,128)(2,1)} %add_convert_fusion), channel_id=1, source_target_pairs={{0,16},{1,3},{2,18},{3,1},{4,20},{5,7},{6,22},{7,5},{8,24},{9,11},... | collective-permute-start | bytes 5505032 | tf_op jit(solution)/shard_map/ppermute | solution.py:69
  247.5 18.0 %collective-permute-start.41 = (bf16[4,32,2560]{2,1,0:T(8,128)(2,1)}, bf16[4,32,2560]{2,1,0:T(8,128)(2,1)}, u32[]{:S(2)}, u32[]{:S(2)}) collective-permute-start(bf16[4,32,2560]{2,1,0:T(8,128)(2,1)} %add_convert_fusion.8), channel_id=1, source_target_pairs={{0,2},{1,17},{2,0},{3,19},{4,6},{5,21},{6,4},{7,23},{8,10},{9,25},... | collective-permute-start | bytes 1966088 | tf_op jit(solution)/shard_map/ppermute | solution.py:69
  273.9 19.1 %collective-permute-start.49 = (bf16[4,32,3584]{2,1,0:T(8,128)(2,1)S(1)}, bf16[4,32,3584]{2,1,0:T(8,128)(2,1)S(1)}, u32[]{:S(2)}, u32[]{:S(2)}) collective-permute-start(bf16[4,32,3584]{2,1,0:T(8,128)(2,1)S(1)} %add_convert_fusion.4), channel_id=1, source_target_pairs={{0,2},{1,17},{2,0},{3,19},{4,6},{5,21},{6,4},{7,23},{8,10},{9,25},... | collective-permute-start | bytes 2752520 | tf_op jit(solution)/shard_map/ppermute | solution.py:69
  275.2 17.9 %collective-permute-start.47 = (bf16[1,32,2560]{2,1,0:T(8,128)(2,1)S(1)}, bf16[1,32,2560]{2,1,0:T(8,128)(2,1)S(1)}, u32[]{:S(2)}, u32[]{:S(2)}) collective-permute-start(bf16[1,32,2560]{2,1,0:T(8,128)(2,1)S(1)} %get-tuple-element.658), channel_id=1, source_target_pairs={{0,12},{1,13},{2,14},{3,15},{4,0},{5,1},{6,2},{7,3},{8,4},{9,5},{1... | collective-permute-start | bytes 491528 | tf_op jit(solution)/shard_map/ppermute | solution.py:57
  276.6 16.4 %collective-permute-start.46 = (bf16[1,32,2560]{2,1,0:T(8,128)(2,1)S(1)}, bf16[1,32,2560]{2,1,0:T(8,128)(2,1)S(1)}, u32[]{:S(2)}, u32[]{:S(2)}) collective-permute-start(bf16[1,32,2560]{2,1,0:T(8,128)(2,1)S(1)} %get-tuple-element.659), channel_id=1, source_target_pairs={{0,8},{1,9},{2,10},{3,11},{4,12},{5,13},{6,14},{7,15},{8,0},{9,1},... | collective-permute-start | bytes 491528 | tf_op jit(solution)/shard_map/ppermute | solution.py:57
  279.8 20.9 %collective-permute-start.52 = (bf16[8,32,1600]{2,1,0:T(8,128)(2,1)S(1)}, bf16[8,32,1600]{2,1,0:T(8,128)(2,1)S(1)}, u32[]{:S(2)}, u32[]{:S(2)}) collective-permute-start(bf16[8,32,1600]{2,1,0:T(8,128)(2,1)S(1)} %add_convert_fusion.5), channel_id=1, source_target_pairs={{0,16},{1,3},{2,18},{3,1},{4,20},{5,7},{6,22},{7,5},{8,24},{9,11},... | collective-permute-start | bytes 2457608 | tf_op jit(solution)/shard_map/ppermute | solution.py:69
  296.0 16.2 %collective-permute-start.56 = (bf16[1,32,3584]{2,1,0:T(8,128)(2,1)}, bf16[1,32,3584]{2,1,0:T(8,128)(2,1)}, u32[]{:S(2)}, u32[]{:S(2)}) collective-permute-start(bf16[1,32,3584]{2,1,0:T(8,128)(2,1)} %get-tuple-element.655), channel_id=1, source_target_pairs={{0,12},{1,13},{2,14},{3,15},{4,0},{5,1},{6,2},{7,3},{8,4},{9,5},{1... | collective-permute-start | bytes 688136 | tf_op jit(solution)/shard_map/ppermute | solution.py:57
  296.8 21.6 %collective-permute-start.55 = (bf16[1,32,3584]{2,1,0:T(8,128)(2,1)}, bf16[1,32,3584]{2,1,0:T(8,128)(2,1)}, u32[]{:S(2)}, u32[]{:S(2)}) collective-permute-start(bf16[1,32,3584]{2,1,0:T(8,128)(2,1)} %get-tuple-element.656), channel_id=1, source_target_pairs={{0,8},{1,9},{2,10},{3,11},{4,12},{5,13},{6,14},{7,15},{8,0},{9,1},... | collective-permute-start | bytes 688136 | tf_op jit(solution)/shard_map/ppermute | solution.py:57
  298.7 19.8 %collective-permute-start.54 = (bf16[1,32,3584]{2,1,0:T(8,128)(2,1)}, bf16[1,32,3584]{2,1,0:T(8,128)(2,1)}, u32[]{:S(2)}, u32[]{:S(2)}) collective-permute-start(bf16[1,32,3584]{2,1,0:T(8,128)(2,1)} %get-tuple-element.657), channel_id=1, source_target_pairs={{0,4},{1,5},{2,6},{3,7},{4,8},{5,9},{6,10},{7,11},{8,12},{9,13},{1... | collective-permute-start | bytes 688136 | tf_op jit(solution)/shard_map/ppermute | solution.py:57
  301.8 17.7 %collective-permute-start.53 = (bf16[4,32,1600]{2,1,0:T(8,128)(2,1)}, bf16[4,32,1600]{2,1,0:T(8,128)(2,1)}, u32[]{:S(2)}, u32[]{:S(2)}) collective-permute-start(bf16[4,32,1600]{2,1,0:T(8,128)(2,1)} %add_convert_fusion.11), channel_id=1, source_target_pairs={{0,2},{1,17},{2,0},{3,19},{4,6},{5,21},{6,4},{7,23},{8,10},{9,25},... | collective-permute-start | bytes 1228808 | tf_op jit(solution)/shard_map/ppermute | solution.py:69
  309.7 22.9 %collective-permute-start.64 = (bf16[32,2560]{1,0:T(8,128)(2,1)S(1)}, bf16[32,2560]{1,0:T(8,128)(2,1)}, u32[]{:S(2)}, u32[]{:S(2)}) collective-permute-start(bf16[32,2560]{1,0:T(8,128)(2,1)S(1)} %bitcast.112), channel_id=1, source_target_pairs={{0,16},{16,0},{1,17},{17,1},{2,18},{18,2},{3,19},{19,3},{4,20},{20... | collective-permute-start | bytes 491528 | tf_op jit(solution)/shard_map/ppermute | solution.py:60
  (80 other events, 716.9 us)
